TPU v7x, 512 devices: a whole 4x4x16 slice. The times are simulated.
512 devices in a mesh: dp: 8 (over x, y_hi), latent: 64 (over z, y_lo, core).
Axes of the slice: x: 4, y: 4 (y_hi: 2, y_lo: 2; y = y_hi * 2 + y_lo), z: 16, core: 2. Of those that a mesh axis runs over, the one named last changes fastest.
Arguments:
- resid: bfloat16 [1024, 3, 2304], P('dp', None, 'latent'), may hold values from -6 to 6
- target: bfloat16 [1024, 3, 2304], P('dp', None, 'latent'), may hold values from -6 to 6
- enc_weight: bfloat16 [24576, 2304], P('latent', 'dp'), may hold values from -0.125 to 0.125
- enc_bias: float32 [24576], P('latent'), may hold values from -0.6 to 0.6
- dec_weight: bfloat16 [24576, 3, 2304], P('latent', None, 'dp'), may hold values from -0.0625 to 0.0625
- source: int32 [24576], P('latent'), may hold values from 0 to 2, as said below
Outputs:
- loss: float32 [], replicated
- recon: bfloat16 [1024, 3, 2304], P('dp', None, 'latent')
- enc_grad: float32 [24576, 2304], P('latent', 'dp')
- bias_grad: float32 [24576], P('latent')
- dec_grad: float32 [24576, 3, 2304], P('latent', None, 'dp')
Inputs may be any that keep to these rules, and one draw needn't show every extreme that they name: Each layer 0 to 2 is the source of exactly 8192 latents.
All inputs are finite; a program needn't handle non-finite values.
Results may differ from a plain program's by a relative error of at most 0.0095.
Values may be sent and summed in bfloat16 or wider, within the bound.
No kernel may reach another device: no remote copies, remote signals or barrier semaphores. Data moves between devices by JAX's collectives and lax.ppermute only.
A program may use at most 64 MiB of HBM per device.

v0:
```python
import jax
import jax.numpy as jnp
from jax import lax
from jax.sharding import PartitionSpec as P

LAYERS = 3
TOK_DEV = 128


sparsity_weight = 0.5
norm_epsilon = 1e-06


def on_device(resid, target, enc_weight, enc_bias, dec_weight, source):
    layer_ids = jnp.arange(LAYERS, dtype=jnp.int32)
    pick = (source[:, None] == layer_ids[None, :]).astype(jnp.float32)
    reach = (source[:, None] <= layer_ids[None, :]).astype(jnp.float32)
    gathered = lax.all_gather(resid, "latent", axis=2, tiled=True)
    enc_rows, dec_rows = (
        lax.all_gather(enc_weight, "dp", axis=1, tiled=True),
        lax.all_gather(dec_weight, "dp", axis=2, tiled=True),
    )
    every = jnp.einsum("tld,jd->tlj", gathered, enc_rows, preferred_element_type=jnp.float32)
    pre = jnp.sum(every * pick.T[None, :, :], axis=1) + enc_bias[None, :]
    acts = jnp.maximum(pre, 0.0).astype(jnp.bfloat16)
    acts_wide = acts.astype(jnp.float32)
    masked = dec_rows * reach.astype(jnp.bfloat16)[:, :, None]
    norms = jnp.sqrt(
        jnp.einsum("jld,jld->j", masked, masked, preferred_element_type=jnp.float32) + norm_epsilon
    )
    terms = jnp.einsum("tj,jld->tld", acts, masked, preferred_element_type=jnp.float32)
    recon_sum = lax.psum_scatter(terms, "latent", scatter_dimension=2, tiled=True)
    error = recon_sum - target.astype(jnp.float32)
    local_loss = jnp.sum(error * error) + sparsity_weight * jnp.sum(acts_wide * norms[None, :])
    gout = (2.0 * error / TOK_DEV).astype(jnp.bfloat16)
    grads_full = lax.all_gather(gout, "latent", axis=2, tiled=True)
    dacts = jnp.einsum("tld,jld->tj", grads_full, masked, preferred_element_type=jnp.float32)
    dacts = dacts + sparsity_weight * norms[None, :] / TOK_DEV
    dpre = jnp.where(pre > 0, dacts, 0.0)
    dpre_low = dpre.astype(jnp.bfloat16)
    acts_every, dpre_every = (
        lax.all_gather(acts, "dp", axis=0, tiled=True),
        lax.all_gather(dpre_low, "dp", axis=0, tiled=True),
    )
    resid_cols, gout_cols = (
        lax.all_to_all(gathered, "dp", split_axis=2, concat_axis=0, tiled=True),
        lax.all_to_all(grads_full, "dp", split_axis=2, concat_axis=0, tiled=True),
    )
    weighted = dpre_every[:, None, :] * pick.T.astype(jnp.bfloat16)[None, :, :]
    enc_grad = jnp.einsum("tlj,tld->jd", weighted, resid_cols, preferred_element_type=jnp.float32)
    bias_grad = lax.psum(jnp.sum(dpre, axis=0), "dp")
    colsum = jnp.sum(acts_every.astype(jnp.float32), axis=0)
    dec_product = jnp.einsum(
        "tj,tld->jld", acts_every, gout_cols, preferred_element_type=jnp.float32
    )
    local_dec = dec_weight.astype(jnp.float32) * reach[:, :, None]
    dec_grad = reach[:, :, None] * (
        dec_product
        + sparsity_weight * colsum[:, None, None] / TOK_DEV * local_dec / norms[:, None, None]
    )
    loss = lax.psum(local_loss, ("dp", "latent")) / TOK_DEV
    return (loss, recon_sum.astype(jnp.bfloat16), enc_grad, bias_grad, dec_grad)


def solution(mesh):
    in_specs = (
        P("dp", None, "latent"),
        P("dp", None, "latent"),
        P("latent", "dp"),
        P("latent"),
        P("latent", None, "dp"),
        P("latent"),
    )
    out_specs = (
        P(),
        P("dp", None, "latent"),
        P("latent", "dp"),
        P("latent"),
        P("latent", None, "dp"),
    )
    return jax.shard_map(
        on_device, mesh=mesh, in_specs=in_specs, out_specs=out_specs, check_vma=False
    )
```

profile of v0, /device:TPU:1, one launch (start us, length us, event | category | flops | bytes accessed | tf_op | source)
XLA Modules:
  0.0 1089.4 jit_solution(855709626275781736)
XLA Ops:
  7.2 0.0 all-gather.7.cloned.1.call-start
  7.2 0.7 all-gather.7.cloned.1.call-update
  7.9 0.0 all-gather.5.cloned.1.call-start
  7.9 1.4 copy.14
  9.3 0.0 all-gather.5.cloned.1.call-update
  9.4 0.0 all-gather.9.cloned.1.call-start
  9.4 0.7 all-gather.9.cloned.1.call-update
  10.1 0.0 all-reduce.3.cloned.1.call-start
  10.1 0.7 fusion.47
  10.8 0.7 fusion.49
  11.5 71.4 %all-gather.7.cloned.1.call-done = bf16[384,2304]{0,1:T(8,128)(2,1)} async-done(((bf16[384,288]{0,1:T(8,128)(2,1)}), bf16[384,2304]{0,1:T(8,128)(2,1)}) %all-gather.7.cloned.1.call-update) | async-done | bytes 1769488 | tf_op jit(solution)/shard_map/all_gather | solution.py:20
  83.0 126.5 %all-gather.5.cloned.1.call-done = bf16[128,3,2304]{0,1,2:T(4,128)(2,1)} async-done(((bf16[128,3,36]{0,1,2:T(4,128)(2,1)}), bf16[128,3,2304]{0,1,2:T(4,128)(2,1)}) %all-gather.5.cloned.1.call-update) | async-done | bytes 1769488 | tf_op jit(solution)/shard_map/all_gather | solution.py:18
  209.5 3.3 fusion.22
  212.8 91.7 %all-gather.9.cloned.1.call-done = bf16[384,3,2304]{0,2,1:T(8,128)(2,1)} async-done(((bf16[384,3,288]{0,2,1:T(8,128)(2,1)}), bf16[384,3,2304]{0,2,1:T(8,128)(2,1)}) %all-gather.9.cloned.1.call-update) | async-done | bytes 5308432 | tf_op jit(solution)/shard_map/all_gather | solution.py:21
  304.5 0.0 copy-start.4
  304.5 0.0 copy-start
  304.5 4.1 fusion
  308.6 0.0 copy-done.4
  308.6 0.7 multiply_reduce_fusion
  309.3 0.0 copy-done
  309.3 3.3 fusion.3
  312.6 0.0 copy-start.3
  312.6 0.0 copy-start.1
  312.6 0.0 all-reduce.3.cloned.1.call-update
  312.7 0.0 all-gather.11.cloned.1.call-start
  312.7 1.4 dynamic-slice
  314.8 441.6 %all-reduce.3.cloned.1.call-done = f32[128,3,2304]{0,2,1:T(8,128)} async-done(((f32[128,3,2304]{0,2,1:T(8,128)}), f32[128,3,2304]{0,2,1:T(8,128)}) %all-reduce.3.cloned.1.call-update) | async-done | bytes 3538960
  756.3 0.0 copy-done.3
  756.3 1.5 multiply_convert_fusion
  757.9 0.6 copy.16
  758.5 0.0 all-gather.11.cloned.1.call-update
  758.5 0.0 copy-done.1
  758.5 32.6 %all_to_all.36 = bf16[128,3,2304]{0,1,2:T(4,128)(2,1)S(1)} all-to-all(bf16[128,3,2304]{0,1,2:T(4,128)(2,1)S(1)} %copy-done.1), channel_id=1, replica_groups=mesh['dp'=8,'latent'=64] {'dp'}, dimensions={2} | all-to-all | bytes 3538944 | tf_op jit(solution)/shard_map/all_to_all | solution.py:46
  791.1 1.4 copy.49
  792.5 2.2 all_to_all.29
  794.7 32.3 %all_gather.23 = bf16[1024,384]{1,0:T(8,128)(2,1)S(1)} all-gather(bf16[128,384]{1,0:T(8,128)(2,1)S(1)} %get-tuple-element.6), channel_id=1, replica_groups=mesh['dp'=8,'latent'=64] {'dp'}, dimensions={0}, use_global_device_ids=true | all-gather | bytes 884736 | tf_op jit(solution)/shard_map/all_gather | solution.py:42
  827.0 57.1 %all-gather.11.cloned.1.call-done = bf16[128,3,2304]{0,1,2:T(4,128)(2,1)} async-done(((bf16[128,3,36]{0,1,2:T(4,128)(2,1)}), bf16[128,3,2304]{0,1,2:T(4,128)(2,1)}) %all-gather.11.cloned.1.call-update) | async-done | bytes 1769488 | tf_op jit(solution)/shard_map/all_gather | solution.py:36
  884.1 6.0 all-to-all-start.1
  890.1 0.2 convert_reduce_fusion
  891.6 124.4 %psum.14 = f32[]{:T(128)} all-reduce(f32[]{:T(128)S(6)} %add.38), channel_id=1, replica_groups=mesh['dp'=8,'latent'=64] {'dp','latent'}, use_global_device_ids=true, to_apply=%region_4.5 | all-reduce | flops 1 | bytes 8 | tf_op jit(solution)/shard_map/psum | solution.py:61
  1016.7 1.5 dynamic-slice_convert_fusion
  1018.2 4.4 fusion.50
  1022.6 17.6 %psum.15 = f32[384]{0:T(512)} all-reduce(f32[384]{0:T(512)S(1)} %get-tuple-element.9), channel_id=1, replica_groups=mesh['dp'=8,'latent'=64] {'dp'}, use_global_device_ids=true, to_apply=%region_6.7 | all-reduce | flops 384 | bytes 3072 | tf_op jit(solution)/shard_map/psum | solution.py:51
  1040.1 30.6 %all_gather.22 = bf16[1024,384]{1,0:T(8,128)(2,1)S(1)} all-gather(bf16[128,384]{1,0:T(8,128)(2,1)S(1)} %get-tuple-element.10), channel_id=1, replica_groups=mesh['dp'=8,'latent'=64] {'dp'}, dimensions={0}, use_global_device_ids=true | all-gather | bytes 884736 | tf_op jit(solution)/shard_map/all_gather | solution.py:43
  1070.7 3.4 fusion.19
  1074.1 0.0 all-to-all-done.1
  1074.1 2.7 copy.48
  1076.8 0.0 copy-start.2
  1076.8 2.7 all_to_all.33
  1079.5 0.0 copy-done.2
  1079.5 2.2 fusion.13
  (2 shorter events, 0.0 us)
Async XLA Ops:
  7.2 75.8 %all-gather.7.cloned.1.call-start = ((), (), s32[]{:S(2)}) async-start(), calls=%async_computation.3 | async-start | bytes 1990656 | tf_op jit(solution)/shard_map/all_gather | solution.py:20
  7.9 201.6 %all-gather.5.cloned.1.call-start = ((), (), s32[]{:S(2)}) async-start(), calls=%async_computation.2 | async-start | bytes 2396160 | tf_op jit(solution)/shard_map/all_gather | solution.py:18
  9.4 295.1 %all-gather.9.cloned.1.call-start = ((), (), s32[]{:S(2)}) async-start(), calls=%async_computation.4 | async-start | bytes 5971968 | tf_op jit(solution)/shard_map/all_gather | solution.py:21
  10.1 746.3 %all-reduce.3.cloned.1.call-start = ((), (), s32[]{:S(2)}) async-start(), calls=%async_computation.6 | async-start | bytes 7077888
  304.5 4.1 copy-start.4
  304.5 4.8 copy-start
  312.6 443.7 %copy-start.3 = (bf16[128,3,36]{0,2,1:T(8,128)(2,1)S(1)}, bf16[128,3,36]{0,2,1:T(8,128)(2,1)}, u32[]{:S(2)}) copy-start(bf16[128,3,36]{0,2,1:T(8,128)(2,1)} %param.7) | copy-start | bytes 82948
  312.6 445.9 %copy-start.1 = (bf16[128,3,2304]{0,1,2:T(4,128)(2,1)S(1)}, bf16[128,3,2304]{0,1,2:T(4,128)(2,1)}, u32[]{:S(2)}) copy-start(bf16[128,3,2304]{0,1,2:T(4,128)(2,1)} %all-gather.5.cloned.1.call-done) | copy-start | bytes 5308420
  312.7 571.5 %all-gather.11.cloned.1.call-start = ((), (), s32[]{:S(2)}) async-start(), calls=%async_computation.5 | async-start | bytes 2396160 | tf_op jit(solution)/shard_map/all_gather | solution.py:36
  884.1 189.9 %all-to-all-start.1 = ((bf16[128,3,2304]{0,1,2:T(4,128)(2,1)}), bf16[128,3,2304]{0,1,2:T(4,128)(2,1)S(1)}, u32[]{:S(2)}, u32[]{:S(2)}) async-start(bf16[128,3,2304]{0,1,2:T(4,128)(2,1)} %all-gather.11.cloned.1.call-done), calls=%async_computation.1 | async-start | bytes 4718592 | tf_op jit(solution)/shard_map/all_to_all | solution.py:47
  1076.8 2.7 copy-start.2
Sparse Core Ops, SparseCore 0:
  11.2 71.7 all-gather.6
  85.7 123.7 all-gather.4
  212.7 91.7 all-gather.8
  312.8 443.5 all-reduce.2
  759.1 124.9 all-gather.10
where the time goes:
time: 1100 us; the launch traced here: 1090 us
  waiting for transfers between devices  790 us (72%)
  blocking collectives  237 us (22%)
  between operations  17.6 us (2%)
  matrix products  16.6 us (2%)
  local copies, waits for them, and re-layouts  14 us (1%)
    unnamed x6, waiting for transfers between devices  443 us
    all_gather x1, waiting for transfers between devices, on_device(): gathered = lax.all_gather(resid, 'latent', axis=2, tiled=True)  127 us
    psum x1, blocking collectives, on_device(): loss = lax.psum(local_loss, ('dp', 'latent')) / TOK_DEV  124 us
    all_gather x1, waiting for transfers between devices, on_device(): lax.all_gather(dec_weight, 'dp', axis=2, tiled=True)  91.7 us
    all_gather x1, waiting for transfers between devices, on_device(): lax.all_gather(enc_weight, 'dp', axis=1, tiled=True)  71.4 us
    all_gather x1, waiting for transfers between devices, on_device(): grads_full = lax.all_gather(gout, 'latent', axis=2, tiled=True)  57.1 us
    all_to_all x1, blocking collectives, on_device(): lax.all_to_all(gathered, 'dp', split_axis=2, concat_axis=0, tiled=True)  32.6 us
    all_gather x1, blocking collectives, on_device(): lax.all_gather(acts, 'dp', axis=0, tiled=True)  32.3 us
  transfers between devices with their start and end apart: 6, of which 5 were waited for; matrix products, arithmetic and copies ran while one was open for 2% of the time, Pallas kernels for 0%

commit v1 on v0

v1 whole, which is shorter than its diff:
```python
import jax
import jax.numpy as jnp
import numpy as np
from jax import lax
from jax.sharding import Mesh
from jax.sharding import PartitionSpec as P

LAYERS = 3
TOK_DEV = 128
SIZES = (4, 2, 16, 2, 2)
ALL = ("x", "yh", "z", "yl", "c")
DP = ("x", "yh")
LATENT = ("z", "yl", "c")
QUAD = ("yl", "c")
BLOCK = 112

sparsity_weight = 0.5
norm_epsilon = 1e-06
bf16, f32 = jnp.bfloat16, jnp.float32


def spread():
    pairs = []
    for a in range(8):
        for b in range(64):
            i, r = divmod(b, 8)
            pairs.append((a * 64 + b, i * 64 + ((a % 2) * 8 + r) * 4 + a // 2))
    return pairs


def pieces(value):
    high = lax.reduce_precision(value, 8, 7)
    middle = lax.reduce_precision(value - high, 8, 7)
    low = value - high - middle
    return [high.astype(bf16), middle.astype(bf16), low.astype(bf16)]


def share(block, axes, count):
    return lax.all_to_all(jnp.broadcast_to(block[None], (count, *block.shape)), axes, 0, 0)


def dot(spec, a, b):
    return jnp.einsum(spec, a, b, preferred_element_type=f32)


def on_device(resid, target, enc_weight, enc_bias, dec_weight, source):
    to = spread()
    back = [(d, s) for s, d in to]
    layer_ids = jnp.arange(LAYERS, dtype=jnp.int32)
    pick = source[None, :] == layer_ids[:, None]
    reach = source[None, :] <= layer_ids[:, None]

    both = jnp.stack([resid, target]).transpose(0, 2, 3, 1).reshape(2, 108, 128)
    both = jnp.pad(both, ((0, 0), (0, BLOCK - 108), (0, 0)))
    both = lax.ppermute(both, ALL, to)
    x_block, target_block = both[0], both[1]

    enc_t = enc_weight.T
    dec_t = jnp.where(reach[:, None, :], dec_weight.transpose(1, 2, 0), 0)
    square = jnp.sum(jnp.square(dec_t.astype(f32)), axis=(0, 1))
    dec_own = dec_t.reshape(3, 8, 36, 384).transpose(1, 0, 2, 3).reshape(8, 108, 384)
    dec_own = jnp.pad(dec_own, ((0, 0), (0, BLOCK - 108), (0, 0))).reshape(8 * BLOCK, 384)
    extra = jnp.stack([source.astype(bf16), *pieces(enc_bias), *pieces(square)])
    enc_own = jnp.concatenate([enc_t, jnp.pad(extra, ((0, 9), (0, 0)))])
    enc_quad = lax.all_gather(enc_own, QUAD)
    dec_quad = lax.all_gather(dec_own, QUAD)
    tail = enc_quad[:, 288:295].astype(f32)
    source_quad = tail[:, 0]
    bias_quad = (tail[:, 1] + tail[:, 2] + tail[:, 3]).reshape(1536)
    square_quad = (tail[:, 4] + tail[:, 5] + tail[:, 6]).reshape(1536)
    enc_rows = enc_quad[:, :288].reshape(4, 8, 1, 36, 384)
    pick_quad = source_quad[:, None, :] == layer_ids[None, :, None].astype(f32)
    enc_rows = jnp.where(pick_quad[:, None, :, None, :], enc_rows, 0).reshape(4, 8, 108, 384)
    enc_rows = jnp.pad(enc_rows, ((0, 0), (0, 0), (0, BLOCK - 108), (0, 0)))
    enc_rows = enc_rows.reshape(4, 8 * BLOCK, 384)

    x_quad = share(x_block, "z", 16).reshape(2, 8 * BLOCK, 128)
    partial = dot("akt,qkj->atqj", x_quad, enc_rows).reshape(8, 32, 1536)
    squares = jnp.broadcast_to(square_quad[None, None], (8, 8, 1536))
    summed = lax.all_to_all(jnp.concatenate([partial, squares], axis=1), DP, 0, 0).sum(0)
    pre = summed[:32] + bias_quad[None]
    norms = jnp.sqrt(summed[32] + norm_epsilon)
    acts = jnp.maximum(pre, 0.0).astype(bf16)
    sparsity = jnp.sum(acts.astype(f32) * norms[None])
    acts_quad = share(acts, DP, 8).reshape(2, 128, 4, 384)

    terms = dot("qkj,atqj->akt", dec_quad, acts_quad).astype(bf16).reshape(16, BLOCK, 128)
    recon_sum = lax.all_to_all(terms, "z", 0, 0).astype(f32).sum(0)
    recon = lax.ppermute(recon_sum.astype(bf16), ALL, back)
    recon = recon[:108].reshape(3, 36, 128).transpose(2, 0, 1)
    error = recon_sum - target_block.astype(f32)
    local_loss = jnp.sum(error * error) + sparsity_weight * sparsity
    gout = (2.0 * error / TOK_DEV).astype(bf16)
    loss_row = jnp.pad(jnp.stack(pieces(local_loss)), (0, 125))
    row_ids = lax.broadcasted_iota(jnp.int32, (BLOCK, 128), 0)
    gout = jnp.where(row_ids == 108, loss_row[None], gout)
    gout_all = share(gout, "z", 16)
    loss_z = jnp.sum(gout_all[:, 108, :3].astype(f32))
    gout_quad = gout_all.reshape(2, 8 * BLOCK, 128)

    slopes = dot("akt,qkj->atqj", gout_quad, dec_quad).astype(bf16).reshape(8, 32, 1536)
    slopes = lax.all_to_all(slopes, DP, 0, 0).astype(f32).sum(0)
    slopes = slopes + (sparsity_weight / TOK_DEV) * norms[None]
    dpre = jnp.where(pre > 0, slopes, 0.0)
    bias_rows = jnp.stack(pieces(dpre.sum(0))).reshape(3, 4, 384)
    loss_rows = jnp.broadcast_to(jnp.pad(jnp.stack(pieces(loss_z)), (0, 381)), (1, 4, 384))
    sent = jnp.concatenate(
        [dpre.astype(bf16).reshape(32, 4, 384), bias_rows, loss_rows, jnp.zeros((12, 4, 384), bf16)]
    )
    got = lax.all_to_all(sent.transpose(1, 0, 2), QUAD, 0, 0)
    bias_rows = jnp.stack(pieces(got[:, 32:35].astype(f32).sum((0, 1))))
    loss_row = jnp.pad(jnp.stack(pieces(got[:, 35, :3].astype(f32).sum())), (0, 381))[None]
    sent = jnp.concatenate(
        [got[:, :32].reshape(128, 384), bias_rows, loss_row, jnp.zeros((12, 384), bf16)]
    )
    got = share(sent, DP, 8)
    bias_grad = got[:, 128:131].astype(f32).sum((0, 1))
    loss = got[:, 131, :3].astype(f32).sum() / TOK_DEV
    dpre_every = got[:, :128].reshape(2, 4, 4, 32, 384).transpose(2, 0, 1, 3, 4)
    dpre_every = dpre_every.reshape(4, 2, 128, 384)

    x_every = lax.all_gather(x_quad, QUAD)
    gout_every = lax.all_gather(gout_quad, QUAD)
    acts_every = acts_quad.reshape(256, 4, 384).transpose(1, 0, 2)
    acts_every = lax.all_to_all(acts_every, QUAD, 0, 0).reshape(4, 2, 128, 384)
    enc_full = dot("qakt,qatj->kj", x_every, dpre_every)
    enc_full = enc_full.reshape(8, BLOCK, 384)[:, :108].reshape(8, 3, 36, 384)
    enc_grad = jnp.sum(jnp.where(pick[None, :, None, :], enc_full, 0.0), axis=1).reshape(288, 384)
    dec_full = dot("qakt,qatj->kj", gout_every, acts_every)
    dec_full = dec_full.reshape(8, BLOCK, 384)[:, :108].reshape(8, 3, 36, 384)
    dec_full = dec_full.transpose(1, 0, 2, 3).reshape(3, 288, 384)
    colsum = jnp.sum(acts_every.astype(f32), axis=(0, 1, 2))
    member = lax.axis_index(QUAD)
    own_norms = lax.dynamic_index_in_dim(norms.reshape(4, 384), member, 0, False)
    pull = (sparsity_weight / TOK_DEV) * colsum / own_norms
    dec_grad = jnp.where(reach[:, None, :], dec_full + pull * dec_t.astype(f32), 0.0)
    return (loss, recon, enc_grad.T, bias_grad, dec_grad.transpose(2, 0, 1))


def solution(mesh):
    fine = Mesh(np.asarray(mesh.devices).reshape(SIZES), ALL)
    in_specs = (
        P(DP, None, LATENT),
        P(DP, None, LATENT),
        P(LATENT, DP),
        P(LATENT),
        P(LATENT, None, DP),
        P(LATENT),
    )
    out_specs = (
        P(),
        P(DP, None, LATENT),
        P(LATENT, DP),
        P(LATENT),
        P(LATENT, None, DP),
    )
    return jax.shard_map(
        on_device, mesh=fine, in_specs=in_specs, out_specs=out_specs, check_vma=False
    )
```

time: 1100 us -> 295 us (0.27)
  the two profiles are of different devices: /device:TPU:1 before, /device:TPU:20 now
where the time goes in v1:
time: 295 us; the launch traced here: 294 us
  starting transfers between devices  83.1 us (28%)
  waiting for transfers between devices  76.8 us (26%)
  blocking collectives  57.3 us (19%)
  between operations  30.9 us (10%)
  local copies, waits for them, and re-layouts  20.8 us (7%)
  matrix products  13 us (4%)
  other arithmetic  12 us (4%)
    all_to_all x2, blocking collectives, share(): lax.all_to_all(jnp.broadcast_to(block[None], (count, *block.shape)), axes...  46.7 us
    all_to_all x1, waiting for transfers between devices, on_device(): recon_sum = lax.all_to_all(terms, 'z', 0, 0).astype(f32).sum(0)  22.8 us
    all_to_all x1, waiting for transfers between devices, on_device(): lax.all_to_all(jnp.concatenate([partial, squares], axis=1), DP, 0, 0).sum(0)  19.1 us
    all_to_all x2, starting transfers between devices, share(): lax.all_to_all(jnp.broadcast_to(block[None], (count, *block.shape)), axes...  15.7 us
    ppermute x1, starting transfers between devices, on_device(): both = lax.ppermute(both, ALL, to)  15.6 us
    all_to_all x1, starting transfers between devices, on_device(): recon_sum = lax.all_to_all(terms, 'z', 0, 0).astype(f32).sum(0)  15.1 us
    all_to_all x1, starting transfers between devices, on_device(): lax.all_to_all(jnp.concatenate([partial, squares], axis=1), DP, 0, 0).sum(0)  14.2 us
    all_to_all x1, waiting for transfers between devices, on_device(): acts_every = lax.all_to_all(acts_every, QUAD, 0, 0).reshape(4, 2, 128, 384)  13.9 us
  transfers between devices with their start and end apart: 12, of which 7 were waited for; matrix products, arithmetic and copies ran while one was open for 12% of the time, Pallas kernels for 0%

profile of v1, /device:TPU:20, one launch (start us, length us, event | category | flops | bytes accessed | tf_op | source)
XLA Modules:
  0.0 293.9 jit_solution(2684986245609074990)
XLA Ops:
  7.2 0.8 maximum_bitcast_fusion
  8.1 15.6 %collective-permute-start = (bf16[2,112,128]{2,0,1:T(2,128)(2,1)S(1)}, bf16[2,112,128]{2,0,1:T(2,128)(2,1)S(1)}, u32[]{:S(2)}, u32[]{:S(2)}) collective-permute-start(bf16[2,112,128]{2,0,1:T(2,128)(2,1)S(1)} %pad.27), channel_id=1, source_target_pairs={{0,0},{1,4},{2,8},{3,12},{4,16},{5,20},{6,24},{7,28},{8,64},{9,68}... | collective-permute-start | bytes 172040 | tf_op jit(solution)/shard_map/ppermute | solution.py:55
  23.7 1.3 iota_compare_fusion.1
  24.9 1.3 fusion.10
  26.6 0.9 pad.30.clone
  27.8 0.8 broadcast_in_dim.130
  28.6 7.6 %all-to-all-start = ((bf16[16,112,128]{2,1,0:T(8,128)(2,1)}), bf16[16,112,128]{2,1,0:T(8,128)(2,1)}, u32[]{:S(2)}, u32[]{:S(2)}) async-start(bf16[16,112,128]{2,1,0:T(8,128)(2,1)} %broadcast_in_dim.130), calls=%async_computation | async-start | bytes 917504 | tf_op jit(solution)/shard_map/all_to_all | solution.py:39
  36.3 10.6 %all-gather = bf16[1216,384]{1,0:T(8,128)(2,1)S(1)} all-gather(bf16[304,384]{1,0:T(8,128)(2,1)S(1)} %fusion.23), channel_id=2, replica_groups=mesh['x'=4,'yh'=2,'z'=16,'yl'=2,'c'=2] {'yl','c'}, dimensions={0}, use_global_device_ids=true | all-gather | bytes 1167360 | tf_op jit(solution)/shard_map/all_gather | solution.py:65
  47.4 0.5 copy.116
  47.8 0.2 copy.84
  48.0 0.2 broadcast_in_dim.137
  48.3 0.8 broadcast_select_fusion
  49.1 0.4 copy.117
  49.5 1.8 pad.29.clone
  51.3 3.3 %copy.86 = bf16[4,384,896]{2,1,0:T(8,128)(2,1)S(1)} copy(bf16[4,384,896]{1,2,0:T(8,128)(2,1)} %bitcast.126) | data formatting | bytes 5505024 | tf_op jit(solution)/shard_map/akt,qkj->atqj/dot_general | solution.py:43
  54.6 5.1 %all-to-all-done = bf16[16,112,128]{2,1,0:T(8,128)(2,1)} async-done(((bf16[16,112,128]{2,1,0:T(8,128)(2,1)}), bf16[16,112,128]{2,1,0:T(8,128)(2,1)}, u32[]{:S(2)}, u32[]{:S(2)}) %all-to-all-start) | async-done | bytes 458784 | tf_op jit(solution)/shard_map/all_to_all | solution.py:39
  59.7 2.0 copy.81
  61.7 2.0 fusion.48
  63.8 1.4 pad_maximum_fusion
  65.2 14.2 %all-to-all-start.1 = ((f32[8,40,1536]{2,1,0:T(8,128)}), f32[8,40,1536]{2,1,0:T(8,128)S(1)}, u32[]{:S(2)}, u32[]{:S(2)}) async-start(f32[8,40,1536]{2,1,0:T(8,128)} %pad_maximum_fusion), calls=%async_computation.1 | async-start | bytes 3932160 | tf_op jit(solution)/shard_map/all_to_all | solution.py:80
  79.5 19.1 %all-to-all-done.1 = f32[8,40,1536]{2,1,0:T(8,128)S(1)} async-done(((f32[8,40,1536]{2,1,0:T(8,128)}), f32[8,40,1536]{2,1,0:T(8,128)S(1)}, u32[]{:S(2)}, u32[]{:S(2)}) %all-to-all-start.1) | async-done | bytes 1966112 | tf_op jit(solution)/shard_map/all_to_all | solution.py:80
  98.8 0.7 multiply_reduce_fusion
  99.5 15.5 %all_to_all.45 = bf16[8,32,1536]{2,1,0:T(8,128)(2,1)S(1)} all-to-all(bf16[8,32,1536]{2,1,0:T(8,128)(2,1)S(1)} %broadcast_in_dim.141), channel_id=1, replica_groups=mesh['x'=4,'yh'=2,'z'=16,'yl'=2,'c'=2] {'x','yh'}, dimensions={0} | all-to-all | bytes 1572864 | tf_op jit(solution)/shard_map/all_to_all | solution.py:39
  115.0 0.2 reshape.306
  115.2 2.8 fusion.17
  118.0 1.0 copy.90
  119.0 15.1 %all-to-all-start.3 = ((bf16[16,112,128]{2,1,0:T(8,128)(2,1)}), bf16[16,112,128]{2,1,0:T(8,128)(2,1)S(1)}, u32[]{:S(2)}, u32[]{:S(2)}) async-start(bf16[16,112,128]{2,1,0:T(8,128)(2,1)} %bitcast.24), calls=%async_computation.3 | async-start | bytes 917504 | tf_op jit(solution)/shard_map/all_to_all | solution.py:88
  134.2 0.7 all-gather.7.cloned.1.call-update
  135.5 22.8 %all-to-all-done.3 = bf16[16,112,128]{2,1,0:T(8,128)(2,1)S(1)} async-done(((bf16[16,112,128]{2,1,0:T(8,128)(2,1)}), bf16[16,112,128]{2,1,0:T(8,128)(2,1)S(1)}, u32[]{:S(2)}, u32[]{:S(2)}) %all-to-all-start.3) | async-done | bytes 458784 | tf_op jit(solution)/shard_map/all_to_all | solution.py:88
  158.3 0.6 fusion.47
  163.3 0.2 broadcast_select_fusion.1
  163.6 31.3 %all_to_all.46 = bf16[16,112,128]{2,1,0:T(8,128)(2,1)S(1)} all-to-all(bf16[16,112,128]{2,1,0:T(8,128)(2,1)S(1)} %broadcast_in_dim.144), channel_id=1, replica_groups=mesh['x'=4,'yh'=2,'z'=16,'yl'=2,'c'=2] {'z'}, dimensions={0} | all-to-all | bytes 917504 | tf_op jit(solution)/shard_map/all_to_all | solution.py:39
  194.8 2.9 %fusion.4 = bf16[2,128,4,384]{3,1,2,0:T(8,128)(2,1)S(1)} fusion(bf16[2,896,128,1]{2,1,3,0:T(8,128)(2,1)S(1)} %bitcast.130, bf16[4,896,384]{2,1,0:T(8,128)(2,1)} %all-gather.5.cloned.1.call-done), kind=kOutput, calls=%fused_computation.12 | convolution fusion | flops 705036288 | bytes 3997696 | tf_op jit(solution)/shard_map/akt,qkj->atqj/dot_general | solution.py:43
  197.8 0.6 copy.92
  198.4 1.2 reshape.311
  199.6 7.4 %all-to-all-start.5 = ((bf16[8,32,1536]{2,1,0:T(8,128)(2,1)}), bf16[8,32,1536]{2,1,0:T(8,128)(2,1)S(1)}, u32[]{:S(2)}, u32[]{:S(2)}) async-start(bf16[8,32,1536]{2,1,0:T(8,128)(2,1)} %reshape.311), calls=%async_computation.5 | async-start | bytes 1572864 | tf_op jit(solution)/shard_map/all_to_all | solution.py:102
  207.0 0.6 fusion.26
  212.7 0.9 all-to-all-done.5
  214.0 0.7 copy.93
  214.6 4.2 %all-to-all-start.6 = ((bf16[4,48,384]{2,1,0:T(8,128)(2,1)}), bf16[4,48,384]{2,1,0:T(8,128)(2,1)S(1)}, u32[]{:S(2)}, u32[]{:S(2)}) async-start(bf16[4,48,384]{2,1,0:T(8,128)(2,1)} %copy.93), calls=%async_computation.6 | async-start | bytes 294912 | tf_op jit(solution)/shard_map/all_to_all | solution.py:110
  218.8 0.2 reshape_reshape.3
  219.0 1.0 copy.99
  220.0 3.6 %all-to-all-done.6 = bf16[4,48,384]{2,1,0:T(8,128)(2,1)S(1)} async-done(((bf16[4,48,384]{2,1,0:T(8,128)(2,1)}), bf16[4,48,384]{2,1,0:T(8,128)(2,1)S(1)}, u32[]{:S(2)}, u32[]{:S(2)}) %all-to-all-start.6) | async-done | bytes 147488 | tf_op jit(solution)/shard_map/all_to_all | solution.py:110
  223.6 3.7 %all-to-all-start.8 = ((bf16[4,256,384]{2,1,0:T(8,128)(2,1)}), bf16[4,256,384]{2,1,0:T(8,128)(2,1)S(1)}, u32[]{:S(2)}, u32[]{:S(2)}) async-start(bf16[4,256,384]{2,1,0:T(8,128)(2,1)} %copy.99), calls=%async_computation.8 | async-start | bytes 1572864 | tf_op jit(solution)/shard_map/all_to_all | solution.py:125
  227.3 0.6 fusion.33
  233.0 0.2 concatenate.17
  233.2 13.9 %all-to-all-done.8 = bf16[4,256,384]{2,1,0:T(8,128)(2,1)S(1)} async-done(((bf16[4,256,384]{2,1,0:T(8,128)(2,1)}), bf16[4,256,384]{2,1,0:T(8,128)(2,1)S(1)}, u32[]{:S(2)}, u32[]{:S(2)}) %all-to-all-start.8) | async-done | bytes 786464 | tf_op jit(solution)/shard_map/all_to_all | solution.py:125
  247.1 1.0 broadcast_in_dim.149
  248.1 8.1 %all-to-all-start.7 = ((bf16[8,144,384]{2,1,0:T(8,128)(2,1)}), bf16[8,144,384]{2,1,0:T(8,128)(2,1)S(1)}, u32[]{:S(2)}, u32[]{:S(2)}) async-start(bf16[8,144,384]{2,1,0:T(8,128)(2,1)} %broadcast_in_dim.149), calls=%async_computation.7 | async-start | bytes 1769472 | tf_op jit(solution)/shard_map/all_to_all | solution.py:39
  256.2 0.2 convert_reduce_fusion
  256.3 7.2 %collective-permute-start.1 = (bf16[112,128]{1,0:T(8,128)(2,1)S(1)}, bf16[112,128]{1,0:T(8,128)(2,1)S(1)}, u32[]{:S(2)}, u32[]{:S(2)}) collective-permute-start(bf16[112,128]{1,0:T(8,128)(2,1)S(1)} %get-tuple-element.15), channel_id=1, source_target_pairs={{0,0},{4,1},{8,2},{12,3},{16,4},{20,5},{24,6},{28,7},{64,8},{68,9}... | collective-permute-start | bytes 86024 | tf_op jit(solution)/shard_map/ppermute | solution.py:89
  263.5 10.6 %collective-permute-done.1 = bf16[112,128]{1,0:T(8,128)(2,1)S(1)} collective-permute-done((bf16[112,128]{1,0:T(8,128)(2,1)S(1)}, bf16[112,128]{1,0:T(8,128)(2,1)S(1)}, u32[]{:S(2)}, u32[]{:S(2)}) %collective-permute-start.1) | collective-permute-done | bytes 28704 | tf_op jit(solution)/shard_map/ppermute | solution.py:89
  274.1 0.6 reshape.314
  275.0 2.6 convolution_bitcast_fusion.1
  277.6 0.4 copy.96
  278.0 0.2 copy-done.5
  278.5 0.8 reshape.318
  279.3 0.6 fusion.31
  280.5 0.6 convert_reduce_fusion.3
  281.1 2.6 convolution_bitcast_fusion
  283.7 0.4 copy.101
  284.2 0.2 copy.102
  284.6 0.5 copy-done.3
  285.0 1.2 fusion.13
  (82 shorter events, 2.7 us)
Async XLA Ops:
  7.2 108.0 %all-gather.5.cloned.1.call-start = ((), (), s32[]{:S(2)}) async-start(), calls=%async_computation.9 | async-start | bytes 3440640 | tf_op jit(solution)/shard_map/all_gather | solution.py:66
  8.1 19.6 %collective-permute-start = (bf16[2,112,128]{2,0,1:T(2,128)(2,1)S(1)}, bf16[2,112,128]{2,0,1:T(2,128)(2,1)S(1)}, u32[]{:S(2)}, u32[]{:S(2)}) collective-permute-start(bf16[2,112,128]{2,0,1:T(2,128)(2,1)S(1)} %pad.27), channel_id=1, source_target_pairs={{0,0},{1,4},{2,8},{3,12},{4,16},{5,20},{6,24},{7,28},{8,64},{9,68}... | collective-permute-start | bytes 172040 | tf_op jit(solution)/shard_map/ppermute | solution.py:55
  24.9 1.6 copy-start.2
  26.5 1.1 copy-start.6
  26.5 1.1 copy-start.4
  26.6 9.7 %copy-start.1 = (bf16[384,288]{0,1:T(8,128)(2,1)S(1)}, bf16[384,288]{0,1:T(8,128)(2,1)}, u32[]{:S(2)}) copy-start(bf16[384,288]{0,1:T(8,128)(2,1)} %param.8) | copy-start | bytes 663556
  28.6 31.1 %all-to-all-start = ((bf16[16,112,128]{2,1,0:T(8,128)(2,1)}), bf16[16,112,128]{2,1,0:T(8,128)(2,1)}, u32[]{:S(2)}, u32[]{:S(2)}) async-start(bf16[16,112,128]{2,1,0:T(8,128)(2,1)} %broadcast_in_dim.130), calls=%async_computation | async-start | bytes 917504 | tf_op jit(solution)/shard_map/all_to_all | solution.py:39
  65.2 33.4 %all-to-all-start.1 = ((f32[8,40,1536]{2,1,0:T(8,128)}), f32[8,40,1536]{2,1,0:T(8,128)S(1)}, u32[]{:S(2)}, u32[]{:S(2)}) async-start(f32[8,40,1536]{2,1,0:T(8,128)} %pad_maximum_fusion), calls=%async_computation.1 | async-start | bytes 3932160 | tf_op jit(solution)/shard_map/all_to_all | solution.py:80
  119.0 39.3 %all-to-all-start.3 = ((bf16[16,112,128]{2,1,0:T(8,128)(2,1)}), bf16[16,112,128]{2,1,0:T(8,128)(2,1)S(1)}, u32[]{:S(2)}, u32[]{:S(2)}) async-start(bf16[16,112,128]{2,1,0:T(8,128)(2,1)} %bitcast.24), calls=%async_computation.3 | async-start | bytes 917504 | tf_op jit(solution)/shard_map/all_to_all | solution.py:88
  134.1 140.9 %all-gather.7.cloned.1.call-start = ((), (), s32[]{:S(2)}) async-start(), calls=%async_computation.10 | async-start | bytes 2293760 | tf_op jit(solution)/shard_map/all_gather | solution.py:122
  194.8 12.2 %copy-start = (bf16[16,112,128]{2,1,0:T(8,128)(2,1)}, bf16[16,112,128]{2,1,0:T(8,128)(2,1)S(1)}, u32[]{:S(2)}) copy-start(bf16[16,112,128]{2,1,0:T(8,128)(2,1)S(1)} %all_to_all.46) | copy-start | bytes 1376260
  199.6 14.0 %all-to-all-start.5 = ((bf16[8,32,1536]{2,1,0:T(8,128)(2,1)}), bf16[8,32,1536]{2,1,0:T(8,128)(2,1)S(1)}, u32[]{:S(2)}, u32[]{:S(2)}) async-start(bf16[8,32,1536]{2,1,0:T(8,128)(2,1)} %reshape.311), calls=%async_computation.5 | async-start | bytes 1572864 | tf_op jit(solution)/shard_map/all_to_all | solution.py:102
  207.0 74.1 %all-gather.9.cloned.1.call-start = ((), (), s32[]{:S(2)}) async-start(), calls=%async_computation.11 | async-start | bytes 2293760 | tf_op jit(solution)/shard_map/all_gather | solution.py:123
  214.6 9.0 %all-to-all-start.6 = ((bf16[4,48,384]{2,1,0:T(8,128)(2,1)}), bf16[4,48,384]{2,1,0:T(8,128)(2,1)S(1)}, u32[]{:S(2)}, u32[]{:S(2)}) async-start(bf16[4,48,384]{2,1,0:T(8,128)(2,1)} %copy.93), calls=%async_computation.6 | async-start | bytes 294912 | tf_op jit(solution)/shard_map/all_to_all | solution.py:110
  223.6 23.5 %all-to-all-start.8 = ((bf16[4,256,384]{2,1,0:T(8,128)(2,1)}), bf16[4,256,384]{2,1,0:T(8,128)(2,1)S(1)}, u32[]{:S(2)}, u32[]{:S(2)}) async-start(bf16[4,256,384]{2,1,0:T(8,128)(2,1)} %copy.99), calls=%async_computation.8 | async-start | bytes 1572864 | tf_op jit(solution)/shard_map/all_to_all | solution.py:125
  248.1 26.7 %all-to-all-start.7 = ((bf16[8,144,384]{2,1,0:T(8,128)(2,1)}), bf16[8,144,384]{2,1,0:T(8,128)(2,1)S(1)}, u32[]{:S(2)}, u32[]{:S(2)}) async-start(bf16[8,144,384]{2,1,0:T(8,128)(2,1)} %broadcast_in_dim.149), calls=%async_computation.7 | async-start | bytes 1769472 | tf_op jit(solution)/shard_map/all_to_all | solution.py:39
  256.3 17.8 %collective-permute-start.1 = (bf16[112,128]{1,0:T(8,128)(2,1)S(1)}, bf16[112,128]{1,0:T(8,128)(2,1)S(1)}, u32[]{:S(2)}, u32[]{:S(2)}) collective-permute-start(bf16[112,128]{1,0:T(8,128)(2,1)S(1)} %get-tuple-element.15), channel_id=1, source_target_pairs={{0,0},{4,1},{8,2},{12,3},{16,4},{20,5},{24,6},{28,7},{64,8},{68,9}... | collective-permute-start | bytes 86024 | tf_op jit(solution)/shard_map/ppermute | solution.py:89
  277.6 0.7 copy-start.5
  284.4 0.6 copy-start.3
Sparse Core Ops, SparseCore 0:
  27.7 37.5 all-gather.4
  137.0 36.9 all-gather.6
  212.7 40.2 all-gather.8

commit v2 on v1

--- a/solution.py
+++ b/solution.py
@@ -39,6 +39,25 @@
     return lax.all_to_all(jnp.broadcast_to(block[None], (count, *block.shape)), axes, 0, 0)
 
 
+def neighbour(block, axis):
+    return lax.ppermute(block, axis, [(0, 1), (1, 0)])
+
+
+def quad_of(block):
+    pair = jnp.stack([block, neighbour(block, "yl")])
+    other = neighbour(pair, "c")
+    return jnp.stack([pair[0], other[0], pair[1], other[1]])
+
+
+def relative(blocks):
+    yl, c = lax.axis_index("yl"), lax.axis_index("c")
+    blocks = jnp.where(yl == 1, blocks[jnp.array([2, 3, 0, 1])], blocks)
+    return jnp.where(c == 1, blocks[jnp.array([1, 0, 3, 2])], blocks)
+
+
+together = lax.optimization_barrier
+
+
 def dot(spec, a, b):
     return jnp.einsum(spec, a, b, preferred_element_type=f32)
 
@@ -52,18 +71,20 @@
 
     both = jnp.stack([resid, target]).transpose(0, 2, 3, 1).reshape(2, 108, 128)
     both = jnp.pad(both, ((0, 0), (0, BLOCK - 108), (0, 0)))
+    both, enc_weight, dec_weight = together((both, enc_weight, dec_weight))
     both = lax.ppermute(both, ALL, to)
-    x_block, target_block = both[0], both[1]
 
     enc_t = enc_weight.T
     dec_t = jnp.where(reach[:, None, :], dec_weight.transpose(1, 2, 0), 0)
     square = jnp.sum(jnp.square(dec_t.astype(f32)), axis=(0, 1))
+    extra = jnp.stack([source.astype(bf16), *pieces(enc_bias), *pieces(square)])
+    enc_own = jnp.concatenate([enc_t, jnp.pad(extra, ((0, 9), (0, 0)))])
+    enc_quad = quad_of(enc_own)
     dec_own = dec_t.reshape(3, 8, 36, 384).transpose(1, 0, 2, 3).reshape(8, 108, 384)
     dec_own = jnp.pad(dec_own, ((0, 0), (0, BLOCK - 108), (0, 0))).reshape(8 * BLOCK, 384)
-    extra = jnp.stack([source.astype(bf16), *pieces(enc_bias), *pieces(square)])
-    enc_own = jnp.concatenate([enc_t, jnp.pad(extra, ((0, 9), (0, 0)))])
-    enc_quad = lax.all_gather(enc_own, QUAD)
-    dec_quad = lax.all_gather(dec_own, QUAD)
+    dec_own, both, enc_quad = together((dec_own, both, enc_quad))
+    dec_quad = quad_of(dec_own)
+    x_block, target_block = both[0], both[1]
     tail = enc_quad[:, 288:295].astype(f32)
     source_quad = tail[:, 0]
     bias_quad = (tail[:, 1] + tail[:, 2] + tail[:, 3]).reshape(1536)
@@ -75,54 +96,65 @@
     enc_rows = enc_rows.reshape(4, 8 * BLOCK, 384)
 
     x_quad = share(x_block, "z", 16).reshape(2, 8 * BLOCK, 128)
+    x_quad, enc_rows, dec_quad = together((x_quad, enc_rows, dec_quad))
     partial = dot("akt,qkj->atqj", x_quad, enc_rows).reshape(8, 32, 1536)
     squares = jnp.broadcast_to(square_quad[None, None], (8, 8, 1536))
     summed = lax.all_to_all(jnp.concatenate([partial, squares], axis=1), DP, 0, 0).sum(0)
     pre = summed[:32] + bias_quad[None]
     norms = jnp.sqrt(summed[32] + norm_epsilon)
     acts = jnp.maximum(pre, 0.0).astype(bf16)
-    sparsity = jnp.sum(acts.astype(f32) * norms[None])
+    sparsity = jnp.sum(acts.astype(f32) * norms[None], axis=0).reshape(12, 128).sum(0)
     acts_quad = share(acts, DP, 8).reshape(2, 128, 4, 384)
 
     terms = dot("qkj,atqj->akt", dec_quad, acts_quad).astype(bf16).reshape(16, BLOCK, 128)
+    terms, acts_sent, x_sent = together((terms, acts_quad, x_quad))
     recon_sum = lax.all_to_all(terms, "z", 0, 0).astype(f32).sum(0)
-    recon = lax.ppermute(recon_sum.astype(bf16), ALL, back)
+    acts_sent = acts_sent.reshape(256, 4, 384).transpose(1, 0, 2)
+    kept, away = acts_sent[:2], acts_sent[2:]
+    away = neighbour(away, "yl")
+    acts_every = jnp.stack([kept[0], away[0]])
+    away = neighbour(jnp.stack([kept[1], away[1]]), "c")
+    acts_every = jnp.stack([acts_every[0], away[0], acts_every[1], away[1]])
+    acts_every = relative(acts_every).reshape(4, 2, 128, 384)
+    recon_sum, acts_every = together((recon_sum, acts_every))
+    x_every = lax.all_gather(x_sent, QUAD)
+    error = recon_sum - target_block.astype(f32)
+    local_loss = jnp.sum(error * error, axis=0) + sparsity_weight * sparsity
+    gout = (2.0 * error / TOK_DEV).astype(bf16)
+    row_ids = lax.broadcasted_iota(jnp.int32, (BLOCK, 128), 0)
+    for row, piece in enumerate(pieces(local_loss)):
+        gout = jnp.where(row_ids == 108 + row, piece[None], gout)
+    gout, recon = together((gout, recon_sum.astype(bf16)))
+    recon = lax.ppermute(recon, ALL, back)
+    gout_all = share(gout, "z", 16)
+    gout_all, recon = together((gout_all, recon))
     recon = recon[:108].reshape(3, 36, 128).transpose(2, 0, 1)
-    error = recon_sum - target_block.astype(f32)
-    local_loss = jnp.sum(error * error) + sparsity_weight * sparsity
-    gout = (2.0 * error / TOK_DEV).astype(bf16)
-    loss_row = jnp.pad(jnp.stack(pieces(local_loss)), (0, 125))
-    row_ids = lax.broadcasted_iota(jnp.int32, (BLOCK, 128), 0)
-    gout = jnp.where(row_ids == 108, loss_row[None], gout)
-    gout_all = share(gout, "z", 16)
-    loss_z = jnp.sum(gout_all[:, 108, :3].astype(f32))
+    loss_z = jnp.sum(gout_all[:, 108:111].astype(f32), axis=(0, 1))
     gout_quad = gout_all.reshape(2, 8 * BLOCK, 128)
 
+    gout_every = lax.all_gather(gout_quad, QUAD)
     slopes = dot("akt,qkj->atqj", gout_quad, dec_quad).astype(bf16).reshape(8, 32, 1536)
     slopes = lax.all_to_all(slopes, DP, 0, 0).astype(f32).sum(0)
     slopes = slopes + (sparsity_weight / TOK_DEV) * norms[None]
     dpre = jnp.where(pre > 0, slopes, 0.0)
     bias_rows = jnp.stack(pieces(dpre.sum(0))).reshape(3, 4, 384)
-    loss_rows = jnp.broadcast_to(jnp.pad(jnp.stack(pieces(loss_z)), (0, 381)), (1, 4, 384))
+    loss_rows = jnp.broadcast_to(jnp.concatenate(pieces(loss_z)), (1, 4, 384))
     sent = jnp.concatenate(
         [dpre.astype(bf16).reshape(32, 4, 384), bias_rows, loss_rows, jnp.zeros((12, 4, 384), bf16)]
     )
-    got = lax.all_to_all(sent.transpose(1, 0, 2), QUAD, 0, 0)
+    got = lax.all_to_all(relative(sent.transpose(1, 0, 2)), QUAD, 0, 0)
     bias_rows = jnp.stack(pieces(got[:, 32:35].astype(f32).sum((0, 1))))
-    loss_row = jnp.pad(jnp.stack(pieces(got[:, 35, :3].astype(f32).sum())), (0, 381))[None]
+    loss_q = got[:, 35].astype(f32).sum(0).reshape(3, 128).sum(0)
+    loss_row = jnp.concatenate(pieces(loss_q))[None]
     sent = jnp.concatenate(
         [got[:, :32].reshape(128, 384), bias_rows, loss_row, jnp.zeros((12, 384), bf16)]
     )
     got = share(sent, DP, 8)
     bias_grad = got[:, 128:131].astype(f32).sum((0, 1))
-    loss = got[:, 131, :3].astype(f32).sum() / TOK_DEV
+    loss = got[:, 131].astype(f32).sum() / TOK_DEV
     dpre_every = got[:, :128].reshape(2, 4, 4, 32, 384).transpose(2, 0, 1, 3, 4)
     dpre_every = dpre_every.reshape(4, 2, 128, 384)
 
-    x_every = lax.all_gather(x_quad, QUAD)
-    gout_every = lax.all_gather(gout_quad, QUAD)
-    acts_every = acts_quad.reshape(256, 4, 384).transpose(1, 0, 2)
-    acts_every = lax.all_to_all(acts_every, QUAD, 0, 0).reshape(4, 2, 128, 384)
     enc_full = dot("qakt,qatj->kj", x_every, dpre_every)
     enc_full = enc_full.reshape(8, BLOCK, 384)[:, :108].reshape(8, 3, 36, 384)
     enc_grad = jnp.sum(jnp.where(pick[None, :, None, :], enc_full, 0.0), axis=1).reshape(288, 384)
@@ -130,8 +162,7 @@
     dec_full = dec_full.reshape(8, BLOCK, 384)[:, :108].reshape(8, 3, 36, 384)
     dec_full = dec_full.transpose(1, 0, 2, 3).reshape(3, 288, 384)
     colsum = jnp.sum(acts_every.astype(f32), axis=(0, 1, 2))
-    member = lax.axis_index(QUAD)
-    own_norms = lax.dynamic_index_in_dim(norms.reshape(4, 384), member, 0, False)
+    own_norms = norms[:384]
     pull = (sparsity_weight / TOK_DEV) * colsum / own_norms
     dec_grad = jnp.where(reach[:, None, :], dec_full + pull * dec_t.astype(f32), 0.0)
     return (loss, recon, enc_grad.T, bias_grad, dec_grad.transpose(2, 0, 1))

time: 295 us -> 334 us (1.13)
  the two profiles are of different devices: /device:TPU:20 before, /device:TPU:1 now
where the time goes in v2:
time: 334 us; the launch traced here: 332 us
  waiting for transfers between devices  103 us (31%)
  starting transfers between devices  102 us (31%)
  local copies, waits for them, and re-layouts  35.5 us (11%)
  other arithmetic  34.9 us (10%)
  blocking collectives  29.8 us (9%)
  between operations  16.6 us (5%)
  matrix products  9.42 us (3%)
    all_to_all x3, starting transfers between devices, share(): lax.all_to_all(jnp.broadcast_to(block[None], (count, *block.shape)), axes...  37 us
    ppermute x6, starting transfers between devices, neighbour(): return lax.ppermute(block, axis, [(0, 1), (1, 0)])  29.2 us
    all_to_all x3, waiting for transfers between devices, share(): lax.all_to_all(jnp.broadcast_to(block[None], (count, *block.shape)), axes...  26.9 us
    all_to_all x1, waiting for transfers between devices, on_device(): lax.all_to_all(jnp.concatenate([partial, squares], axis=1), DP, 0, 0).sum(0)  23 us
    ppermute x1, waiting for transfers between devices, on_device(): recon = lax.ppermute(recon, ALL, back)  22.3 us
    ppermute x6, waiting for transfers between devices, neighbour(): return lax.ppermute(block, axis, [(0, 1), (1, 0)])  19 us
    all_to_all x1, starting transfers between devices, on_device(): recon_sum = lax.all_to_all(terms, 'z', 0, 0).astype(f32).sum(0)  17.3 us
    all_to_all x1, blocking collectives, share(): lax.all_to_all(jnp.broadcast_to(block[None], (count, *block.shape)), axes...  16.1 us
  transfers between devices with their start and end apart: 16, of which 8 were waited for; matrix products, arithmetic and copies ran while one was open for 14% of the time, Pallas kernels for 0%

profile of v2, /device:TPU:1, one launch (start us, length us, event | category | flops | bytes accessed | tf_op | source)
XLA Modules:
  0.0 331.8 jit_solution(9747236607879725132)
XLA Ops:
  7.2 1.3 iota_compare_fusion.1
  10.0 1.3 fusion.12
  12.3 4.0 %collective-permute-start.1 = (bf16[304,384]{1,0:T(8,128)(2,1)S(1)}, bf16[304,384]{1,0:T(8,128)(2,1)S(1)}, u32[]{:S(2)}, u32[]{:S(2)}) collective-permute-start(bf16[304,384]{1,0:T(8,128)(2,1)S(1)} %get-tuple-element.63), channel_id=1, source_target_pairs={{0,2},{2,0},{1,3},{3,1},{4,6},{6,4},{5,7},{7,5},{8,10},{10,8},{9,1... | collective-permute-start | bytes 700424 | tf_op jit(solution)/shard_map/ppermute | solution.py:43
  16.3 3.4 %collective-permute-done.1 = bf16[304,384]{1,0:T(8,128)(2,1)S(1)} collective-permute-done((bf16[304,384]{1,0:T(8,128)(2,1)S(1)}, bf16[304,384]{1,0:T(8,128)(2,1)S(1)}, u32[]{:S(2)}, u32[]{:S(2)}) %collective-permute-start.1) | collective-permute-done | bytes 233504 | tf_op jit(solution)/shard_map/ppermute | solution.py:43
  19.8 0.8 pad_maximum_fusion.5
  20.6 9.3 %collective-permute-start.2 = (bf16[2,304,384]{2,1,0:T(8,128)(2,1)}, bf16[2,304,384]{2,1,0:T(8,128)(2,1)S(1)}, u32[]{:S(2)}, u32[]{:S(2)}) collective-permute-start(bf16[2,304,384]{2,1,0:T(8,128)(2,1)} %pad_maximum_fusion.5), channel_id=1, source_target_pairs={{0,1},{1,0},{2,3},{3,2},{4,5},{5,4},{6,7},{7,6},{8,9},{9,8},{10,11... | collective-permute-start | bytes 1400840 | tf_op jit(solution)/shard_map/ppermute | solution.py:43
  29.9 1.9 collective-permute-start
  32.4 3.1 collective-permute-done
  35.5 5.4 %collective-permute-start.3 = (bf16[896,384]{1,0:T(8,128)(2,1)S(1)}, bf16[896,384]{1,0:T(8,128)(2,1)S(1)}, u32[]{:S(2)}, u32[]{:S(2)}) collective-permute-start(bf16[896,384]{1,0:T(8,128)(2,1)S(1)} %bitcast.125), channel_id=1, source_target_pairs={{0,2},{2,0},{1,3},{3,1},{4,6},{6,4},{5,7},{7,5},{8,10},{10,8},{9,1... | collective-permute-start | bytes 2064392 | tf_op jit(solution)/shard_map/ppermute | solution.py:43
  40.9 15.6 %collective-permute-done.3 = bf16[896,384]{1,0:T(8,128)(2,1)S(1)} collective-permute-done((bf16[896,384]{1,0:T(8,128)(2,1)S(1)}, bf16[896,384]{1,0:T(8,128)(2,1)S(1)}, u32[]{:S(2)}, u32[]{:S(2)}) %collective-permute-start.3) | collective-permute-done | bytes 688160 | tf_op jit(solution)/shard_map/ppermute | solution.py:43
  56.5 1.3 pad_maximum_fusion.2
  57.8 2.3 collective-permute-start.4
  60.8 0.8 broadcast_in_dim.154
  61.7 21.4 %all-to-all-start = ((bf16[16,112,128]{2,1,0:T(8,128)(2,1)}), bf16[16,112,128]{2,1,0:T(8,128)(2,1)}, u32[]{:S(2)}, u32[]{:S(2)}) async-start(bf16[16,112,128]{2,1,0:T(8,128)(2,1)} %broadcast_in_dim.154), calls=%async_computation | async-start | bytes 917504 | tf_op jit(solution)/shard_map/all_to_all | solution.py:39
  84.4 0.8 broadcast_select_fusion
  85.6 1.8 pad.19.clone
  87.5 1.4 fusion.48
  88.9 1.4 pad_maximum_fusion
  90.4 14.2 %all-to-all-done = bf16[16,112,128]{2,1,0:T(8,128)(2,1)} async-done(((bf16[16,112,128]{2,1,0:T(8,128)(2,1)}), bf16[16,112,128]{2,1,0:T(8,128)(2,1)}, u32[]{:S(2)}, u32[]{:S(2)}) %all-to-all-start) | async-done | bytes 458784 | tf_op jit(solution)/shard_map/all_to_all | solution.py:39
  104.6 2.9 fusion.4
  107.5 2.2 copy.129
  109.7 2.8 reshape.327
  112.5 2.9 pad_maximum_fusion.1
  115.4 4.5 %all-to-all-start.1 = ((f32[8,40,1536]{2,1,0:T(8,128)}), f32[8,40,1536]{2,1,0:T(8,128)}, u32[]{:S(2)}, u32[]{:S(2)}) async-start(f32[8,40,1536]{2,1,0:T(8,128)} %pad_maximum_fusion.1), calls=%async_computation.1 | async-start | bytes 3932160 | tf_op jit(solution)/shard_map/all_to_all | solution.py:102
  119.9 23.0 %all-to-all-done.1 = f32[8,40,1536]{2,1,0:T(8,128)} async-done(((f32[8,40,1536]{2,1,0:T(8,128)}), f32[8,40,1536]{2,1,0:T(8,128)}, u32[]{:S(2)}, u32[]{:S(2)}) %all-to-all-start.1) | async-done | bytes 1966112 | tf_op jit(solution)/shard_map/all_to_all | solution.py:102
  143.0 1.7 reduce_sum.152
  146.1 16.1 %all_to_all.40 = bf16[8,32,1536]{2,1,0:T(8,128)(2,1)} all-to-all(bf16[8,32,1536]{2,1,0:T(8,128)(2,1)S(1)} %broadcast_in_dim.163), channel_id=1, replica_groups=mesh['x'=4,'yh'=2,'z'=16,'yl'=2,'c'=2] {'x','yh'}, dimensions={0} | all-to-all | bytes 1572864 | tf_op jit(solution)/shard_map/all_to_all | solution.py:39
  162.1 1.8 reshape.328
  163.9 1.8 fusion.19
  165.7 2.0 copy.131
  167.8 0.9 copy-done.7
  169.4 3.0 collective-permute-start.5
  173.0 17.3 %all-to-all-start.3 = ((bf16[16,112,128]{2,1,0:T(8,128)(2,1)}), bf16[16,112,128]{2,1,0:T(8,128)(2,1)}, u32[]{:S(2)}, u32[]{:S(2)}) async-start(bf16[16,112,128]{2,1,0:T(8,128)(2,1)} %bitcast.147), calls=%async_computation.3 | async-start | bytes 917504 | tf_op jit(solution)/shard_map/all_to_all | solution.py:111
  190.4 1.1 fusion.49
  192.3 5.2 %collective-permute-start.6 = (bf16[2,256,384]{2,1,0:T(8,128)(2,1)}, bf16[2,256,384]{2,1,0:T(8,128)(2,1)S(1)}, u32[]{:S(2)}, u32[]{:S(2)}) collective-permute-start(bf16[2,256,384]{2,1,0:T(8,128)(2,1)} %pad_maximum_fusion.6), channel_id=1, source_target_pairs={{0,1},{1,0},{2,3},{3,2},{4,5},{5,4},{6,7},{7,6},{8,9},{9,8},{10,11... | collective-permute-start | bytes 1179656 | tf_op jit(solution)/shard_map/ppermute | solution.py:43
  198.1 1.3 pad_clamp_fusion.1
  199.4 1.2 pad_clamp_fusion
  200.6 1.2 bitcast_reduce_fusion
  202.6 1.0 pad_maximum_fusion.4
  203.6 2.0 gather_fusion
  205.6 2.2 broadcast_select_fusion.1
  207.9 2.8 gather_fusion.1
  210.7 2.5 fusion.22
  213.2 1.1 convert_reduce_fusion.2
  214.2 0.9 fusion.53
  215.7 1.0 fusion.33
  216.7 0.8 broadcast_in_dim.169
  217.5 11.7 %all-to-all-start.4 = ((bf16[16,112,128]{2,1,0:T(8,128)(2,1)}), bf16[16,112,128]{2,1,0:T(8,128)(2,1)S(1)}, u32[]{:S(2)}, u32[]{:S(2)}) async-start(bf16[16,112,128]{2,1,0:T(8,128)(2,1)} %broadcast_in_dim.169), calls=%async_computation.4 | async-start | bytes 917504 | tf_op jit(solution)/shard_map/all_to_all | solution.py:39
  229.2 1.9 collective-permute-start.7
  231.1 22.3 %collective-permute-done.7 = bf16[112,128]{1,0:T(8,128)(2,1)S(1)} collective-permute-done((bf16[112,128]{1,0:T(8,128)(2,1)S(1)}, bf16[112,128]{1,0:T(8,128)(2,1)S(1)}, u32[]{:S(2)}, u32[]{:S(2)}) %collective-permute-start.7) | collective-permute-done | bytes 28704 | tf_op jit(solution)/shard_map/ppermute | solution.py:128
  253.4 1.0 fusion.6
  255.1 1.2 reshape.333
  256.2 10.2 %all-to-all-start.5 = ((bf16[8,32,1536]{2,1,0:T(8,128)(2,1)}), bf16[8,32,1536]{2,1,0:T(8,128)(2,1)S(1)}, u32[]{:S(2)}, u32[]{:S(2)}) async-start(bf16[8,32,1536]{2,1,0:T(8,128)(2,1)} %reshape.333), calls=%async_computation.5 | async-start | bytes 1572864 | tf_op jit(solution)/shard_map/all_to_all | solution.py:137
  268.0 8.3 %all-to-all-done.5 = bf16[8,32,1536]{2,1,0:T(8,128)(2,1)S(1)} async-done(((bf16[8,32,1536]{2,1,0:T(8,128)(2,1)}), bf16[8,32,1536]{2,1,0:T(8,128)(2,1)S(1)}, u32[]{:S(2)}, u32[]{:S(2)}) %all-to-all-start.5) | async-done | bytes 786464 | tf_op jit(solution)/shard_map/all_to_all | solution.py:137
  278.4 13.7 %all_to_all.41 = bf16[4,48,384]{2,1,0:T(8,128)(2,1)S(1)} all-to-all(bf16[4,48,384]{2,1,0:T(8,128)(2,1)S(1)} %broadcast_select_fusion.3), channel_id=1, replica_groups=mesh['x'=4,'yh'=2,'z'=16,'yl'=2,'c'=2] {'yl','c'}, dimensions={0} | all-to-all | bytes 294912 | tf_op jit(solution)/shard_map/all_to_all | solution.py:145
  292.5 1.0 broadcast_in_dim.176
  293.5 3.9 %all-to-all-start.7 = ((bf16[8,144,384]{2,1,0:T(8,128)(2,1)}), bf16[8,144,384]{2,1,0:T(8,128)(2,1)S(1)}, u32[]{:S(2)}, u32[]{:S(2)}) async-start(bf16[8,144,384]{2,1,0:T(8,128)(2,1)} %broadcast_in_dim.176), calls=%async_computation.7 | async-start | bytes 1769472 | tf_op jit(solution)/shard_map/all_to_all | solution.py:39
  298.3 1.6 copy.139
  300.6 12.7 %all-to-all-done.7 = bf16[8,144,384]{2,1,0:T(8,128)(2,1)S(1)} async-done(((bf16[8,144,384]{2,1,0:T(8,128)(2,1)}), bf16[8,144,384]{2,1,0:T(8,128)(2,1)S(1)}, u32[]{:S(2)}, u32[]{:S(2)}) %all-to-all-start.7) | async-done | bytes 884768 | tf_op jit(solution)/shard_map/all_to_all | solution.py:39
  313.5 1.1 convolution_bitcast_fusion
  315.5 0.8 reshape.341
  318.2 2.6 fusion.23
  321.6 0.9 copy-done.1
  322.5 1.2 fusion.15
  (131 shorter events, 20.1 us)
Async XLA Ops:
  7.2 5.1 %copy-start.12 = (bf16[384,288]{0,1:T(8,128)(2,1)S(1)}, bf16[384,288]{0,1:T(8,128)(2,1)}, u32[]{:S(2)}) copy-start(bf16[384,288]{0,1:T(8,128)(2,1)} %param.12) | copy-start | bytes 663556
  8.5 3.8 %copy-start.13 = (pred[3,384]{1,0:T(4,128)(4,1)}, pred[3,384]{1,0:T(4,128)(4,1)S(1)}, u32[]{:S(2)}) copy-start(pred[3,384]{1,0:T(4,128)(4,1)S(1)} %get-tuple-element.73) | copy-start | bytes 3460
  11.4 20.6 %copy-start = (bf16[3,288,384]{2,1,0:T(8,128)(2,1)}, bf16[3,288,384]{2,1,0:T(8,128)(2,1)S(1)}, u32[]{:S(2)}) copy-start(bf16[3,288,384]{2,1,0:T(8,128)(2,1)S(1)} %get-tuple-element.49) | copy-start | bytes 1990660
  12.3 7.5 %collective-permute-start.1 = (bf16[304,384]{1,0:T(8,128)(2,1)S(1)}, bf16[304,384]{1,0:T(8,128)(2,1)S(1)}, u32[]{:S(2)}, u32[]{:S(2)}) collective-permute-start(bf16[304,384]{1,0:T(8,128)(2,1)S(1)} %get-tuple-element.63), channel_id=1, source_target_pairs={{0,2},{2,0},{1,3},{3,1},{4,6},{6,4},{5,7},{7,5},{8,10},{10,8},{9,1... | collective-permute-start | bytes 700424 | tf_op jit(solution)/shard_map/ppermute | solution.py:43
  20.6 11.6 %collective-permute-start.2 = (bf16[2,304,384]{2,1,0:T(8,128)(2,1)}, bf16[2,304,384]{2,1,0:T(8,128)(2,1)S(1)}, u32[]{:S(2)}, u32[]{:S(2)}) collective-permute-start(bf16[2,304,384]{2,1,0:T(8,128)(2,1)} %pad_maximum_fusion.5), channel_id=1, source_target_pairs={{0,1},{1,0},{2,3},{3,2},{4,5},{5,4},{6,7},{7,6},{8,9},{9,8},{10,11... | collective-permute-start | bytes 1400840 | tf_op jit(solution)/shard_map/ppermute | solution.py:43
  29.9 5.7 %collective-permute-start = (bf16[2,112,128]{2,0,1:T(2,128)(2,1)S(1)}, bf16[2,112,128]{2,0,1:T(2,128)(2,1)S(1)}, u32[]{:S(2)}, u32[]{:S(2)}) collective-permute-start(bf16[2,112,128]{2,0,1:T(2,128)(2,1)S(1)} %pad.16), channel_id=1, source_target_pairs={{0,0},{1,4},{2,8},{3,12},{4,16},{5,20},{6,24},{7,28},{8,64},{9,68}... | collective-permute-start | bytes 172040 | tf_op jit(solution)/shard_map/ppermute | solution.py:75
  35.5 21.0 %collective-permute-start.3 = (bf16[896,384]{1,0:T(8,128)(2,1)S(1)}, bf16[896,384]{1,0:T(8,128)(2,1)S(1)}, u32[]{:S(2)}, u32[]{:S(2)}) collective-permute-start(bf16[896,384]{1,0:T(8,128)(2,1)S(1)} %bitcast.125), channel_id=1, source_target_pairs={{0,2},{2,0},{1,3},{3,1},{4,6},{6,4},{5,7},{7,5},{8,10},{10,8},{9,1... | collective-permute-start | bytes 2064392 | tf_op jit(solution)/shard_map/ppermute | solution.py:43
  56.5 5.2 %copy-start.9 = (bf16[896,384]{1,0:T(8,128)(2,1)}, bf16[896,384]{1,0:T(8,128)(2,1)S(1)}, u32[]{:S(2)}) copy-start(bf16[896,384]{1,0:T(8,128)(2,1)S(1)} %collective-permute-done.3) | copy-start | bytes 2064388
  57.8 29.7 %collective-permute-start.4 = (bf16[2,896,384]{2,1,0:T(8,128)(2,1)}, bf16[2,896,384]{2,1,0:T(8,128)(2,1)}, u32[]{:S(2)}, u32[]{:S(2)}) collective-permute-start(bf16[2,896,384]{2,1,0:T(8,128)(2,1)} %pad_maximum_fusion.2), channel_id=1, source_target_pairs={{0,1},{1,0},{2,3},{3,2},{4,5},{5,4},{6,7},{7,6},{8,9},{9,8},{10,11... | collective-permute-start | bytes 4128776 | tf_op jit(solution)/shard_map/ppermute | solution.py:43
  61.7 42.9 %all-to-all-start = ((bf16[16,112,128]{2,1,0:T(8,128)(2,1)}), bf16[16,112,128]{2,1,0:T(8,128)(2,1)}, u32[]{:S(2)}, u32[]{:S(2)}) async-start(bf16[16,112,128]{2,1,0:T(8,128)(2,1)} %broadcast_in_dim.154), calls=%async_computation | async-start | bytes 917504 | tf_op jit(solution)/shard_map/all_to_all | solution.py:39
  115.4 27.5 %all-to-all-start.1 = ((f32[8,40,1536]{2,1,0:T(8,128)}), f32[8,40,1536]{2,1,0:T(8,128)}, u32[]{:S(2)}, u32[]{:S(2)}) async-start(f32[8,40,1536]{2,1,0:T(8,128)} %pad_maximum_fusion.1), calls=%async_computation.1 | async-start | bytes 3932160 | tf_op jit(solution)/shard_map/all_to_all | solution.py:102
  144.6 1.4 copy-start.10
  167.8 0.9 copy-start.7
  169.4 22.0 %collective-permute-start.5 = (bf16[2,256,384]{2,1,0:T(8,128)(2,1)}, bf16[2,256,384]{2,1,0:T(8,128)(2,1)S(1)}, u32[]{:S(2)}, u32[]{:S(2)}) collective-permute-start(bf16[2,256,384]{2,1,0:T(8,128)(2,1)} %slice.169), channel_id=1, source_target_pairs={{0,2},{2,0},{1,3},{3,1},{4,6},{6,4},{5,7},{7,5},{8,10},{10,8},{9,1... | collective-permute-start | bytes 1179656 | tf_op jit(solution)/shard_map/ppermute | solution.py:43
  173.0 40.1 %all-to-all-start.3 = ((bf16[16,112,128]{2,1,0:T(8,128)(2,1)}), bf16[16,112,128]{2,1,0:T(8,128)(2,1)}, u32[]{:S(2)}, u32[]{:S(2)}) async-start(bf16[16,112,128]{2,1,0:T(8,128)(2,1)} %bitcast.147), calls=%async_computation.3 | async-start | bytes 917504 | tf_op jit(solution)/shard_map/all_to_all | solution.py:111
  190.3 108.0 %all-gather.6.cloned.1.call-start = ((), (), s32[]{:S(2)}) async-start(), calls=%async_computation.9 | async-start | bytes 2293760 | tf_op jit(solution)/shard_map/all_gather | solution.py:120
  191.4 10.5 %copy-start.3 = (bf16[1,256,384]{2,1,0:T(8,128)(2,1)}, bf16[1,256,384]{2,1,0:T(8,128)(2,1)S(1)}, u32[]{:S(2)}) copy-start(bf16[1,256,384]{2,1,0:T(8,128)(2,1)S(1)} %get-tuple-element.52) | copy-start | bytes 589828
  191.5 10.4 %copy-start.4 = (bf16[1,256,384]{2,1,0:T(8,128)(2,1)}, bf16[1,256,384]{2,1,0:T(8,128)(2,1)S(1)}, u32[]{:S(2)}) copy-start(bf16[1,256,384]{2,1,0:T(8,128)(2,1)S(1)} %get-tuple-element.60) | copy-start | bytes 589828
  192.3 9.5 %collective-permute-start.6 = (bf16[2,256,384]{2,1,0:T(8,128)(2,1)}, bf16[2,256,384]{2,1,0:T(8,128)(2,1)S(1)}, u32[]{:S(2)}, u32[]{:S(2)}) collective-permute-start(bf16[2,256,384]{2,1,0:T(8,128)(2,1)} %pad_maximum_fusion.6), channel_id=1, source_target_pairs={{0,1},{1,0},{2,3},{3,2},{4,5},{5,4},{6,7},{7,6},{8,9},{9,8},{10,11... | collective-permute-start | bytes 1179656 | tf_op jit(solution)/shard_map/ppermute | solution.py:43
  201.9 0.7 copy-start.5
  201.9 0.7 copy-start.6
  217.5 36.0 %all-to-all-start.4 = ((bf16[16,112,128]{2,1,0:T(8,128)(2,1)}), bf16[16,112,128]{2,1,0:T(8,128)(2,1)S(1)}, u32[]{:S(2)}, u32[]{:S(2)}) async-start(bf16[16,112,128]{2,1,0:T(8,128)(2,1)} %broadcast_in_dim.169), calls=%async_computation.4 | async-start | bytes 917504 | tf_op jit(solution)/shard_map/all_to_all | solution.py:39
  229.2 24.2 %collective-permute-start.7 = (bf16[112,128]{1,0:T(8,128)(2,1)S(1)}, bf16[112,128]{1,0:T(8,128)(2,1)S(1)}, u32[]{:S(2)}, u32[]{:S(2)}) collective-permute-start(bf16[112,128]{1,0:T(8,128)(2,1)S(1)} %get-tuple-element.36), channel_id=1, source_target_pairs={{0,0},{4,1},{8,2},{12,3},{16,4},{20,5},{24,6},{28,7},{64,8},{68,9}... | collective-permute-start | bytes 86024 | tf_op jit(solution)/shard_map/ppermute | solution.py:128
  253.4 1.0 copy-start.2
  256.2 20.2 %copy-start.11 = (f32[40,1536]{1,0:T(8,128)S(1)}, f32[40,1536]{1,0:T(8,128)}, u32[]{:S(2)}) copy-start(f32[40,1536]{1,0:T(8,128)} %copy-done.10) | copy-start | bytes 737284
  256.2 20.1 %all-to-all-start.5 = ((bf16[8,32,1536]{2,1,0:T(8,128)(2,1)}), bf16[8,32,1536]{2,1,0:T(8,128)(2,1)S(1)}, u32[]{:S(2)}, u32[]{:S(2)}) async-start(bf16[8,32,1536]{2,1,0:T(8,128)(2,1)} %reshape.333), calls=%async_computation.5 | async-start | bytes 1572864 | tf_op jit(solution)/shard_map/all_to_all | solution.py:137
  266.4 51.7 %all-gather.4.cloned.1.call-start = ((), (), s32[]{:S(2)}) async-start(), calls=%async_computation.8 | async-start | bytes 2293760 | tf_op jit(solution)/shard_map/all_gather | solution.py:135
  278.4 19.7 %copy-start.8 = (bf16[4,2,128,384]{3,2,1,0:T(8,128)(2,1)S(1)}, bf16[4,2,128,384]{3,2,1,0:T(8,128)(2,1)}, u32[]{:S(2)}) copy-start(bf16[4,2,128,384]{3,2,1,0:T(8,128)(2,1)} %fusion.22) | copy-start | bytes 2359300
  293.5 19.8 %all-to-all-start.7 = ((bf16[8,144,384]{2,1,0:T(8,128)(2,1)}), bf16[8,144,384]{2,1,0:T(8,128)(2,1)S(1)}, u32[]{:S(2)}, u32[]{:S(2)}) async-start(bf16[8,144,384]{2,1,0:T(8,128)(2,1)} %broadcast_in_dim.176), calls=%async_computation.7 | async-start | bytes 1769472 | tf_op jit(solution)/shard_map/all_to_all | solution.py:39
  314.6 0.7 copy-start.15
  321.4 1.1 copy-start.1
  321.5 1.1 copy-start.14
Sparse Core Ops, SparseCore 0:
  202.0 32.5 all-gather.5
  269.4 43.8 all-gather.3

commit v3 on v1

--- a/solution.py
+++ b/solution.py
@@ -37,6 +37,21 @@
 
 def share(block, axes, count):
     return lax.all_to_all(jnp.broadcast_to(block[None], (count, *block.shape)), axes, 0, 0)
+
+
+def neighbour(block, axis):
+    return lax.ppermute(block, axis, [(0, 1), (1, 0)])
+
+
+def relative(blocks):
+    yl, c = lax.axis_index("yl"), lax.axis_index("c")
+    swapped = jnp.concatenate([blocks[2:], blocks[:2]])
+    blocks = jnp.where(yl == 1, swapped, blocks)
+    swapped = jnp.stack([blocks[1], blocks[0], blocks[3], blocks[2]])
+    return jnp.where(c == 1, swapped, blocks)
+
+
+together = lax.optimization_barrier
 
 
 def dot(spec, a, b):
@@ -81,21 +96,31 @@
     pre = summed[:32] + bias_quad[None]
     norms = jnp.sqrt(summed[32] + norm_epsilon)
     acts = jnp.maximum(pre, 0.0).astype(bf16)
-    sparsity = jnp.sum(acts.astype(f32) * norms[None])
+    sparsity = jnp.sum(acts.astype(f32) * norms[None], axis=0).reshape(12, 128).sum(0)
     acts_quad = share(acts, DP, 8).reshape(2, 128, 4, 384)
 
     terms = dot("qkj,atqj->akt", dec_quad, acts_quad).astype(bf16).reshape(16, BLOCK, 128)
+    terms, acts_sent = together((terms, acts_quad))
     recon_sum = lax.all_to_all(terms, "z", 0, 0).astype(f32).sum(0)
+    acts_sent = relative(acts_sent.reshape(256, 4, 384).transpose(1, 0, 2))
+    near, far = acts_sent[:2], neighbour(acts_sent[2:], "yl")
+    mine = jnp.stack([near[0], far[0]])
+    other = neighbour(jnp.stack([near[1], far[1]]), "c")
+    acts_every = relative(jnp.stack([mine[0], other[0], mine[1], other[1]]))
+    acts_every = acts_every.reshape(1024, 384)
+    colsum = jnp.sum(acts_every.astype(f32), axis=0)
+    recon_sum, acts_every, colsum = together((recon_sum, acts_every, colsum))
+    acts_every = acts_every.reshape(4, 2, 128, 384)
     recon = lax.ppermute(recon_sum.astype(bf16), ALL, back)
     recon = recon[:108].reshape(3, 36, 128).transpose(2, 0, 1)
     error = recon_sum - target_block.astype(f32)
-    local_loss = jnp.sum(error * error) + sparsity_weight * sparsity
+    local_loss = jnp.sum(error * error, axis=0) + sparsity_weight * sparsity
     gout = (2.0 * error / TOK_DEV).astype(bf16)
-    loss_row = jnp.pad(jnp.stack(pieces(local_loss)), (0, 125))
     row_ids = lax.broadcasted_iota(jnp.int32, (BLOCK, 128), 0)
-    gout = jnp.where(row_ids == 108, loss_row[None], gout)
+    for row, piece in enumerate(pieces(local_loss)):
+        gout = jnp.where(row_ids == 108 + row, piece[None], gout)
     gout_all = share(gout, "z", 16)
-    loss_z = jnp.sum(gout_all[:, 108, :3].astype(f32))
+    loss_z = jnp.sum(gout_all[:, 108:111].astype(f32), axis=(0, 1))
     gout_quad = gout_all.reshape(2, 8 * BLOCK, 128)
 
     slopes = dot("akt,qkj->atqj", gout_quad, dec_quad).astype(bf16).reshape(8, 32, 1536)
@@ -103,33 +128,31 @@
     slopes = slopes + (sparsity_weight / TOK_DEV) * norms[None]
     dpre = jnp.where(pre > 0, slopes, 0.0)
     bias_rows = jnp.stack(pieces(dpre.sum(0))).reshape(3, 4, 384)
-    loss_rows = jnp.broadcast_to(jnp.pad(jnp.stack(pieces(loss_z)), (0, 381)), (1, 4, 384))
+    loss_rows = jnp.broadcast_to(jnp.concatenate(pieces(loss_z)), (1, 4, 384))
     sent = jnp.concatenate(
         [dpre.astype(bf16).reshape(32, 4, 384), bias_rows, loss_rows, jnp.zeros((12, 4, 384), bf16)]
     )
     got = lax.all_to_all(sent.transpose(1, 0, 2), QUAD, 0, 0)
     bias_rows = jnp.stack(pieces(got[:, 32:35].astype(f32).sum((0, 1))))
-    loss_row = jnp.pad(jnp.stack(pieces(got[:, 35, :3].astype(f32).sum())), (0, 381))[None]
+    loss_q = got[:, 35].astype(f32).sum(0).reshape(3, 128).sum(0)
+    loss_row = jnp.concatenate(pieces(loss_q))[None]
     sent = jnp.concatenate(
         [got[:, :32].reshape(128, 384), bias_rows, loss_row, jnp.zeros((12, 384), bf16)]
     )
     got = share(sent, DP, 8)
     bias_grad = got[:, 128:131].astype(f32).sum((0, 1))
-    loss = got[:, 131, :3].astype(f32).sum() / TOK_DEV
+    loss = got[:, 131].astype(f32).sum() / TOK_DEV
     dpre_every = got[:, :128].reshape(2, 4, 4, 32, 384).transpose(2, 0, 1, 3, 4)
     dpre_every = dpre_every.reshape(4, 2, 128, 384)
 
     x_every = lax.all_gather(x_quad, QUAD)
     gout_every = lax.all_gather(gout_quad, QUAD)
-    acts_every = acts_quad.reshape(256, 4, 384).transpose(1, 0, 2)
-    acts_every = lax.all_to_all(acts_every, QUAD, 0, 0).reshape(4, 2, 128, 384)
     enc_full = dot("qakt,qatj->kj", x_every, dpre_every)
     enc_full = enc_full.reshape(8, BLOCK, 384)[:, :108].reshape(8, 3, 36, 384)
     enc_grad = jnp.sum(jnp.where(pick[None, :, None, :], enc_full, 0.0), axis=1).reshape(288, 384)
     dec_full = dot("qakt,qatj->kj", gout_every, acts_every)
     dec_full = dec_full.reshape(8, BLOCK, 384)[:, :108].reshape(8, 3, 36, 384)
     dec_full = dec_full.transpose(1, 0, 2, 3).reshape(3, 288, 384)
-    colsum = jnp.sum(acts_every.astype(f32), axis=(0, 1, 2))
     member = lax.axis_index(QUAD)
     own_norms = lax.dynamic_index_in_dim(norms.reshape(4, 384), member, 0, False)
     pull = (sparsity_weight / TOK_DEV) * colsum / own_norms

time: 295 us -> 271 us (0.919)
  the two profiles are of different devices: /device:TPU:20 before, /device:TPU:1 now
where the time goes in v3:
time: 271 us; the launch traced here: 268 us
  starting transfers between devices  77.4 us (29%)
  waiting for transfers between devices  67 us (25%)
  blocking collectives  62.7 us (23%)
  local copies, waits for them, and re-layouts  19.7 us (7%)
  between operations  16.3 us (6%)
  other arithmetic  13.8 us (5%)
  matrix products  11 us (4%)
    all_to_all x3, starting transfers between devices, share(): lax.all_to_all(jnp.broadcast_to(block[None], (count, *block.shape)), axes...  33.6 us
    all_to_all x1, blocking collectives, share(): lax.all_to_all(jnp.broadcast_to(block[None], (count, *block.shape)), axes...  32.2 us
    all_to_all x1, waiting for transfers between devices, on_device(): lax.all_to_all(jnp.concatenate([partial, squares], axis=1), DP, 0, 0).sum(0)  24.6 us
    all_gather x1, blocking collectives, on_device(): enc_quad = lax.all_gather(enc_own, QUAD)  16 us
    all_to_all x1, blocking collectives, on_device(): got = lax.all_to_all(sent.transpose(1, 0, 2), QUAD, 0, 0)  14.5 us
    all_to_all x3, waiting for transfers between devices, share(): lax.all_to_all(jnp.broadcast_to(block[None], (count, *block.shape)), axes...  14.1 us
    all_to_all x1, starting transfers between devices, on_device(): recon_sum = lax.all_to_all(terms, 'z', 0, 0).astype(f32).sum(0)  12.7 us
    ppermute x2, starting transfers between devices, neighbour(): return lax.ppermute(block, axis, [(0, 1), (1, 0)])  12.6 us
  transfers between devices with their start and end apart: 13, of which 7 were waited for; matrix products, arithmetic and copies ran while one was open for 13% of the time, Pallas kernels for 0%

profile of v3, /device:TPU:1, one launch (start us, length us, event | category | flops | bytes accessed | tf_op | source)
XLA Modules:
  0.0 268.0 jit_solution(10775462435141203462)
XLA Ops:
  7.2 0.8 maximum_bitcast_fusion
  8.1 4.9 %collective-permute-start = (bf16[2,112,128]{2,0,1:T(2,128)(2,1)S(1)}, bf16[2,112,128]{2,0,1:T(2,128)(2,1)S(1)}, u32[]{:S(2)}, u32[]{:S(2)}) collective-permute-start(bf16[2,112,128]{2,0,1:T(2,128)(2,1)S(1)} %pad.16), channel_id=1, source_target_pairs={{0,0},{1,4},{2,8},{3,12},{4,16},{5,20},{6,24},{7,28},{8,64},{9,68}... | collective-permute-start | bytes 172040 | tf_op jit(solution)/shard_map/ppermute | solution.py:70
  13.0 0.7 iota_compare_fusion.1
  13.7 1.3 fusion.10
  15.1 0.1 reshape.326
  15.4 0.9 pad.19.clone
  16.6 0.8 broadcast_in_dim.140
  17.4 25.3 %all-to-all-start = ((bf16[16,112,128]{2,1,0:T(8,128)(2,1)}), bf16[16,112,128]{2,1,0:T(8,128)(2,1)}, u32[]{:S(2)}, u32[]{:S(2)}) async-start(bf16[16,112,128]{2,1,0:T(8,128)(2,1)} %broadcast_in_dim.140), calls=%async_computation | async-start | bytes 917504 | tf_op jit(solution)/shard_map/all_to_all | solution.py:39
  42.8 16.0 %all-gather = bf16[1216,384]{1,0:T(8,128)(2,1)S(1)} all-gather(bf16[304,384]{1,0:T(8,128)(2,1)S(1)} %fusion.23), channel_id=2, replica_groups=mesh['x'=4,'yh'=2,'z'=16,'yl'=2,'c'=2] {'yl','c'}, dimensions={0}, use_global_device_ids=true | all-gather | bytes 1167360 | tf_op jit(solution)/shard_map/all_gather | solution.py:80
  59.3 0.5 copy.139
  59.8 0.2 copy.108
  60.0 0.2 broadcast_in_dim.147
  60.2 0.8 broadcast_select_fusion
  61.1 0.4 copy.140
  61.5 1.8 pad.18.clone
  63.3 3.3 %copy.110 = bf16[4,384,896]{2,1,0:T(8,128)(2,1)S(1)} copy(bf16[4,384,896]{1,2,0:T(8,128)(2,1)} %bitcast.121) | data formatting | bytes 5505024 | tf_op jit(solution)/shard_map/akt,qkj->atqj/dot_general | solution.py:58
  66.6 2.0 copy.105
  68.6 2.0 fusion.49
  70.7 1.4 pad_maximum_fusion
  72.1 3.8 %all-to-all-start.1 = ((f32[8,40,1536]{2,1,0:T(8,128)}), f32[8,40,1536]{2,1,0:T(8,128)S(1)}, u32[]{:S(2)}, u32[]{:S(2)}) async-start(f32[8,40,1536]{2,1,0:T(8,128)} %pad_maximum_fusion), calls=%async_computation.1 | async-start | bytes 3932160 | tf_op jit(solution)/shard_map/all_to_all | solution.py:95
  75.9 24.6 %all-to-all-done.1 = f32[8,40,1536]{2,1,0:T(8,128)S(1)} async-done(((f32[8,40,1536]{2,1,0:T(8,128)}), f32[8,40,1536]{2,1,0:T(8,128)S(1)}, u32[]{:S(2)}, u32[]{:S(2)}) %all-to-all-start.1) | async-done | bytes 1966112 | tf_op jit(solution)/shard_map/all_to_all | solution.py:95
  100.8 0.9 broadcast_in_dim.151
  101.8 4.7 %all-to-all-start.2 = ((bf16[8,32,1536]{2,1,0:T(8,128)(2,1)}), bf16[8,32,1536]{2,1,0:T(8,128)(2,1)S(1)}, u32[]{:S(2)}, u32[]{:S(2)}) async-start(bf16[8,32,1536]{2,1,0:T(8,128)(2,1)} %broadcast_in_dim.151), calls=%async_computation.2 | async-start | bytes 1572864 | tf_op jit(solution)/shard_map/all_to_all | solution.py:39
  106.5 10.0 %all-to-all-done.2 = bf16[8,32,1536]{2,1,0:T(8,128)(2,1)S(1)} async-done(((bf16[8,32,1536]{2,1,0:T(8,128)(2,1)}), bf16[8,32,1536]{2,1,0:T(8,128)(2,1)S(1)}, u32[]{:S(2)}, u32[]{:S(2)}) %all-to-all-start.2) | async-done | bytes 786464 | tf_op jit(solution)/shard_map/all_to_all | solution.py:39
  116.4 0.2 reshape.325
  116.6 2.8 %fusion.17 = bf16[2,896,128]{1,2,0:T(8,128)(2,1)S(1)} fusion(bf16[4,896,384]{2,1,0:T(8,128)(2,1)} %all-gather.5.cloned.1.call-done, bf16[2,128,4,384]{3,2,1,0:T(4,128)(2,1)S(1)} %reshape.325), kind=kOutput, calls=%fused_computation.20 | convolution fusion | flops 704872448 | bytes 3997696 | tf_op jit(solution)/shard_map/qkj,atqj->akt/dot_general | solution.py:58
  119.4 1.0 copy.114
  120.6 0.2 maximum_select_fusion
  121.0 0.2 maximum_select_fusion.1
  121.2 8.6 %collective-permute-start.1 = (bf16[2,256,384]{2,1,0:T(8,128)(2,1)S(1)}, bf16[2,256,384]{2,1,0:T(8,128)(2,1)S(1)}, u32[]{:S(2)}, u32[]{:S(2)}) collective-permute-start(bf16[2,256,384]{2,1,0:T(8,128)(2,1)S(1)} %slice.184), channel_id=1, source_target_pairs={{0,2},{2,0},{1,3},{3,1},{4,6},{6,4},{5,7},{7,5},{8,10},{10,8},{9,1... | collective-permute-start | bytes 1179656 | tf_op jit(solution)/shard_map/ppermute | solution.py:43
  129.8 12.7 %all-to-all-start.3 = ((bf16[16,112,128]{2,1,0:T(8,128)(2,1)}), bf16[16,112,128]{2,1,0:T(8,128)(2,1)}, u32[]{:S(2)}, u32[]{:S(2)}) async-start(bf16[16,112,128]{2,1,0:T(8,128)(2,1)} %bitcast.24), calls=%async_computation.3 | async-start | bytes 917504 | tf_op jit(solution)/shard_map/all_to_all | solution.py:104
  142.7 3.9 %collective-permute-start.2 = (bf16[2,256,384]{2,1,0:T(8,128)(2,1)S(1)}, bf16[2,256,384]{2,1,0:T(8,128)(2,1)S(1)}, u32[]{:S(2)}, u32[]{:S(2)}) collective-permute-start(bf16[2,256,384]{2,1,0:T(8,128)(2,1)S(1)} %pad_maximum_fusion.1), channel_id=1, source_target_pairs={{0,1},{1,0},{2,3},{3,2},{4,5},{5,4},{6,7},{7,6},{8,9},{9,8},{10,11... | collective-permute-start | bytes 1179656 | tf_op jit(solution)/shard_map/ppermute | solution.py:43
  146.7 1.3 collective-permute-done.2
  148.0 0.2 maximum_select_fusion.2
  148.4 2.6 convert_reduce_fusion.1
  150.9 11.1 %all-to-all-done.3 = bf16[16,112,128]{2,1,0:T(8,128)(2,1)} async-done(((bf16[16,112,128]{2,1,0:T(8,128)(2,1)}), bf16[16,112,128]{2,1,0:T(8,128)(2,1)}, u32[]{:S(2)}, u32[]{:S(2)}) %all-to-all-start.3) | async-done | bytes 458784 | tf_op jit(solution)/shard_map/all_to_all | solution.py:104
  162.1 1.1 convert_reduce_fusion.2
  163.3 0.1 fusion.28
  163.5 32.2 %all_to_all.40 = bf16[16,112,128]{2,1,0:T(8,128)(2,1)S(1)} all-to-all(bf16[16,112,128]{2,1,0:T(8,128)(2,1)S(1)} %broadcast_in_dim.155), channel_id=1, replica_groups=mesh['x'=4,'yh'=2,'z'=16,'yl'=2,'c'=2] {'z'}, dimensions={0} | all-to-all | bytes 917504 | tf_op jit(solution)/shard_map/all_to_all | solution.py:39
  195.6 1.0 fusion.4
  196.6 0.6 copy.117
  197.3 1.2 reshape.332
  198.4 5.7 %all-to-all-start.5 = ((bf16[8,32,1536]{2,1,0:T(8,128)(2,1)}), bf16[8,32,1536]{2,1,0:T(8,128)(2,1)S(1)}, u32[]{:S(2)}, u32[]{:S(2)}) async-start(bf16[8,32,1536]{2,1,0:T(8,128)(2,1)} %reshape.332), calls=%async_computation.5 | async-start | bytes 1572864 | tf_op jit(solution)/shard_map/all_to_all | solution.py:127
  204.2 0.7 all-gather.9.cloned.1.call-update
  204.9 0.8 convert_reduce_fusion.4
  205.7 8.2 %all-to-all-done.5 = bf16[8,32,1536]{2,1,0:T(8,128)(2,1)S(1)} async-done(((bf16[8,32,1536]{2,1,0:T(8,128)(2,1)}), bf16[8,32,1536]{2,1,0:T(8,128)(2,1)S(1)}, u32[]{:S(2)}, u32[]{:S(2)}) %all-to-all-start.5) | async-done | bytes 786464 | tf_op jit(solution)/shard_map/all_to_all | solution.py:127
  214.3 14.5 %all_to_all.41 = bf16[4,48,384]{2,1,0:T(8,128)(2,1)S(1)} all-to-all(bf16[4,48,384]{2,1,0:T(8,128)(2,1)S(1)} %copy.118), channel_id=1, replica_groups=mesh['x'=4,'yh'=2,'z'=16,'yl'=2,'c'=2] {'yl','c'}, dimensions={0} | all-to-all | bytes 294912 | tf_op jit(solution)/shard_map/all_to_all | solution.py:135
  228.9 0.2 concatenate.36
  229.2 1.0 broadcast_in_dim.160
  230.1 3.6 %all-to-all-start.7 = ((bf16[8,144,384]{2,1,0:T(8,128)(2,1)}), bf16[8,144,384]{2,1,0:T(8,128)(2,1)S(1)}, u32[]{:S(2)}, u32[]{:S(2)}) async-start(bf16[8,144,384]{2,1,0:T(8,128)(2,1)} %broadcast_in_dim.160), calls=%async_computation.7 | async-start | bytes 1769472 | tf_op jit(solution)/shard_map/all_to_all | solution.py:39
  233.7 4.1 %collective-permute-start.3 = (bf16[112,128]{1,0:T(8,128)(2,1)S(1)}, bf16[112,128]{1,0:T(8,128)(2,1)S(1)}, u32[]{:S(2)}, u32[]{:S(2)}) collective-permute-start(bf16[112,128]{1,0:T(8,128)(2,1)S(1)} %get-tuple-element.43), channel_id=1, source_target_pairs={{0,0},{4,1},{8,2},{12,3},{16,4},{20,5},{24,6},{28,7},{64,8},{68,9}... | collective-permute-start | bytes 86024 | tf_op jit(solution)/shard_map/ppermute | solution.py:114
  237.8 6.9 %collective-permute-done.3 = bf16[112,128]{1,0:T(8,128)(2,1)S(1)} collective-permute-done((bf16[112,128]{1,0:T(8,128)(2,1)S(1)}, bf16[112,128]{1,0:T(8,128)(2,1)S(1)}, u32[]{:S(2)}, u32[]{:S(2)}) %collective-permute-start.3) | collective-permute-done | bytes 28704 | tf_op jit(solution)/shard_map/ppermute | solution.py:114
  244.7 0.6 reshape.336
  245.3 4.1 %all-to-all-done.7 = bf16[8,144,384]{2,1,0:T(8,128)(2,1)S(1)} async-done(((bf16[8,144,384]{2,1,0:T(8,128)(2,1)}), bf16[8,144,384]{2,1,0:T(8,128)(2,1)S(1)}, u32[]{:S(2)}, u32[]{:S(2)}) %all-to-all-start.7) | async-done | bytes 884768 | tf_op jit(solution)/shard_map/all_to_all | solution.py:39
  249.7 2.6 convolution_bitcast_fusion.1
  252.3 0.4 copy.121
  253.0 0.8 reshape.340
  253.8 0.6 fusion.29
  255.0 0.6 convert_reduce_fusion.3
  255.6 2.6 convolution_bitcast_fusion
  258.3 0.4 copy.125
  258.7 0.2 copy.126
  258.9 0.1 reshape.343
  259.1 1.2 fusion.13
  (104 shorter events, 3.0 us)
Async XLA Ops:
  7.2 109.5 %all-gather.5.cloned.1.call-start = ((), (), s32[]{:S(2)}) async-start(), calls=%async_computation.8 | async-start | bytes 3440640 | tf_op jit(solution)/shard_map/all_gather | solution.py:81
  8.1 8.4 %collective-permute-start = (bf16[2,112,128]{2,0,1:T(2,128)(2,1)S(1)}, bf16[2,112,128]{2,0,1:T(2,128)(2,1)S(1)}, u32[]{:S(2)}, u32[]{:S(2)}) collective-permute-start(bf16[2,112,128]{2,0,1:T(2,128)(2,1)S(1)} %pad.16), channel_id=1, source_target_pairs={{0,0},{1,4},{2,8},{3,12},{4,16},{5,20},{6,24},{7,28},{8,64},{9,68}... | collective-permute-start | bytes 172040 | tf_op jit(solution)/shard_map/ppermute | solution.py:70
  15.3 1.1 copy-start.9
  15.3 1.1 copy-start.8
  15.4 27.4 %copy-start.7 = (bf16[384,288]{0,1:T(8,128)(2,1)S(1)}, bf16[384,288]{0,1:T(8,128)(2,1)}, u32[]{:S(2)}) copy-start(bf16[384,288]{0,1:T(8,128)(2,1)} %param.8) | copy-start | bytes 663556
  17.4 49.2 %all-to-all-start = ((bf16[16,112,128]{2,1,0:T(8,128)(2,1)}), bf16[16,112,128]{2,1,0:T(8,128)(2,1)}, u32[]{:S(2)}, u32[]{:S(2)}) async-start(bf16[16,112,128]{2,1,0:T(8,128)(2,1)} %broadcast_in_dim.140), calls=%async_computation | async-start | bytes 917504 | tf_op jit(solution)/shard_map/all_to_all | solution.py:39
  72.1 28.5 %all-to-all-start.1 = ((f32[8,40,1536]{2,1,0:T(8,128)}), f32[8,40,1536]{2,1,0:T(8,128)S(1)}, u32[]{:S(2)}, u32[]{:S(2)}) async-start(f32[8,40,1536]{2,1,0:T(8,128)} %pad_maximum_fusion), calls=%async_computation.1 | async-start | bytes 3932160 | tf_op jit(solution)/shard_map/all_to_all | solution.py:95
  100.7 15.9 %copy-start.4 = (f32[40,1536]{1,0:T(8,128)}, f32[40,1536]{1,0:T(8,128)S(1)}, u32[]{:S(2)}) copy-start(f32[40,1536]{1,0:T(8,128)S(1)} %reduce_sum.152) | copy-start | bytes 737284
  101.8 14.7 %all-to-all-start.2 = ((bf16[8,32,1536]{2,1,0:T(8,128)(2,1)}), bf16[8,32,1536]{2,1,0:T(8,128)(2,1)S(1)}, u32[]{:S(2)}, u32[]{:S(2)}) async-start(bf16[8,32,1536]{2,1,0:T(8,128)(2,1)} %broadcast_in_dim.151), calls=%async_computation.2 | async-start | bytes 1572864 | tf_op jit(solution)/shard_map/all_to_all | solution.py:39
  121.2 21.4 %collective-permute-start.1 = (bf16[2,256,384]{2,1,0:T(8,128)(2,1)S(1)}, bf16[2,256,384]{2,1,0:T(8,128)(2,1)S(1)}, u32[]{:S(2)}, u32[]{:S(2)}) collective-permute-start(bf16[2,256,384]{2,1,0:T(8,128)(2,1)S(1)} %slice.184), channel_id=1, source_target_pairs={{0,2},{2,0},{1,3},{3,1},{4,6},{6,4},{5,7},{7,5},{8,10},{10,8},{9,1... | collective-permute-start | bytes 1179656 | tf_op jit(solution)/shard_map/ppermute | solution.py:43
  129.8 32.3 %all-to-all-start.3 = ((bf16[16,112,128]{2,1,0:T(8,128)(2,1)}), bf16[16,112,128]{2,1,0:T(8,128)(2,1)}, u32[]{:S(2)}, u32[]{:S(2)}) async-start(bf16[16,112,128]{2,1,0:T(8,128)(2,1)} %bitcast.24), calls=%async_computation.3 | async-start | bytes 917504 | tf_op jit(solution)/shard_map/all_to_all | solution.py:104
  142.5 107.2 %all-gather.7.cloned.1.call-start = ((), (), s32[]{:S(2)}) async-start(), calls=%async_computation.9 | async-start | bytes 2293760 | tf_op jit(solution)/shard_map/all_gather | solution.py:148
  142.6 5.7 %copy-start.2 = (bf16[1,256,384]{2,1,0:T(8,128)(2,1)}, bf16[1,256,384]{2,1,0:T(8,128)(2,1)S(1)}, u32[]{:S(2)}) copy-start(bf16[1,256,384]{2,1,0:T(8,128)(2,1)S(1)} %get-tuple-element.29) | copy-start | bytes 589828
  142.6 5.7 %copy-start.3 = (bf16[1,256,384]{2,1,0:T(8,128)(2,1)}, bf16[1,256,384]{2,1,0:T(8,128)(2,1)S(1)}, u32[]{:S(2)}) copy-start(bf16[1,256,384]{2,1,0:T(8,128)(2,1)S(1)} %get-tuple-element.39) | copy-start | bytes 589828
  142.7 5.3 %collective-permute-start.2 = (bf16[2,256,384]{2,1,0:T(8,128)(2,1)S(1)}, bf16[2,256,384]{2,1,0:T(8,128)(2,1)S(1)}, u32[]{:S(2)}, u32[]{:S(2)}) collective-permute-start(bf16[2,256,384]{2,1,0:T(8,128)(2,1)S(1)} %pad_maximum_fusion.1), channel_id=1, source_target_pairs={{0,1},{1,0},{2,3},{3,2},{4,5},{5,4},{6,7},{7,6},{8,9},{9,8},{10,11... | collective-permute-start | bytes 1179656 | tf_op jit(solution)/shard_map/ppermute | solution.py:43
  148.4 47.2 %copy-start.1 = (bf16[4,896,384]{2,1,0:T(8,128)(2,1)S(1)}, bf16[4,896,384]{2,1,0:T(8,128)(2,1)}, u32[]{:S(2)}) copy-start(bf16[4,896,384]{2,1,0:T(8,128)(2,1)} %all-gather.5.cloned.1.call-done) | copy-start | bytes 8257540
  195.6 1.0 copy-start
  198.4 15.6 %copy-start.5 = (f32[40,1536]{1,0:T(8,128)S(1)}, f32[40,1536]{1,0:T(8,128)}, u32[]{:S(2)}) copy-start(f32[40,1536]{1,0:T(8,128)} %copy-done.4) | copy-start | bytes 737284
  198.4 15.5 %all-to-all-start.5 = ((bf16[8,32,1536]{2,1,0:T(8,128)(2,1)}), bf16[8,32,1536]{2,1,0:T(8,128)(2,1)S(1)}, u32[]{:S(2)}, u32[]{:S(2)}) async-start(bf16[8,32,1536]{2,1,0:T(8,128)(2,1)} %reshape.332), calls=%async_computation.5 | async-start | bytes 1572864 | tf_op jit(solution)/shard_map/all_to_all | solution.py:127
  204.1 51.5 %all-gather.9.cloned.1.call-start = ((), (), s32[]{:S(2)}) async-start(), calls=%async_computation.10 | async-start | bytes 2293760 | tf_op jit(solution)/shard_map/all_gather | solution.py:149
  230.1 19.3 %all-to-all-start.7 = ((bf16[8,144,384]{2,1,0:T(8,128)(2,1)}), bf16[8,144,384]{2,1,0:T(8,128)(2,1)S(1)}, u32[]{:S(2)}, u32[]{:S(2)}) async-start(bf16[8,144,384]{2,1,0:T(8,128)(2,1)} %broadcast_in_dim.160), calls=%async_computation.7 | async-start | bytes 1769472 | tf_op jit(solution)/shard_map/all_to_all | solution.py:39
  233.7 10.9 %collective-permute-start.3 = (bf16[112,128]{1,0:T(8,128)(2,1)S(1)}, bf16[112,128]{1,0:T(8,128)(2,1)S(1)}, u32[]{:S(2)}, u32[]{:S(2)}) collective-permute-start(bf16[112,128]{1,0:T(8,128)(2,1)S(1)} %get-tuple-element.43), channel_id=1, source_target_pairs={{0,0},{4,1},{8,2},{12,3},{16,4},{20,5},{24,6},{28,7},{64,8},{68,9}... | collective-permute-start | bytes 86024 | tf_op jit(solution)/shard_map/ppermute | solution.py:114
  252.7 2.9 %copy-start.6 = (bf16[4,256,384]{2,1,0:T(8,128)(2,1)S(1)}, bf16[4,256,384]{2,1,0:T(8,128)(2,1)}, u32[]{:S(2)}) copy-start(bf16[4,256,384]{2,1,0:T(8,128)(2,1)} %get-tuple-element.22) | copy-start | bytes 2359300
Sparse Core Ops, SparseCore 0:
  16.5 53.5 all-gather.4
  146.8 33.7 all-gather.6
  207.0 46.4 all-gather.8

commit v4 on v3

v4 whole, which is shorter than its diff:
```python
import jax
import jax.numpy as jnp
import numpy as np
from jax import lax
from jax.experimental import pallas as pl
from jax.experimental.pallas import tpu as pltpu
from jax.sharding import Mesh
from jax.sharding import PartitionSpec as P

LAYERS = 3
TOK_DEV = 128
SIZES = (4, 2, 16, 2, 2)
ALL = ("x", "yh", "z", "yl", "c")
DP = ("x", "yh")
LATENT = ("z", "yl", "c")
QUAD = ("yl", "c")
BLOCK = 112

sparsity_weight = 0.5
norm_epsilon = 1e-06
bf16, f32 = jnp.bfloat16, jnp.float32


def spread():
    pairs = []
    for a in range(8):
        for b in range(64):
            i, r = divmod(b, 8)
            pairs.append((a * 64 + b, i * 64 + ((a % 2) * 8 + r) * 4 + a // 2))
    return pairs


def pieces(value):
    high = lax.reduce_precision(value, 8, 7)
    middle = lax.reduce_precision(value - high, 8, 7)
    low = value - high - middle
    return [high.astype(bf16), middle.astype(bf16), low.astype(bf16)]


def share(block, axes, count):
    return lax.all_to_all(jnp.broadcast_to(block[None], (count, *block.shape)), axes, 0, 0)


def call(kernel, *args, out):
    return pl.pallas_call(
        kernel,
        out_shape=[jax.ShapeDtypeStruct(shape, dtype) for shape, dtype in out],
        compiler_params=pltpu.CompilerParams(vmem_limit_bytes=40 * 1024 * 1024),
    )(*args)


def split(value):
    high = value.astype(bf16)
    rest = value - high.astype(f32)
    middle = rest.astype(bf16)
    return [high, middle, (rest - middle.astype(f32)).astype(bf16)]


def matmul(a, b, left, right):
    return lax.dot_general(a, b, (((left,), (right,)), ((), ())), preferred_element_type=f32)


def encode(x, rows, squares, out):
    for half in range(2):
        for q in range(4):
            product = matmul(x[half], rows[q], 0, 0)
            for g in range(4):
                for c in range(3):
                    at = (q * 3 + c) * 32
                    out[half * 4 + g, at : at + 32] = product[
                        g * 32 : g * 32 + 32, c * 128 : c * 128 + 128
                    ]
    for g in range(8):
        out[g, 384:] = squares[...]


def activate(parts, bias, pre, norms, acts, sparsity):
    total = jnp.sum(parts[...], axis=0)
    norm = jnp.sqrt(total[384:396] + norm_epsilon)
    norms[0:12] = norm
    norms[12:16] = jnp.zeros((4, 128), f32)
    weighted = jnp.zeros((32, 128), f32)
    for c in range(12):
        here = total[c * 32 : c * 32 + 32] + bias[c : c + 1]
        pre[c * 32 : c * 32 + 32] = here
        low = jnp.maximum(here, 0.0).astype(bf16)
        weighted = weighted + low.astype(f32) * norm[c : c + 1]
        for g in range(8):
            acts[g, c * 32 : c * 32 + 32] = low
    sparsity[...] = jnp.broadcast_to(jnp.sum(weighted, axis=0, keepdims=True), (8, 128))


def tokens_of(ref, half, column):
    return ref[half * 4 : half * 4 + 4, column * 32 : column * 32 + 32].reshape(128, 128)


def decode(rows, acts, out):
    for half in range(2):
        total = None
        for q in range(4):
            wide = jnp.concatenate([tokens_of(acts, half, q * 3 + c) for c in range(3)], axis=1)
            product = matmul(rows[q], wide, 1, 1)
            total = product if total is None else total + product
        low = total.astype(bf16)
        for r in range(8):
            out[half * 8 + r] = low[r * BLOCK : (r + 1) * BLOCK]


def compare(parts, target, sparsity, recon, gout):
    recon_sum = jnp.sum(parts[...].astype(f32), axis=0)
    recon[...] = recon_sum.astype(bf16)
    error = recon_sum - target[...].astype(f32)
    by_lane = jnp.sum(error * error, axis=0, keepdims=True) + sparsity_weight * sparsity[0:1]
    slope = 2.0 * error / TOK_DEV
    row = lax.broadcasted_iota(jnp.int32, (BLOCK, 128), 0)
    for k, piece in enumerate(split(by_lane)):
        slope = jnp.where(row == 108 + k, piece.astype(f32), slope)
    low = slope.astype(bf16)
    for z in range(16):
        gout[z] = low


def pull_back(gout, rows, out, loss):
    total = jnp.sum(gout[:, 96:112].astype(f32), axis=0)
    loss[...] = jnp.broadcast_to(jnp.sum(total[12:15], axis=0, keepdims=True), (8, 128))
    for half in range(2):
        tokens = jnp.concatenate([gout[half * 8 + r] for r in range(8)], axis=0)
        for q in range(4):
            product = matmul(tokens, rows[q], 0, 0).astype(bf16)
            for g in range(4):
                for c in range(3):
                    at = (q * 3 + c) * 32
                    out[half * 4 + g, at : at + 32] = product[
                        g * 32 : g * 32 + 32, c * 128 : c * 128 + 128
                    ]


def tail_of(values):
    row = lax.broadcasted_iota(jnp.int32, (16, 128), 0)
    tail = jnp.zeros((16, 128), f32)
    for k, value in enumerate(values):
        for p, piece in enumerate(split(value)):
            tail = jnp.where(row == 4 * p + k, piece.astype(f32), tail)
    return tail.astype(bf16)


def slopes_of(parts, pre, norms, loss, out):
    total = jnp.sum(parts[...].astype(f32), axis=0)
    for q in range(4):
        sums = []
        for c in range(3):
            k = q * 3 + c
            slope = total[k * 32 : k * 32 + 32] + (sparsity_weight / TOK_DEV) * norms[k : k + 1]
            slope = jnp.where(pre[k * 32 : k * 32 + 32] > 0, slope, 0.0)
            sums.append(jnp.sum(slope, axis=0, keepdims=True))
            out[q, c * 32 : c * 32 + 32] = slope.astype(bf16)
        out[q, 96:112] = tail_of([*sums, loss[0:1]])


def regroup(got, out):
    tail = jnp.sum(got[:, 96:112].astype(f32), axis=0)
    tail = tail[0:4] + tail[4:8] + tail[8:12]
    tail = tail_of([tail[k : k + 1] for k in range(4)])
    for g in range(8):
        for q in range(4):
            out[g, q * 96 : q * 96 + 96] = got[q, 0:96]
        out[g, 384:400] = tail


def over_tokens(blocks, values, out):
    total = None
    for q in range(4):
        wide = jnp.concatenate([blocks[q, 0], blocks[q, 1]], axis=1)
        column = lambda c: jnp.concatenate([tokens_of(values, h, q * 3 + c) for h in range(2)], axis=0)
        product = matmul(wide, jnp.concatenate([column(c) for c in range(3)], axis=1), 1, 0)
        total = product if total is None else total + product
    out[...] = total


def neighbour(block, axis):
    return lax.ppermute(block, axis, [(0, 1), (1, 0)])


def relative(blocks):
    yl, c = lax.axis_index("yl"), lax.axis_index("c")
    swapped = jnp.concatenate([blocks[2:], blocks[:2]])
    blocks = jnp.where(yl == 1, swapped, blocks)
    swapped = jnp.stack([blocks[1], blocks[0], blocks[3], blocks[2]])
    return jnp.where(c == 1, swapped, blocks)


together = lax.optimization_barrier


def on_device(resid, target, enc_weight, enc_bias, dec_weight, source):
    to = spread()
    back = [(d, s) for s, d in to]
    layer_ids = jnp.arange(LAYERS, dtype=jnp.int32)
    pick = source[None, :] == layer_ids[:, None]
    reach = source[None, :] <= layer_ids[:, None]

    both = jnp.stack([resid, target]).transpose(0, 2, 3, 1).reshape(2, 108, 128)
    both = jnp.pad(both, ((0, 0), (0, BLOCK - 108), (0, 0)))
    both = lax.ppermute(both, ALL, to)
    x_block, target_block = both[0], both[1]

    enc_t = enc_weight.T
    dec_t = jnp.where(reach[:, None, :], dec_weight.transpose(1, 2, 0), 0)
    square = jnp.sum(jnp.square(dec_t.astype(f32)), axis=(0, 1))
    dec_own = dec_t.reshape(3, 8, 36, 384).transpose(1, 0, 2, 3).reshape(8, 108, 384)
    dec_own = jnp.pad(dec_own, ((0, 0), (0, BLOCK - 108), (0, 0))).reshape(8 * BLOCK, 384)
    extra = jnp.stack([source.astype(bf16), *pieces(enc_bias), *pieces(square)])
    enc_own = jnp.concatenate([enc_t, jnp.pad(extra, ((0, 9), (0, 0)))])
    enc_quad = lax.all_gather(enc_own, QUAD)
    dec_quad = lax.all_gather(dec_own, QUAD)
    tail = enc_quad[:, 288:295].astype(f32)
    source_quad = tail[:, 0]
    bias_quad = (tail[:, 1] + tail[:, 2] + tail[:, 3]).reshape(1536)
    square_quad = (tail[:, 4] + tail[:, 5] + tail[:, 6]).reshape(1536)
    enc_rows = enc_quad[:, :288].reshape(4, 8, 1, 36, 384)
    pick_quad = source_quad[:, None, :] == layer_ids[None, :, None].astype(f32)
    enc_rows = jnp.where(pick_quad[:, None, :, None, :], enc_rows, 0).reshape(4, 8, 108, 384)
    enc_rows = jnp.pad(enc_rows, ((0, 0), (0, 0), (0, BLOCK - 108), (0, 0)))
    enc_rows = enc_rows.reshape(4, 8 * BLOCK, 384)

    x_quad = share(x_block, "z", 16).reshape(2, 8 * BLOCK, 128)
    squares = jnp.pad(square_quad.reshape(12, 128), ((0, 4), (0, 0)))
    (partial,) = call(encode, x_quad, enc_rows, squares, out=[((8, 400, 128), f32)])
    partial = lax.all_to_all(partial, DP, 0, 0)
    pre, norms, acts, sparsity = call(
        activate,
        partial,
        bias_quad.reshape(12, 128),
        out=[((384, 128), f32), ((16, 128), f32), ((8, 384, 128), bf16), ((8, 128), f32)],
    )
    acts_quad = lax.all_to_all(acts, DP, 0, 0)

    (terms,) = call(decode, dec_quad, acts_quad, out=[((16, BLOCK, 128), bf16)])
    terms, acts_sent = together((terms, acts_quad))
    parts = lax.all_to_all(terms, "z", 0, 0)
    acts_sent = relative(acts_sent.reshape(8, 4, 96, 128).transpose(1, 0, 2, 3))
    near, far = acts_sent[:2], neighbour(acts_sent[2:], "yl")
    mine = jnp.stack([near[0], far[0]])
    other = neighbour(jnp.stack([near[1], far[1]]), "c")
    acts_every = relative(jnp.stack([mine[0], other[0], mine[1], other[1]]))
    acts_every = acts_every.transpose(1, 0, 2, 3).reshape(8, 384, 128)
    colsum = jnp.sum(acts_every.reshape(8, 4, 3, 32, 128).astype(f32), axis=(0, 1, 3)).reshape(384)
    parts, acts_every, colsum = together((parts, acts_every, colsum))
    recon, gout = call(
        compare,
        parts,
        target_block,
        sparsity,
        out=[((BLOCK, 128), bf16), ((16, BLOCK, 128), bf16)],
    )
    gout_all = lax.all_to_all(gout, "z", 0, 0)

    gout_every = lax.all_gather(gout_all.reshape(2, 8 * BLOCK, 128), QUAD)
    slopes, loss_z = call(
        pull_back, gout_all, dec_quad, out=[((8, 384, 128), bf16), ((8, 128), f32)]
    )
    slopes = lax.all_to_all(slopes, DP, 0, 0)
    (sent,) = call(slopes_of, slopes, pre, norms, loss_z, out=[((4, 112, 128), bf16)])
    got = lax.all_to_all(sent, QUAD, 0, 0)
    (sent,) = call(regroup, got, out=[((8, 400, 128), bf16)])
    got = lax.all_to_all(sent, DP, 0, 0)

    (dec_full,) = call(over_tokens, gout_every, acts_every, out=[((8 * BLOCK, 384), f32)])
    dec_full = dec_full.reshape(8, BLOCK, 384)[:, :108].reshape(8, 3, 36, 384)
    dec_full = dec_full.transpose(1, 0, 2, 3).reshape(3, 288, 384)
    member = lax.axis_index(QUAD)
    own_norms = lax.dynamic_index_in_dim(norms[:12].reshape(4, 384), member, 0, False)
    pull = (sparsity_weight / TOK_DEV) * colsum / own_norms
    dec_grad = jnp.where(reach[:, None, :], dec_full + pull * dec_t.astype(f32), 0.0)
    got, dec_grad = together((got, dec_grad))
    x_every = lax.all_gather(x_quad, QUAD)
    (enc_full,) = call(over_tokens, x_every, got, out=[((8 * BLOCK, 384), f32)])
    enc_full = enc_full.reshape(8, BLOCK, 384)[:, :108].reshape(8, 3, 36, 384)
    enc_grad = jnp.sum(jnp.where(pick[None, :, None, :], enc_full, 0.0), axis=1).reshape(288, 384)
    tail = got[:, 384:396].astype(f32).sum(0).reshape(3, 4, 128).sum(0)
    bias_grad = tail[:3].reshape(384)
    loss = tail[3].sum() / TOK_DEV
    recon = lax.ppermute(recon, ALL, back)
    recon, enc_grad = together((recon, enc_grad))
    recon = recon[:108].reshape(3, 36, 128).transpose(2, 0, 1)
    return (loss, recon, enc_grad.T, bias_grad, dec_grad.transpose(2, 0, 1))


def solution(mesh):
    fine = Mesh(np.asarray(mesh.devices).reshape(SIZES), ALL)
    in_specs = (
        P(DP, None, LATENT),
        P(DP, None, LATENT),
        P(LATENT, DP),
        P(LATENT),
        P(LATENT, None, DP),
        P(LATENT),
    )
    out_specs = (
        P(),
        P(DP, None, LATENT),
        P(LATENT, DP),
        P(LATENT),
        P(LATENT, None, DP),
    )
    return jax.shard_map(
        on_device, mesh=fine, in_specs=in_specs, out_specs=out_specs, check_vma=False
    )
```

time: 271 us -> 275 us (1.015)
  blocking collectives: 62.7 us -> 80 us
  matrix products: 11 us -> 0 us
  Pallas kernels: 0 us -> 10.5 us
  starting transfers between devices: 77.4 us -> 72.5 us
  other arithmetic: 13.8 us -> 10.5 us
    all_gather x1, waiting for transfers between devices: 0.02 us -> 21.5 us  [on_device(): x_every = lax.all_gather(x_quad, QUAD)]
    all_to_all x2 -> x3, blocking collectives: 46.6 us -> 64 us  [the longest x1 31 us: on_device(): gout_all = lax.all_to_all(gout, 'z', 0, 0)]
    all_to_all x3 -> x1, waiting for transfers between devices: 14.1 us -> 1.72 us  [share(): lax.all_to_all(jnp.broadcast_to(block[None], (count, *block.shape)), axes...]
    dot_general x5 -> x0, matrix products: 11 us -> none  [dot(): return jnp.einsum(spec, a, b, preferred_element_type=f32)]
    pallas_call x0 -> x9, Pallas kernels: none -> 10.5 us  [call(): pl.pallas_call(kernel, out_shape=[jax.ShapeDtypeStruct(shape, dtype) for...]
    unnamed x27 -> x43, local copies, waits for them, and re-layouts: 1.02 us -> 10.8 us
    all_to_all x3 -> x1, starting transfers between devices: 33.6 us -> 24.1 us  [share(): lax.all_to_all(jnp.broadcast_to(block[None], (count, *block.shape)), axes...]
    ppermute x1, waiting for transfers between devices: 6.87 us -> 0.01 us  [on_device(): recon = lax.ppermute(recon, ALL, back)]
  transfers between devices with their start and end apart: 13 -> 12, of which waited for: 7 -> 7; matrix products, arithmetic and copies ran while one was open for 13% -> 7% of each run, Pallas kernels for 0% -> 3%
where the time goes in v4:
time: 275 us; the launch traced here: 274 us
  blocking collectives  80 us (29%)
  starting transfers between devices  72.5 us (26%)
  waiting for transfers between devices  65.7 us (24%)
  local copies, waits for them, and re-layouts  18.4 us (7%)
  between operations  16.1 us (6%)
  other arithmetic  10.5 us (4%)
  Pallas kernels  10.5 us (4%)
    all_to_all x1, blocking collectives, on_device(): gout_all = lax.all_to_all(gout, 'z', 0, 0)  31 us
    all_to_all x1, starting transfers between devices, share(): lax.all_to_all(jnp.broadcast_to(block[None], (count, *block.shape)), axes...  24.1 us
    all_gather x1, waiting for transfers between devices, on_device(): x_every = lax.all_gather(x_quad, QUAD)  21.5 us
    ppermute x2, starting transfers between devices, neighbour(): return lax.ppermute(block, axis, [(0, 1), (1, 0)])  17.6 us
    all_to_all x1, waiting for transfers between devices, on_device(): partial = lax.all_to_all(partial, DP, 0, 0)  17.4 us
    all_to_all x1, blocking collectives, on_device(): slopes = lax.all_to_all(slopes, DP, 0, 0)  16.9 us
    all_to_all x1, blocking collectives, on_device(): got = lax.all_to_all(sent, QUAD, 0, 0)  16.1 us
    all_gather x1, blocking collectives, on_device(): enc_quad = lax.all_gather(enc_own, QUAD)  16 us
  transfers between devices with their start and end apart: 12, of which 7 were waited for; matrix products, arithmetic and copies ran while one was open for 7% of the time, Pallas kernels for 3%

profile of v4, /device:TPU:1, one launch (start us, length us, event | category | flops | bytes accessed | tf_op | source)
XLA Modules:
  0.0 273.7 jit_solution(2599692133832360180)
XLA Ops:
  7.2 0.8 maximum_bitcast_fusion
  8.1 4.9 %collective-permute-start = (bf16[2,112,128]{2,1,0:T(8,128)(2,1)S(1)}, bf16[2,112,128]{2,1,0:T(8,128)(2,1)S(1)}, u32[]{:S(2)}, u32[]{:S(2)}) collective-permute-start(bf16[2,112,128]{2,1,0:T(8,128)(2,1)S(1)} %pad.21), channel_id=1, source_target_pairs={{0,0},{1,4},{2,8},{3,12},{4,16},{5,20},{6,24},{7,28},{8,64},{9,68}... | collective-permute-start | bytes 172040 | tf_op jit(solution)/shard_map/ppermute | solution.py:204
  13.0 1.3 iota_compare_fusion.1
  14.3 1.3 fusion
  15.7 0.1 reshape.155
  15.9 0.6 copy-done.12
  16.6 1.0 pad.20.clone
  17.7 0.6 slice_bitcast_fusion
  18.3 0.8 broadcast_in_dim.82
  19.1 24.1 %all-to-all-start = ((bf16[16,112,128]{2,1,0:T(8,128)(2,1)}), bf16[16,112,128]{2,1,0:T(8,128)(2,1)S(1)}, u32[]{:S(2)}, u32[]{:S(2)}) async-start(bf16[16,112,128]{2,1,0:T(8,128)(2,1)} %broadcast_in_dim.82), calls=%async_computation | async-start | bytes 917504 | tf_op jit(solution)/shard_map/all_to_all | solution.py:41
  43.3 16.0 %all-gather = bf16[1216,384]{1,0:T(8,128)(2,1)S(1)} all-gather(bf16[304,384]{1,0:T(8,128)(2,1)S(1)} %fusion.4), channel_id=2, replica_groups=mesh['x'=4,'yh'=2,'z'=16,'yl'=2,'c'=2] {'yl','c'}, dimensions={0}, use_global_device_ids=true | all-gather | bytes 1167360 | tf_op jit(solution)/shard_map/all_gather | solution.py:214
  59.7 0.5 copy.65
  60.2 0.2 copy.58
  60.4 0.2 broadcast_in_dim.87
  60.6 0.9 broadcast_select_fusion
  61.5 0.4 copy.69
  61.9 0.3 pad.23.clone
  62.2 1.7 all-to-all-done
  63.9 1.3 shard_map.101
  65.2 1.2 copy-done.2
  66.4 4.4 %all-to-all-start.1 = ((f32[8,400,128]{2,1,0:T(8,128)}), f32[8,400,128]{2,1,0:T(8,128)S(1)}, u32[]{:S(2)}, u32[]{:S(2)}) async-start(f32[8,400,128]{2,1,0:T(8,128)} %copy-done.2), calls=%async_computation.1 | async-start | bytes 3276800 | tf_op jit(solution)/shard_map/all_to_all | solution.py:229
  70.8 17.4 %all-to-all-done.1.parts = f32[8,400,128]{2,1,0:T(8,128)S(1)} async-done(((f32[8,400,128]{2,1,0:T(8,128)}), f32[8,400,128]{2,1,0:T(8,128)S(1)}, u32[]{:S(2)}, u32[]{:S(2)}) %all-to-all-start.1) | async-done | bytes 1638432 | tf_op jit(solution)/shard_map/all_to_all | solution.py:229
  88.2 1.0 shard_map.102
  89.2 0.7 copy-done.7
  89.8 5.2 %all-to-all-start.2 = ((bf16[8,384,128]{2,1,0:T(8,128)(2,1)}), bf16[8,384,128]{2,1,0:T(8,128)(2,1)S(1)}, u32[]{:S(2)}, u32[]{:S(2)}) async-start(bf16[8,384,128]{2,1,0:T(8,128)(2,1)} %get-tuple-element.22), calls=%async_computation.2 | async-start | bytes 1572864 | tf_op jit(solution)/shard_map/all_to_all | solution.py:236
  95.0 9.8 %all-to-all-done.2.acts = bf16[8,384,128]{2,1,0:T(8,128)(2,1)S(1)} async-done(((bf16[8,384,128]{2,1,0:T(8,128)(2,1)}), bf16[8,384,128]{2,1,0:T(8,128)(2,1)S(1)}, u32[]{:S(2)}, u32[]{:S(2)}) %all-to-all-start.2) | async-done | bytes 786464 | tf_op jit(solution)/shard_map/all_to_all | solution.py:236
  104.8 1.8 copy-done
  106.6 2.4 shard_map.103
  109.2 0.2 maximum_select_fusion.1
  109.4 13.6 %collective-permute-start.1 = (bf16[2,8,96,128]{3,2,0,1:T(8,128)(2,1)S(1)}, bf16[2,8,96,128]{3,2,0,1:T(8,128)(2,1)S(1)}, u32[]{:S(2)}, u32[]{:S(2)}) collective-permute-start(bf16[2,8,96,128]{3,2,0,1:T(8,128)(2,1)S(1)} %slice.163), channel_id=1, source_target_pairs={{0,2},{2,0},{1,3},{3,1},{4,6},{6,4},{5,7},{7,5},{8,10},{10,8},{9,1... | collective-permute-start | bytes 1179656 | tf_op jit(solution)/shard_map/ppermute | solution.py:181
  122.9 8.2 %all-to-all-start.3 = ((bf16[16,112,128]{2,1,0:T(8,128)(2,1)}), bf16[16,112,128]{2,1,0:T(8,128)(2,1)}, u32[]{:S(2)}, u32[]{:S(2)}) async-start(bf16[16,112,128]{2,1,0:T(8,128)(2,1)} %shard_map.103), calls=%async_computation.3 | async-start | bytes 917504 | tf_op jit(solution)/shard_map/all_to_all | solution.py:240
  131.3 4.0 %collective-permute-start.2 = (bf16[2,8,96,128]{3,2,0,1:T(8,128)(2,1)S(1)}, bf16[2,8,96,128]{3,2,0,1:T(8,128)(2,1)S(1)}, u32[]{:S(2)}, u32[]{:S(2)}) collective-permute-start(bf16[2,8,96,128]{3,2,0,1:T(8,128)(2,1)S(1)} %pad_maximum_fusion), channel_id=1, source_target_pairs={{0,1},{1,0},{2,3},{3,2},{4,5},{5,4},{6,7},{7,6},{8,9},{9,8},{10,11... | collective-permute-start | bytes 1179656 | tf_op jit(solution)/shard_map/ppermute | solution.py:181
  135.3 1.3 collective-permute-done.2
  136.7 0.2 maximum_select_fusion.2
  136.9 1.0 convert_reduce_fusion
  137.9 1.4 reduce_sum.67
  139.3 11.4 %all-to-all-done.3.parts = bf16[16,112,128]{2,1,0:T(8,128)(2,1)} async-done(((bf16[16,112,128]{2,1,0:T(8,128)(2,1)}), bf16[16,112,128]{2,1,0:T(8,128)(2,1)}, u32[]{:S(2)}, u32[]{:S(2)}) %all-to-all-start.3) | async-done | bytes 458784 | tf_op jit(solution)/shard_map/all_to_all | solution.py:240
  150.8 0.7 copy-done.9
  151.5 1.1 shard_map.104
  152.6 31.0 %all_to_all.40.gout = bf16[16,112,128]{2,1,0:T(8,128)(2,1)} all-to-all(bf16[16,112,128]{2,1,0:T(8,128)(2,1)S(1)} %get-tuple-element.27), channel_id=1, replica_groups=mesh['x'=4,'yh'=2,'z'=16,'yl'=2,'c'=2] {'z'}, dimensions={0} | all-to-all | bytes 917504 | tf_op jit(solution)/shard_map/all_to_all | solution.py:256
  183.7 0.7 all-gather.9.cloned.1.call-update
  184.4 1.0 copy-done.4
  185.4 1.3 shard_map.105
  186.7 16.9 %all_to_all.41.parts = bf16[8,384,128]{2,1,0:T(8,128)(2,1)S(1)} all-to-all(bf16[8,384,128]{2,1,0:T(8,128)(2,1)S(1)} %get-tuple-element.28), channel_id=1, replica_groups=mesh['x'=4,'yh'=2,'z'=16,'yl'=2,'c'=2] {'x','yh'}, dimensions={0} | all-to-all | bytes 1572864 | tf_op jit(solution)/shard_map/all_to_all | solution.py:262
  203.6 0.2 shard_map.106
  203.8 16.1 %all_to_all.42.got = bf16[4,112,128]{2,1,0:T(8,128)(2,1)S(1)} all-to-all(bf16[4,112,128]{2,1,0:T(8,128)(2,1)S(1)} %shard_map.106), channel_id=1, replica_groups=mesh['x'=4,'yh'=2,'z'=16,'yl'=2,'c'=2] {'yl','c'}, dimensions={0} | all-to-all | bytes 229376 | tf_op jit(solution)/shard_map/all_to_all | solution.py:264
  219.9 1.0 shard_map.107
  220.9 3.7 %all-to-all-start.7 = ((bf16[8,400,128]{2,1,0:T(8,128)(2,1)}), bf16[8,400,128]{2,1,0:T(8,128)(2,1)S(1)}, u32[]{:S(2)}, u32[]{:S(2)}) async-start(bf16[8,400,128]{2,1,0:T(8,128)(2,1)} %shard_map.107), calls=%async_computation.7 | async-start | bytes 1638400 | tf_op jit(solution)/shard_map/all_to_all | solution.py:266
  224.7 4.3 %collective-permute-start.3 = (bf16[112,128]{1,0:T(8,128)(2,1)S(1)}, bf16[112,128]{1,0:T(8,128)(2,1)S(1)}, u32[]{:S(2)}, u32[]{:S(2)}) collective-permute-start(bf16[112,128]{1,0:T(8,128)(2,1)S(1)} %copy-done.11), channel_id=1, source_target_pairs={{0,0},{4,1},{8,2},{12,3},{16,4},{20,5},{24,6},{28,7},{64,8},{68,9}... | collective-permute-start | bytes 86024 | tf_op jit(solution)/shard_map/ppermute | solution.py:283
  229.1 1.5 copy-done.6
  230.6 1.1 shard_map.108
  231.7 0.4 copy.66
  232.1 0.2 copy.61
  232.4 1.2 reshape.165
  233.6 2.6 fusion.2
  236.2 1.8 all-to-all-done.7.values
  238.0 21.5 %all-gather.9.cloned.1.call-done.blocks = bf16[4,2,896,128]{3,2,1,0:T(8,128)(2,1)} async-done(((bf16[1,2,896,128]{3,2,1,0:T(8,128)(2,1)}), bf16[4,2,896,128]{3,2,1,0:T(8,128)(2,1)}) %all-gather.9.cloned.1.call-update) | async-done | bytes 1835024 | tf_op jit(solution)/shard_map/all_gather | solution.py:276
  259.5 1.5 copy-done.5
  261.0 1.1 shard_map.109
  262.1 0.4 copy.67
  262.6 0.6 slice_bitcast_fusion.3
  263.3 0.6 slice_reduce_fusion
  264.0 0.8 reshape.170
  264.8 0.6 reshape.171
  (82 shorter events, 1.7 us)
Async XLA Ops:
  7.2 97.6 %all-gather.5.cloned.1.call-start = ((), (), s32[]{:S(2)}) async-start(), calls=%async_computation.8 | async-start | bytes 3440640 | tf_op jit(solution)/shard_map/all_gather | solution.py:215
  8.1 9.6 %collective-permute-start = (bf16[2,112,128]{2,1,0:T(8,128)(2,1)S(1)}, bf16[2,112,128]{2,1,0:T(8,128)(2,1)S(1)}, u32[]{:S(2)}, u32[]{:S(2)}) collective-permute-start(bf16[2,112,128]{2,1,0:T(8,128)(2,1)S(1)} %pad.21), channel_id=1, source_target_pairs={{0,0},{1,4},{2,8},{3,12},{4,16},{5,20},{6,24},{7,28},{8,64},{9,68}... | collective-permute-start | bytes 172040 | tf_op jit(solution)/shard_map/ppermute | solution.py:204
  15.7 0.8 copy-start.12
  16.6 1.0 copy-start.18
  16.6 1.0 copy-start.16
  17.6 25.7 %copy-start.14 = (bf16[384,288]{0,1:T(8,128)(2,1)S(1)}, bf16[384,288]{0,1:T(8,128)(2,1)}, u32[]{:S(2)}) copy-start(bf16[384,288]{0,1:T(8,128)(2,1)} %param.8) | copy-start | bytes 663556
  19.1 44.8 %all-to-all-start = ((bf16[16,112,128]{2,1,0:T(8,128)(2,1)}), bf16[16,112,128]{2,1,0:T(8,128)(2,1)S(1)}, u32[]{:S(2)}, u32[]{:S(2)}) async-start(bf16[16,112,128]{2,1,0:T(8,128)(2,1)} %broadcast_in_dim.82), calls=%async_computation | async-start | bytes 917504 | tf_op jit(solution)/shard_map/all_to_all | solution.py:41
  63.9 1.3 copy-start.3
  65.2 1.2 copy-start.2
  66.4 21.8 %all-to-all-start.1 = ((f32[8,400,128]{2,1,0:T(8,128)}), f32[8,400,128]{2,1,0:T(8,128)S(1)}, u32[]{:S(2)}, u32[]{:S(2)}) async-start(f32[8,400,128]{2,1,0:T(8,128)} %copy-done.2), calls=%async_computation.1 | async-start | bytes 3276800 | tf_op jit(solution)/shard_map/all_to_all | solution.py:229
  89.2 0.7 copy-start.7
  89.8 14.9 %all-to-all-start.2 = ((bf16[8,384,128]{2,1,0:T(8,128)(2,1)}), bf16[8,384,128]{2,1,0:T(8,128)(2,1)S(1)}, u32[]{:S(2)}, u32[]{:S(2)}) async-start(bf16[8,384,128]{2,1,0:T(8,128)(2,1)} %get-tuple-element.22), calls=%async_computation.2 | async-start | bytes 1572864 | tf_op jit(solution)/shard_map/all_to_all | solution.py:236
  104.8 1.8 copy-start
  109.4 21.9 %collective-permute-start.1 = (bf16[2,8,96,128]{3,2,0,1:T(8,128)(2,1)S(1)}, bf16[2,8,96,128]{3,2,0,1:T(8,128)(2,1)S(1)}, u32[]{:S(2)}, u32[]{:S(2)}) collective-permute-start(bf16[2,8,96,128]{3,2,0,1:T(8,128)(2,1)S(1)} %slice.163), channel_id=1, source_target_pairs={{0,2},{2,0},{1,3},{3,1},{4,6},{6,4},{5,7},{7,5},{8,10},{10,8},{9,1... | collective-permute-start | bytes 1179656 | tf_op jit(solution)/shard_map/ppermute | solution.py:181
  122.9 27.8 %all-to-all-start.3 = ((bf16[16,112,128]{2,1,0:T(8,128)(2,1)}), bf16[16,112,128]{2,1,0:T(8,128)(2,1)}, u32[]{:S(2)}, u32[]{:S(2)}) async-start(bf16[16,112,128]{2,1,0:T(8,128)(2,1)} %shard_map.103), calls=%async_computation.3 | async-start | bytes 917504 | tf_op jit(solution)/shard_map/all_to_all | solution.py:240
  131.1 98.0 %all-gather.7.cloned.1.call-start = ((), (), s32[]{:S(2)}) async-start(), calls=%async_computation.9 | async-start | bytes 2293760 | tf_op jit(solution)/shard_map/all_gather | solution.py:258
  131.3 5.4 %collective-permute-start.2 = (bf16[2,8,96,128]{3,2,0,1:T(8,128)(2,1)S(1)}, bf16[2,8,96,128]{3,2,0,1:T(8,128)(2,1)S(1)}, u32[]{:S(2)}, u32[]{:S(2)}) collective-permute-start(bf16[2,8,96,128]{3,2,0,1:T(8,128)(2,1)S(1)} %pad_maximum_fusion), channel_id=1, source_target_pairs={{0,1},{1,0},{2,3},{3,2},{4,5},{5,4},{6,7},{7,6},{8,9},{9,8},{10,11... | collective-permute-start | bytes 1179656 | tf_op jit(solution)/shard_map/ppermute | solution.py:181
  136.9 47.4 %copy-start.1 = (bf16[4,896,384]{2,1,0:T(8,128)(2,1)S(1)}, bf16[4,896,384]{2,1,0:T(8,128)(2,1)}, u32[]{:S(2)}) copy-start(bf16[4,896,384]{2,1,0:T(8,128)(2,1)} %all-gather.5.cloned.1.call-done.rows) | copy-start | bytes 8257540
  150.8 0.7 copy-start.9
  152.6 31.0 %copy-start.10 = (bf16[112,128]{1,0:T(8,128)(2,1)}, bf16[112,128]{1,0:T(8,128)(2,1)S(1)}, u32[]{:S(2)}) copy-start(bf16[112,128]{1,0:T(8,128)(2,1)S(1)} %get-tuple-element.35) | copy-start | bytes 86020
  183.6 75.9 %all-gather.9.cloned.1.call-start = ((), (), s32[]{:S(2)}) async-start(), calls=%async_computation.10 | async-start | bytes 2293760 | tf_op jit(solution)/shard_map/all_gather | solution.py:276
  184.4 1.0 copy-start.4
  186.7 17.0 %copy-start.8 = (f32[384,128]{1,0:T(8,128)S(1)}, f32[384,128]{1,0:T(8,128)}, u32[]{:S(2)}) copy-start(f32[384,128]{1,0:T(8,128)} %copy-done.7) | copy-start | bytes 589828
  219.9 4.8 %copy-start.11 = (bf16[112,128]{1,0:T(8,128)(2,1)S(1)}, bf16[112,128]{1,0:T(8,128)(2,1)}, u32[]{:S(2)}) copy-start(bf16[112,128]{1,0:T(8,128)(2,1)} %copy-done.10) | copy-start | bytes 86020
  219.9 9.2 %copy-start.15 = (f32[3,128]{1,0:T(4,128)S(1)}, f32[3,128]{1,0:T(4,128)}, u32[]{:S(2)}) copy-start(f32[3,128]{1,0:T(4,128)} %reduce_sum.67) | copy-start | bytes 4612
  220.9 17.0 %all-to-all-start.7 = ((bf16[8,400,128]{2,1,0:T(8,128)(2,1)}), bf16[8,400,128]{2,1,0:T(8,128)(2,1)S(1)}, u32[]{:S(2)}, u32[]{:S(2)}) async-start(bf16[8,400,128]{2,1,0:T(8,128)(2,1)} %shard_map.107), calls=%async_computation.7 | async-start | bytes 1638400 | tf_op jit(solution)/shard_map/all_to_all | solution.py:266
  224.7 40.1 %collective-permute-start.3 = (bf16[112,128]{1,0:T(8,128)(2,1)S(1)}, bf16[112,128]{1,0:T(8,128)(2,1)S(1)}, u32[]{:S(2)}, u32[]{:S(2)}) collective-permute-start(bf16[112,128]{1,0:T(8,128)(2,1)S(1)} %copy-done.11), channel_id=1, source_target_pairs={{0,0},{4,1},{8,2},{12,3},{16,4},{20,5},{24,6},{28,7},{64,8},{68,9}... | collective-permute-start | bytes 86024 | tf_op jit(solution)/shard_map/ppermute | solution.py:283
  229.1 1.5 copy-start.6
  232.4 1.2 copy-start.13
  259.5 1.5 copy-start.5
  262.1 1.1 copy-start.17
Sparse Core Ops, SparseCore 0:
  17.7 53.2 all-gather.4
  183.7 40.2 all-gather.6
  226.1 33.3 all-gather.8

commit v5 on v4

--- a/solution.py
+++ b/solution.py
@@ -14,6 +14,7 @@
 DP = ("x", "yh")
 LATENT = ("z", "yl", "c")
 QUAD = ("yl", "c")
+PLANE = ("yh", "yl", "c")
 BLOCK = 112
 
 sparsity_weight = 0.5
@@ -41,10 +42,11 @@
     return lax.all_to_all(jnp.broadcast_to(block[None], (count, *block.shape)), axes, 0, 0)
 
 
-def call(kernel, *args, out):
+def call(kernel, *args, out, scratch=()):
     return pl.pallas_call(
         kernel,
         out_shape=[jax.ShapeDtypeStruct(shape, dtype) for shape, dtype in out],
+        scratch_shapes=scratch,
         compiler_params=pltpu.CompilerParams(vmem_limit_bytes=40 * 1024 * 1024),
     )(*args)
 
@@ -153,28 +155,60 @@
             slope = total[k * 32 : k * 32 + 32] + (sparsity_weight / TOK_DEV) * norms[k : k + 1]
             slope = jnp.where(pre[k * 32 : k * 32 + 32] > 0, slope, 0.0)
             sums.append(jnp.sum(slope, axis=0, keepdims=True))
-            out[q, c * 32 : c * 32 + 32] = slope.astype(bf16)
-        out[q, 96:112] = tail_of([*sums, loss[0:1]])
+            for yh in range(2):
+                out[yh * 4 + q, c * 32 : c * 32 + 32] = slope.astype(bf16)
+        tail = tail_of([*sums, loss[0:1]])
+        for yh in range(2):
+            out[yh * 4 + q, 96:112] = tail
 
 
 def regroup(got, out):
     tail = jnp.sum(got[:, 96:112].astype(f32), axis=0)
     tail = tail[0:4] + tail[4:8] + tail[8:12]
     tail = tail_of([tail[k : k + 1] for k in range(4)])
-    for g in range(8):
-        for q in range(4):
-            out[g, q * 96 : q * 96 + 96] = got[q, 0:96]
-        out[g, 384:400] = tail
-
-
-def over_tokens(blocks, values, out):
+    for x in range(4):
+        for m in range(8):
+            out[x, m * 96 : m * 96 + 96] = got[m, 0:96]
+        out[x, 768:784] = tail
+
+
+def over_tokens(blocks, values):
     total = None
     for q in range(4):
         wide = jnp.concatenate([blocks[q, 0], blocks[q, 1]], axis=1)
-        column = lambda c: jnp.concatenate([tokens_of(values, h, q * 3 + c) for h in range(2)], axis=0)
+        column = lambda c: jnp.concatenate([values(h, q, c) for h in range(2)], axis=0)
         product = matmul(wide, jnp.concatenate([column(c) for c in range(3)], axis=1), 1, 0)
         total = product if total is None else total + product
-    out[...] = total
+    return total
+
+
+def decoder_gradient(blocks, acts, rows, pull, reach, out, total):
+    total[...] = over_tokens(blocks, lambda h, q, c: tokens_of(acts, h, q * 3 + c))
+    for layer in range(LAYERS):
+        for r in range(8):
+            at = r * BLOCK + layer * 36
+            out[layer, r * 36 : r * 36 + 36] = total[at : at + 36]
+        whole = out[layer] + pull[0:1] * rows[layer].astype(f32)
+        out[layer] = jnp.where(reach[layer : layer + 1] > 0, whole, 0.0)
+
+
+def encoder_gradient(blocks, dpre, pick, out, sums, total):
+    def values(half, q, c):
+        parts = [
+            dpre[half * 2 + g // 2, pl.ds(((g % 2) * 4 + q) * 96 + c * 32, 32)] for g in range(4)
+        ]
+        return jnp.concatenate(parts, axis=0)
+
+    total[...] = over_tokens(blocks, values)
+    for r in range(8):
+        own = jnp.zeros((36, 384), f32)
+        for layer in range(LAYERS):
+            at = r * BLOCK + layer * 36
+            own = own + jnp.where(pick[layer : layer + 1] > 0, total[at : at + 36], 0.0)
+        out[r * 36 : r * 36 + 36] = own
+    tail = jnp.sum(dpre[:, 768:784].astype(f32), axis=0)
+    sums[0:4] = tail[0:4] + tail[4:8] + tail[8:12]
+    sums[4:8] = jnp.zeros((4, 128), f32)
 
 
 def neighbour(block, axis):
@@ -225,6 +259,7 @@
 
     x_quad = share(x_block, "z", 16).reshape(2, 8 * BLOCK, 128)
     squares = jnp.pad(square_quad.reshape(12, 128), ((0, 4), (0, 0)))
+    x_quad, dec_quad = together((x_quad, dec_quad))
     (partial,) = call(encode, x_quad, enc_rows, squares, out=[((8, 400, 128), f32)])
     partial = lax.all_to_all(partial, DP, 0, 0)
     pre, norms, acts, sparsity = call(
@@ -253,6 +288,8 @@
         sparsity,
         out=[((BLOCK, 128), bf16), ((16, BLOCK, 128), bf16)],
     )
+    x_every = lax.all_gather(x_quad, QUAD)
+    gout, x_every = together((gout, x_every))
     gout_all = lax.all_to_all(gout, "z", 0, 0)
 
     gout_every = lax.all_gather(gout_all.reshape(2, 8 * BLOCK, 128), QUAD)
@@ -260,26 +297,36 @@
         pull_back, gout_all, dec_quad, out=[((8, 384, 128), bf16), ((8, 128), f32)]
     )
     slopes = lax.all_to_all(slopes, DP, 0, 0)
-    (sent,) = call(slopes_of, slopes, pre, norms, loss_z, out=[((4, 112, 128), bf16)])
-    got = lax.all_to_all(sent, QUAD, 0, 0)
-    (sent,) = call(regroup, got, out=[((8, 400, 128), bf16)])
-    got = lax.all_to_all(sent, DP, 0, 0)
-
-    (dec_full,) = call(over_tokens, gout_every, acts_every, out=[((8 * BLOCK, 384), f32)])
-    dec_full = dec_full.reshape(8, BLOCK, 384)[:, :108].reshape(8, 3, 36, 384)
-    dec_full = dec_full.transpose(1, 0, 2, 3).reshape(3, 288, 384)
+    (sent,) = call(slopes_of, slopes, pre, norms, loss_z, out=[((8, 112, 128), bf16)])
+    got = lax.all_to_all(sent, PLANE, 0, 0)
+    (sent,) = call(regroup, got, out=[((4, 784, 128), bf16)])
+    got = lax.all_to_all(sent, "x", 0, 0)
+
+    total = pltpu.VMEM((8 * BLOCK, 384), f32)
     member = lax.axis_index(QUAD)
     own_norms = lax.dynamic_index_in_dim(norms[:12].reshape(4, 384), member, 0, False)
-    pull = (sparsity_weight / TOK_DEV) * colsum / own_norms
-    dec_grad = jnp.where(reach[:, None, :], dec_full + pull * dec_t.astype(f32), 0.0)
+    pull = ((sparsity_weight / TOK_DEV) * colsum / own_norms)[None]
+    (dec_grad,) = call(
+        decoder_gradient,
+        gout_every,
+        acts_every,
+        dec_t,
+        pull,
+        reach.astype(f32),
+        out=[((LAYERS, 288, 384), f32)],
+        scratch=[total],
+    )
     got, dec_grad = together((got, dec_grad))
-    x_every = lax.all_gather(x_quad, QUAD)
-    (enc_full,) = call(over_tokens, x_every, got, out=[((8 * BLOCK, 384), f32)])
-    enc_full = enc_full.reshape(8, BLOCK, 384)[:, :108].reshape(8, 3, 36, 384)
-    enc_grad = jnp.sum(jnp.where(pick[None, :, None, :], enc_full, 0.0), axis=1).reshape(288, 384)
-    tail = got[:, 384:396].astype(f32).sum(0).reshape(3, 4, 128).sum(0)
-    bias_grad = tail[:3].reshape(384)
-    loss = tail[3].sum() / TOK_DEV
+    enc_grad, sums = call(
+        encoder_gradient,
+        x_every,
+        got,
+        pick.astype(f32),
+        out=[((288, 384), f32), ((8, 128), f32)],
+        scratch=[total],
+    )
+    bias_grad = sums[:3].reshape(384)
+    loss = sums[3].sum() / TOK_DEV
     recon = lax.ppermute(recon, ALL, back)
     recon, enc_grad = together((recon, enc_grad))
     recon = recon[:108].reshape(3, 36, 128).transpose(2, 0, 1)

time: 275 us -> 261 us (0.949)
  waiting for transfers between devices: 65.7 us -> 39.4 us
  starting transfers between devices: 72.5 us -> 81.1 us
  blocking collectives: 80 us -> 83.6 us
  other arithmetic: 10.5 us -> 7.04 us
    all_gather x1, waiting for transfers between devices: 21.5 us -> 0.01 us  [on_device(): x_every = lax.all_gather(x_quad, QUAD)]
    all_to_all x1, waiting for transfers between devices: 11.4 us -> 4.51 us  [on_device(): parts = lax.all_to_all(terms, 'z', 0, 0)]
    ppermute x2, starting transfers between devices: 17.6 us -> 22.1 us  [neighbour(): return lax.ppermute(block, axis, [(0, 1), (1, 0)])]
    all_to_all x1, blocking collectives: 16.1 us -> 19.5 us  [on_device(): got = lax.all_to_all(sent, PLANE, 0, 0)]
    all_to_all x1, starting transfers between devices: 24.1 us -> 27.3 us  [share(): lax.all_to_all(jnp.broadcast_to(block[None], (count, *block.shape)), axes...]
    unnamed x43 -> x53, local copies, waits for them, and re-layouts: 10.8 us -> 11.6 us
  transfers between devices with their start and end apart: 12 -> 12, of which waited for: 7 -> 7; matrix products, arithmetic and copies ran while one was open for 7% -> 4% of each run, Pallas kernels for 3% -> 4%
where the time goes in v5:
time: 261 us; the launch traced here: 258 us
  blocking collectives  83.6 us (32%)
  starting transfers between devices  81.1 us (31%)
  waiting for transfers between devices  39.4 us (15%)
  local copies, waits for them, and re-layouts  18.6 us (7%)
  between operations  16.1 us (6%)
  Pallas kernels  12.1 us (5%)
  other arithmetic  7.04 us (3%)
    all_to_all x1, blocking collectives, on_device(): gout_all = lax.all_to_all(gout, 'z', 0, 0)  31.5 us
    all_to_all x1, starting transfers between devices, share(): lax.all_to_all(jnp.broadcast_to(block[None], (count, *block.shape)), axes...  27.3 us
    ppermute x2, starting transfers between devices, neighbour(): return lax.ppermute(block, axis, [(0, 1), (1, 0)])  22.1 us
    all_to_all x1, blocking collectives, on_device(): got = lax.all_to_all(sent, PLANE, 0, 0)  19.5 us
    all_to_all x1, waiting for transfers between devices, on_device(): partial = lax.all_to_all(partial, DP, 0, 0)  17.5 us
    all_to_all x1, blocking collectives, on_device(): slopes = lax.all_to_all(slopes, DP, 0, 0)  16.6 us
    all_gather x1, blocking collectives, on_device(): enc_quad = lax.all_gather(enc_own, QUAD)  16 us
    pallas_call x9, Pallas kernels, call(): pl.pallas_call(kernel, out_shape=[jax.ShapeDtypeStruct(shape, dtype) for...  12.1 us
  transfers between devices with their start and end apart: 12, of which 7 were waited for; matrix products, arithmetic and copies ran while one was open for 4% of the time, Pallas kernels for 4%

profile of v5, /device:TPU:1, one launch (start us, length us, event | category | flops | bytes accessed | tf_op | source)
XLA Modules:
  0.0 258.1 jit_solution(3367097184804555639)
XLA Ops:
  7.2 1.3 fusion.5
  8.5 1.3 multiply_reduce_fusion
  9.8 0.1 reshape.117
  10.2 0.5 copy-done.2
  10.7 0.9 pad.21.clone
  11.8 4.9 %collective-permute-start = (bf16[2,112,128]{2,1,0:T(8,128)(2,1)S(1)}, bf16[2,112,128]{2,1,0:T(8,128)(2,1)S(1)}, u32[]{:S(2)}, u32[]{:S(2)}) collective-permute-start(bf16[2,112,128]{2,1,0:T(8,128)(2,1)S(1)} %pad.20), channel_id=1, source_target_pairs={{0,0},{1,4},{2,8},{3,12},{4,16},{5,20},{6,24},{7,28},{8,64},{9,68}... | collective-permute-start | bytes 172040 | tf_op jit(solution)/shard_map/ppermute | solution.py:238
  16.8 1.3 collective-permute-done
  18.1 0.6 slice_bitcast_fusion
  18.7 0.8 broadcast_in_dim.58
  19.6 27.3 %all-to-all-start = ((bf16[16,112,128]{2,1,0:T(8,128)(2,1)}), bf16[16,112,128]{2,1,0:T(8,128)(2,1)S(1)}, u32[]{:S(2)}, u32[]{:S(2)}) async-start(bf16[16,112,128]{2,1,0:T(8,128)(2,1)} %broadcast_in_dim.58), calls=%async_computation | async-start | bytes 917504 | tf_op jit(solution)/shard_map/all_to_all | solution.py:42
  47.0 16.0 %all-gather = bf16[1216,384]{1,0:T(8,128)(2,1)S(1)} all-gather(bf16[304,384]{1,0:T(8,128)(2,1)S(1)} %fusion.1), channel_id=2, replica_groups=mesh['x'=4,'yh'=2,'z'=16,'yl'=2,'c'=2] {'yl','c'}, dimensions={0}, use_global_device_ids=true | all-gather | bytes 1167360 | tf_op jit(solution)/shard_map/all_gather | solution.py:248
  63.1 0.5 copy.48
  63.6 0.2 copy.45
  64.1 0.2 broadcast_in_dim.65
  64.3 0.8 broadcast_select_fusion
  65.2 0.4 copy.50
  65.5 0.3 pad.23.clone
  65.8 1.7 all-to-all-done
  67.6 1.3 shard_map.101
  68.9 1.2 copy-done.1
  70.1 4.4 %all-to-all-start.1 = ((f32[8,400,128]{2,1,0:T(8,128)}), f32[8,400,128]{2,1,0:T(8,128)}, u32[]{:S(2)}, u32[]{:S(2)}) async-start(f32[8,400,128]{2,1,0:T(8,128)} %copy-done.1), calls=%async_computation.1 | async-start | bytes 3276800 | tf_op jit(solution)/shard_map/all_to_all | solution.py:264
  74.6 17.5 %all-to-all-done.1.parts = f32[8,400,128]{2,1,0:T(8,128)} async-done(((f32[8,400,128]{2,1,0:T(8,128)}), f32[8,400,128]{2,1,0:T(8,128)}, u32[]{:S(2)}, u32[]{:S(2)}) %all-to-all-start.1) | async-done | bytes 1638432 | tf_op jit(solution)/shard_map/all_to_all | solution.py:264
  92.0 1.5 shard_map.102
  93.6 0.9 copy-done.9
  94.5 0.7 copy-done.11
  95.1 0.6 copy-done.15
  95.7 5.2 %all-to-all-start.2 = ((bf16[8,384,128]{2,1,0:T(8,128)(2,1)}), bf16[8,384,128]{2,1,0:T(8,128)(2,1)S(1)}, u32[]{:S(2)}, u32[]{:S(2)}) async-start(bf16[8,384,128]{2,1,0:T(8,128)(2,1)} %copy-done.9), calls=%async_computation.2 | async-start | bytes 1572864 | tf_op jit(solution)/shard_map/all_to_all | solution.py:271
  100.9 0.7 all-gather.10.cloned.1.call-update
  101.6 9.0 %all-to-all-done.2.acts = bf16[8,384,128]{2,1,0:T(8,128)(2,1)S(1)} async-done(((bf16[8,384,128]{2,1,0:T(8,128)(2,1)}), bf16[8,384,128]{2,1,0:T(8,128)(2,1)S(1)}, u32[]{:S(2)}, u32[]{:S(2)}) %all-to-all-start.2) | async-done | bytes 786464 | tf_op jit(solution)/shard_map/all_to_all | solution.py:271
  110.7 1.6 shard_map.103
  112.4 0.1 maximum_select_fusion
  112.5 0.1 maximum_select_fusion.1
  112.7 0.8 slice.151
  113.4 12.1 %collective-permute-start.1 = (bf16[2,8,96,128]{3,2,0,1:T(8,128)(2,1)}, bf16[2,8,96,128]{3,2,0,1:T(8,128)(2,1)}, u32[]{:S(2)}, u32[]{:S(2)}) collective-permute-start(bf16[2,8,96,128]{3,2,0,1:T(8,128)(2,1)} %slice.151), channel_id=1, source_target_pairs={{0,2},{2,0},{1,3},{3,1},{4,6},{6,4},{5,7},{7,5},{8,10},{10,8},{9,1... | collective-permute-start | bytes 1179656 | tf_op jit(solution)/shard_map/ppermute | solution.py:215
  125.5 9.3 %all-to-all-start.3 = ((bf16[16,112,128]{2,1,0:T(8,128)(2,1)}), bf16[16,112,128]{2,1,0:T(8,128)(2,1)}, u32[]{:S(2)}, u32[]{:S(2)}) async-start(bf16[16,112,128]{2,1,0:T(8,128)(2,1)} %copy-done.8), calls=%async_computation.3 | async-start | bytes 917504 | tf_op jit(solution)/shard_map/all_to_all | solution.py:275
  134.9 1.1 fusion.10
  136.0 10.0 %collective-permute-start.2 = (bf16[2,8,96,128]{3,2,0,1:T(8,128)(2,1)S(1)}, bf16[2,8,96,128]{3,2,0,1:T(8,128)(2,1)S(1)}, u32[]{:S(2)}, u32[]{:S(2)}) collective-permute-start(bf16[2,8,96,128]{3,2,0,1:T(8,128)(2,1)S(1)} %pad_maximum_fusion), channel_id=1, source_target_pairs={{0,1},{1,0},{2,3},{3,2},{4,5},{5,4},{6,7},{7,6},{8,9},{9,8},{10,11... | collective-permute-start | bytes 1179656 | tf_op jit(solution)/shard_map/ppermute | solution.py:215
  146.0 1.3 collective-permute-done.2
  147.3 0.2 maximum_select_fusion.2
  147.6 1.0 convert_reduce_fusion
  148.5 1.4 reduce_sum.40
  149.9 4.5 %all-to-all-done.3.parts = bf16[16,112,128]{2,1,0:T(8,128)(2,1)} async-done(((bf16[16,112,128]{2,1,0:T(8,128)(2,1)}), bf16[16,112,128]{2,1,0:T(8,128)(2,1)}, u32[]{:S(2)}, u32[]{:S(2)}) %all-to-all-start.3) | async-done | bytes 458784 | tf_op jit(solution)/shard_map/all_to_all | solution.py:275
  154.4 0.7 copy-done.13
  155.2 0.7 copy-done.16
  155.9 1.1 shard_map.104
  157.0 0.8 copy-done.10
  157.8 0.6 copy-done.17
  158.4 31.5 %all_to_all.40.gout = bf16[16,112,128]{2,1,0:T(8,128)(2,1)} all-to-all(bf16[16,112,128]{2,1,0:T(8,128)(2,1)} %copy-done.10), channel_id=1, replica_groups=mesh['x'=4,'yh'=2,'z'=16,'yl'=2,'c'=2] {'z'}, dimensions={0} | all-to-all | bytes 917504 | tf_op jit(solution)/shard_map/all_to_all | solution.py:293
  189.9 1.0 copy-done.5
  190.9 1.3 shard_map.105
  192.2 16.6 %all_to_all.41.parts = bf16[8,384,128]{2,1,0:T(8,128)(2,1)S(1)} all-to-all(bf16[8,384,128]{2,1,0:T(8,128)(2,1)S(1)} %get-tuple-element.38), channel_id=1, replica_groups=mesh['x'=4,'yh'=2,'z'=16,'yl'=2,'c'=2] {'x','yh'}, dimensions={0} | all-to-all | bytes 1572864 | tf_op jit(solution)/shard_map/all_to_all | solution.py:299
  208.8 0.2 shard_map.106
  209.0 19.5 %all_to_all.42.got = bf16[8,112,128]{2,1,0:T(8,128)(2,1)S(1)} all-to-all(bf16[8,112,128]{2,1,0:T(8,128)(2,1)S(1)} %shard_map.106), channel_id=1, replica_groups=mesh['x'=4,'yh'=2,'z'=16,'yl'=2,'c'=2] {'yh','yl','c'}, dimensions={0} | all-to-all | bytes 458752 | tf_op jit(solution)/shard_map/all_to_all | solution.py:301
  228.5 1.0 shard_map.107
  229.5 3.5 %all-to-all-start.7 = ((bf16[4,784,128]{2,1,0:T(8,128)(2,1)}), bf16[4,784,128]{2,1,0:T(8,128)(2,1)S(1)}, u32[]{:S(2)}, u32[]{:S(2)}) async-start(bf16[4,784,128]{2,1,0:T(8,128)(2,1)} %shard_map.107), calls=%async_computation.7 | async-start | bytes 1605632 | tf_op jit(solution)/shard_map/all_to_all | solution.py:303
  233.1 4.4 %collective-permute-start.3 = (bf16[112,128]{1,0:T(8,128)(2,1)S(1)}, bf16[112,128]{1,0:T(8,128)(2,1)S(1)}, u32[]{:S(2)}, u32[]{:S(2)}) collective-permute-start(bf16[112,128]{1,0:T(8,128)(2,1)S(1)} %copy-done.18), channel_id=1, source_target_pairs={{0,0},{4,1},{8,2},{12,3},{16,4},{20,5},{24,6},{28,7},{64,8},{68,9}... | collective-permute-start | bytes 86024 | tf_op jit(solution)/shard_map/ppermute | solution.py:330
  237.5 1.5 copy-done.7
  239.0 2.2 shard_map.108
  241.3 3.3 %all-to-all-done.7.dpre = bf16[4,784,128]{2,1,0:T(8,128)(2,1)S(1)} async-done(((bf16[4,784,128]{2,1,0:T(8,128)(2,1)}), bf16[4,784,128]{2,1,0:T(8,128)(2,1)S(1)}, u32[]{:S(2)}, u32[]{:S(2)}) %all-to-all-start.7) | async-done | bytes 802848 | tf_op jit(solution)/shard_map/all_to_all | solution.py:303
  244.5 1.5 copy-done.6
  246.0 1.9 shard_map.109
  247.9 0.6 slice_bitcast_fusion.3
  248.5 0.6 slice_reduce_fusion
  249.1 0.6 reshape.124
  (84 shorter events, 1.3 us)
Async XLA Ops:
  7.2 60.4 %all-gather.6.cloned.1.call-start = ((), (), s32[]{:S(2)}) async-start(), calls=%async_computation.8 | async-start | bytes 3440640 | tf_op jit(solution)/shard_map/all_gather | solution.py:249
  9.8 0.8 copy-start.2
  10.1 1.6 copy-start.20
  10.1 1.6 copy-start.21
  10.1 6.6 %copy-start.24 = (f32[384]{0:T(512)S(1)}, f32[384]{0:T(512)}, u32[]{:S(2)}) copy-start(f32[384]{0:T(512)} %param.9) | copy-start | bytes 4612
  10.1 6.6 %copy-start.23 = (s32[384]{0:T(512)S(1)}, s32[384]{0:T(512)}, u32[]{:S(2)}) copy-start(s32[384]{0:T(512)} %param.11) | copy-start | bytes 4612
  10.7 36.2 %copy-start.19 = (bf16[384,288]{0,1:T(8,128)(2,1)S(1)}, bf16[384,288]{0,1:T(8,128)(2,1)}, u32[]{:S(2)}) copy-start(bf16[384,288]{0,1:T(8,128)(2,1)} %param.8) | copy-start | bytes 663556
  11.8 6.4 %collective-permute-start = (bf16[2,112,128]{2,1,0:T(8,128)(2,1)S(1)}, bf16[2,112,128]{2,1,0:T(8,128)(2,1)S(1)}, u32[]{:S(2)}, u32[]{:S(2)}) collective-permute-start(bf16[2,112,128]{2,1,0:T(8,128)(2,1)S(1)} %pad.20), channel_id=1, source_target_pairs={{0,0},{1,4},{2,8},{3,12},{4,16},{5,20},{6,24},{7,28},{8,64},{9,68}... | collective-permute-start | bytes 172040 | tf_op jit(solution)/shard_map/ppermute | solution.py:238
  19.6 48.0 %all-to-all-start = ((bf16[16,112,128]{2,1,0:T(8,128)(2,1)}), bf16[16,112,128]{2,1,0:T(8,128)(2,1)S(1)}, u32[]{:S(2)}, u32[]{:S(2)}) async-start(bf16[16,112,128]{2,1,0:T(8,128)(2,1)} %broadcast_in_dim.58), calls=%async_computation | async-start | bytes 917504 | tf_op jit(solution)/shard_map/all_to_all | solution.py:42
  67.6 1.3 copy-start.4
  68.9 1.2 copy-start.1
  70.1 21.9 %all-to-all-start.1 = ((f32[8,400,128]{2,1,0:T(8,128)}), f32[8,400,128]{2,1,0:T(8,128)}, u32[]{:S(2)}, u32[]{:S(2)}) async-start(f32[8,400,128]{2,1,0:T(8,128)} %copy-done.1), calls=%async_computation.1 | async-start | bytes 3276800 | tf_op jit(solution)/shard_map/all_to_all | solution.py:264
  74.6 36.1 %copy-start = (bf16[4,896,384]{2,1,0:T(8,128)(2,1)S(1)}, bf16[4,896,384]{2,1,0:T(8,128)(2,1)}, u32[]{:S(2)}) copy-start(bf16[4,896,384]{2,1,0:T(8,128)(2,1)} %all-gather.6.cloned.1.call-done.rows) | copy-start | bytes 8257540
  93.6 0.9 copy-start.9
  94.5 0.7 copy-start.11
  95.1 0.6 copy-start.15
  95.7 14.9 %all-to-all-start.2 = ((bf16[8,384,128]{2,1,0:T(8,128)(2,1)}), bf16[8,384,128]{2,1,0:T(8,128)(2,1)S(1)}, u32[]{:S(2)}, u32[]{:S(2)}) async-start(bf16[8,384,128]{2,1,0:T(8,128)(2,1)} %copy-done.9), calls=%async_computation.2 | async-start | bytes 1572864 | tf_op jit(solution)/shard_map/all_to_all | solution.py:271
  100.9 57.5 %all-gather.10.cloned.1.call-start = ((), (), s32[]{:S(2)}) async-start(), calls=%async_computation.10 | async-start | bytes 2293760 | tf_op jit(solution)/shard_map/all_gather | solution.py:291
  112.3 1.2 copy-start.8
  113.4 21.4 %collective-permute-start.1 = (bf16[2,8,96,128]{3,2,0,1:T(8,128)(2,1)}, bf16[2,8,96,128]{3,2,0,1:T(8,128)(2,1)}, u32[]{:S(2)}, u32[]{:S(2)}) collective-permute-start(bf16[2,8,96,128]{3,2,0,1:T(8,128)(2,1)} %slice.151), channel_id=1, source_target_pairs={{0,2},{2,0},{1,3},{3,1},{4,6},{6,4},{5,7},{7,5},{8,10},{10,8},{9,1... | collective-permute-start | bytes 1179656 | tf_op jit(solution)/shard_map/ppermute | solution.py:215
  125.5 28.9 %all-to-all-start.3 = ((bf16[16,112,128]{2,1,0:T(8,128)(2,1)}), bf16[16,112,128]{2,1,0:T(8,128)(2,1)}, u32[]{:S(2)}, u32[]{:S(2)}) async-start(bf16[16,112,128]{2,1,0:T(8,128)(2,1)} %copy-done.8), calls=%async_computation.3 | async-start | bytes 917504 | tf_op jit(solution)/shard_map/all_to_all | solution.py:275
  134.8 102.7 %all-gather.8.cloned.1.call-start = ((), (), s32[]{:S(2)}) async-start(), calls=%async_computation.9 | async-start | bytes 2293760 | tf_op jit(solution)/shard_map/all_gather | solution.py:295
  136.0 11.3 %collective-permute-start.2 = (bf16[2,8,96,128]{3,2,0,1:T(8,128)(2,1)S(1)}, bf16[2,8,96,128]{3,2,0,1:T(8,128)(2,1)S(1)}, u32[]{:S(2)}, u32[]{:S(2)}) collective-permute-start(bf16[2,8,96,128]{3,2,0,1:T(8,128)(2,1)S(1)} %pad_maximum_fusion), channel_id=1, source_target_pairs={{0,1},{1,0},{2,3},{3,2},{4,5},{5,4},{6,7},{7,6},{8,9},{9,8},{10,11... | collective-permute-start | bytes 1179656 | tf_op jit(solution)/shard_map/ppermute | solution.py:215
  154.4 0.7 copy-start.13
  155.2 0.7 copy-start.16
  157.0 0.8 copy-start.10
  157.8 0.6 copy-start.17
  189.9 1.0 copy-start.5
  190.9 17.9 %copy-start.12 = (f32[384,128]{1,0:T(8,128)S(1)}, f32[384,128]{1,0:T(8,128)}, u32[]{:S(2)}) copy-start(f32[384,128]{1,0:T(8,128)} %copy-done.11) | copy-start | bytes 589828
  209.0 24.0 %copy-start.22 = (f32[3,128]{1,0:T(4,128)S(1)}, f32[3,128]{1,0:T(4,128)}, u32[]{:S(2)}) copy-start(f32[3,128]{1,0:T(4,128)} %reduce_sum.40) | copy-start | bytes 4612
  209.0 24.1 %copy-start.18 = (bf16[112,128]{1,0:T(8,128)(2,1)S(1)}, bf16[112,128]{1,0:T(8,128)(2,1)}, u32[]{:S(2)}) copy-start(bf16[112,128]{1,0:T(8,128)(2,1)} %copy-done.17) | copy-start | bytes 86020
  209.0 28.5 %copy-start.3 = (bf16[3,288,384]{2,1,0:T(8,128)(2,1)S(1)}, bf16[3,288,384]{2,1,0:T(8,128)(2,1)}, u32[]{:S(2)}) copy-start(bf16[3,288,384]{2,1,0:T(8,128)(2,1)} %copy-done.2) | copy-start | bytes 1990660
  229.5 15.1 %all-to-all-start.7 = ((bf16[4,784,128]{2,1,0:T(8,128)(2,1)}), bf16[4,784,128]{2,1,0:T(8,128)(2,1)S(1)}, u32[]{:S(2)}, u32[]{:S(2)}) async-start(bf16[4,784,128]{2,1,0:T(8,128)(2,1)} %shard_map.107), calls=%async_computation.7 | async-start | bytes 1605632 | tf_op jit(solution)/shard_map/all_to_all | solution.py:303
  233.1 16.1 %collective-permute-start.3 = (bf16[112,128]{1,0:T(8,128)(2,1)S(1)}, bf16[112,128]{1,0:T(8,128)(2,1)S(1)}, u32[]{:S(2)}, u32[]{:S(2)}) collective-permute-start(bf16[112,128]{1,0:T(8,128)(2,1)S(1)} %copy-done.18), channel_id=1, source_target_pairs={{0,0},{4,1},{8,2},{12,3},{16,4},{20,5},{24,6},{28,7},{64,8},{68,9}... | collective-permute-start | bytes 86024 | tf_op jit(solution)/shard_map/ppermute | solution.py:330
  237.5 1.5 copy-start.7
  239.0 5.5 %copy-start.14 = (f32[3,384]{1,0:T(4,128)S(1)}, f32[3,384]{1,0:T(4,128)}, u32[]{:S(2)}) copy-start(f32[3,384]{1,0:T(4,128)} %get-tuple-element.78.pick) | copy-start | bytes 13828
  244.5 1.5 copy-start.6
Sparse Core Ops, SparseCore 0:
  11.8 53.1 all-gather.5
  103.8 46.5 all-gather.9
  190.0 40.5 all-gather.7

commit v6 on v5

--- a/solution.py
+++ b/solution.py
@@ -22,12 +22,46 @@
 bf16, f32 = jnp.bfloat16, jnp.float32
 
 
+PAIRS = ((0, 5), (1, 4), (2, 7), (3, 6))
+
+
+def ring(a, b, size):
+    return min((a - b) % size, (b - a) % size)
+
+
+def placing(i, q):
+    x, yh = divmod(i, 2)
+    hops = []
+    for a in PAIRS[q]:
+        for r in range(8):
+            beside = ring(a // 2, x, 4) + ring(2 * (a % 2) + r % 4 // 2, 2 * yh + q // 2, 4)
+            hops.append([beside + ring(2 * i + r // 4, z, 16) for z in range(16)])
+
+    def seat(block, seen):
+        for z in range(16):
+            if hops[block][z] <= most and z not in seen:
+                seen.add(z)
+                if owner[z] is None or seat(owner[z], seen):
+                    owner[z] = block
+                    return True
+        return False
+
+    for most in range(16):
+        owner = [None] * 16
+        if all(seat(block, set()) for block in range(16)):
+            return [owner.index(block) for block in range(16)]
+
+
+PLACE = [[placing(i, q) for q in range(4)] for i in range(8)]
+
+
 def spread():
     pairs = []
-    for a in range(8):
-        for b in range(64):
-            i, r = divmod(b, 8)
-            pairs.append((a * 64 + b, i * 64 + ((a % 2) * 8 + r) * 4 + a // 2))
+    for i in range(8):
+        for q in range(4):
+            for block, z in enumerate(PLACE[i][q]):
+                half, r = divmod(block, 8)
+                pairs.append((PAIRS[q][half] * 64 + 8 * i + r, i * 64 + z * 4 + q))
     return pairs
 
 
@@ -43,11 +77,19 @@
 
 
 def call(kernel, *args, out, scratch=()):
+    def place(arg):
+        if arg.dtype == jnp.int32:
+            return pl.BlockSpec(memory_space=pltpu.SMEM)
+        if arg.shape == (4, 16, BLOCK, 128):
+            return pl.BlockSpec(memory_space=pl.ANY)
+        return pl.BlockSpec(memory_space=pltpu.VMEM)
+
     return pl.pallas_call(
         kernel,
+        in_specs=[place(arg) for arg in args],
         out_shape=[jax.ShapeDtypeStruct(shape, dtype) for shape, dtype in out],
         scratch_shapes=scratch,
-        compiler_params=pltpu.CompilerParams(vmem_limit_bytes=40 * 1024 * 1024),
+        compiler_params=pltpu.CompilerParams(vmem_limit_bytes=(58 if scratch else 40) * 2**20),
     )(*args)
 
 
@@ -62,10 +104,11 @@
     return lax.dot_general(a, b, (((left,), (right,)), ((), ())), preferred_element_type=f32)
 
 
-def encode(x, rows, squares, out):
+def encode(at_z, x, rows, squares, out):
     for half in range(2):
+        tokens = jnp.concatenate([x[at_z[half * 8 + r]] for r in range(8)], axis=0)
         for q in range(4):
-            product = matmul(x[half], rows[q], 0, 0)
+            product = matmul(tokens, rows[q], 0, 0)
             for g in range(4):
                 for c in range(3):
                     at = (q * 3 + c) * 32
@@ -96,7 +139,7 @@
     return ref[half * 4 : half * 4 + 4, column * 32 : column * 32 + 32].reshape(128, 128)
 
 
-def decode(rows, acts, out):
+def decode(at_z, rows, acts, out):
     for half in range(2):
         total = None
         for q in range(4):
@@ -105,7 +148,7 @@
             total = product if total is None else total + product
         low = total.astype(bf16)
         for r in range(8):
-            out[half * 8 + r] = low[r * BLOCK : (r + 1) * BLOCK]
+            out[at_z[half * 8 + r]] = low[r * BLOCK : (r + 1) * BLOCK]
 
 
 def compare(parts, target, sparsity, recon, gout):
@@ -122,11 +165,11 @@
         gout[z] = low
 
 
-def pull_back(gout, rows, out, loss):
+def pull_back(at_z, gout, rows, out, loss):
     total = jnp.sum(gout[:, 96:112].astype(f32), axis=0)
     loss[...] = jnp.broadcast_to(jnp.sum(total[12:15], axis=0, keepdims=True), (8, 128))
     for half in range(2):
-        tokens = jnp.concatenate([gout[half * 8 + r] for r in range(8)], axis=0)
+        tokens = jnp.concatenate([gout[at_z[half * 8 + r]] for r in range(8)], axis=0)
         for q in range(4):
             product = matmul(tokens, rows[q], 0, 0).astype(bf16)
             for g in range(4):
@@ -172,18 +215,27 @@
         out[x, 768:784] = tail
 
 
-def over_tokens(blocks, values):
+def over_tokens(places, blocks, values, held, sems):
+    copies = [pltpu.make_async_copy(blocks.at[q], held.at[q], sems.at[q]) for q in range(4)]
+    for copy in copies:
+        copy.start()
     total = None
     for q in range(4):
-        wide = jnp.concatenate([blocks[q, 0], blocks[q, 1]], axis=1)
+        copies[q].wait()
+        halves = [
+            jnp.concatenate([held[q, places[q, h * 8 + r]] for r in range(8)], axis=0)
+            for h in range(2)
+        ]
+        wide = jnp.concatenate(halves, axis=1)
         column = lambda c: jnp.concatenate([values(h, q, c) for h in range(2)], axis=0)
         product = matmul(wide, jnp.concatenate([column(c) for c in range(3)], axis=1), 1, 0)
         total = product if total is None else total + product
     return total
 
 
-def decoder_gradient(blocks, acts, rows, pull, reach, out, total):
-    total[...] = over_tokens(blocks, lambda h, q, c: tokens_of(acts, h, q * 3 + c))
+def decoder_gradient(places, blocks, acts, rows, pull, reach, out, total, held, sems):
+    values = lambda h, q, c: tokens_of(acts, h, q * 3 + c)
+    total[...] = over_tokens(places, blocks, values, held, sems)
     for layer in range(LAYERS):
         for r in range(8):
             at = r * BLOCK + layer * 36
@@ -192,14 +244,14 @@
         out[layer] = jnp.where(reach[layer : layer + 1] > 0, whole, 0.0)
 
 
-def encoder_gradient(blocks, dpre, pick, out, sums, total):
+def encoder_gradient(places, blocks, dpre, pick, out, bias, loss, total, held, sems):
     def values(half, q, c):
         parts = [
             dpre[half * 2 + g // 2, pl.ds(((g % 2) * 4 + q) * 96 + c * 32, 32)] for g in range(4)
         ]
         return jnp.concatenate(parts, axis=0)
 
-    total[...] = over_tokens(blocks, values)
+    total[...] = over_tokens(places, blocks, values, held, sems)
     for r in range(8):
         own = jnp.zeros((36, 384), f32)
         for layer in range(LAYERS):
@@ -207,8 +259,9 @@
             own = own + jnp.where(pick[layer : layer + 1] > 0, total[at : at + 36], 0.0)
         out[r * 36 : r * 36 + 36] = own
     tail = jnp.sum(dpre[:, 768:784].astype(f32), axis=0)
-    sums[0:4] = tail[0:4] + tail[4:8] + tail[8:12]
-    sums[4:8] = jnp.zeros((4, 128), f32)
+    tail = tail[0:4] + tail[4:8] + tail[8:12]
+    bias[...] = tail[0:3]
+    loss[...] = jnp.sum(tail[3:4], axis=1, keepdims=True) / TOK_DEV
 
 
 def neighbour(block, axis):
@@ -229,6 +282,10 @@
 def on_device(resid, target, enc_weight, enc_bias, dec_weight, source):
     to = spread()
     back = [(d, s) for s, d in to]
+    places = lax.dynamic_index_in_dim(
+        jnp.array(PLACE, dtype=jnp.int32), lax.axis_index(DP), 0, False
+    )
+    at_z = lax.dynamic_index_in_dim(places, lax.axis_index(QUAD), 0, False)
     layer_ids = jnp.arange(LAYERS, dtype=jnp.int32)
     pick = source[None, :] == layer_ids[:, None]
     reach = source[None, :] <= layer_ids[:, None]
@@ -257,11 +314,11 @@
     enc_rows = jnp.pad(enc_rows, ((0, 0), (0, 0), (0, BLOCK - 108), (0, 0)))
     enc_rows = enc_rows.reshape(4, 8 * BLOCK, 384)
 
-    x_quad = share(x_block, "z", 16).reshape(2, 8 * BLOCK, 128)
+    x_quad = share(x_block, "z", 16)
     squares = jnp.pad(square_quad.reshape(12, 128), ((0, 4), (0, 0)))
-    x_quad, dec_quad = together((x_quad, dec_quad))
-    (partial,) = call(encode, x_quad, enc_rows, squares, out=[((8, 400, 128), f32)])
+    (partial,) = call(encode, at_z, x_quad, enc_rows, squares, out=[((8, 400, 128), f32)])
     partial = lax.all_to_all(partial, DP, 0, 0)
+    partial, dec_quad = together((partial, dec_quad))
     pre, norms, acts, sparsity = call(
         activate,
         partial,
@@ -270,17 +327,17 @@
     )
     acts_quad = lax.all_to_all(acts, DP, 0, 0)
 
-    (terms,) = call(decode, dec_quad, acts_quad, out=[((16, BLOCK, 128), bf16)])
+    (terms,) = call(decode, at_z, dec_quad, acts_quad, out=[((16, BLOCK, 128), bf16)])
     terms, acts_sent = together((terms, acts_quad))
     parts = lax.all_to_all(terms, "z", 0, 0)
     acts_sent = relative(acts_sent.reshape(8, 4, 96, 128).transpose(1, 0, 2, 3))
     near, far = acts_sent[:2], neighbour(acts_sent[2:], "yl")
     mine = jnp.stack([near[0], far[0]])
     other = neighbour(jnp.stack([near[1], far[1]]), "c")
+    parts, mine, other = together((parts, mine, other))
     acts_every = relative(jnp.stack([mine[0], other[0], mine[1], other[1]]))
     acts_every = acts_every.transpose(1, 0, 2, 3).reshape(8, 384, 128)
     colsum = jnp.sum(acts_every.reshape(8, 4, 3, 32, 128).astype(f32), axis=(0, 1, 3)).reshape(384)
-    parts, acts_every, colsum = together((parts, acts_every, colsum))
     recon, gout = call(
         compare,
         parts,
@@ -292,45 +349,49 @@
     gout, x_every = together((gout, x_every))
     gout_all = lax.all_to_all(gout, "z", 0, 0)
 
-    gout_every = lax.all_gather(gout_all.reshape(2, 8 * BLOCK, 128), QUAD)
+    gout_every = lax.all_gather(gout_all, QUAD)
     slopes, loss_z = call(
-        pull_back, gout_all, dec_quad, out=[((8, 384, 128), bf16), ((8, 128), f32)]
+        pull_back, at_z, gout_all, dec_quad, out=[((8, 384, 128), bf16), ((8, 128), f32)]
     )
     slopes = lax.all_to_all(slopes, DP, 0, 0)
     (sent,) = call(slopes_of, slopes, pre, norms, loss_z, out=[((8, 112, 128), bf16)])
     got = lax.all_to_all(sent, PLANE, 0, 0)
     (sent,) = call(regroup, got, out=[((4, 784, 128), bf16)])
+    recon = lax.ppermute(recon, ALL, back)
+    sent, recon = together((sent, recon))
     got = lax.all_to_all(sent, "x", 0, 0)
 
-    total = pltpu.VMEM((8 * BLOCK, 384), f32)
+    scratch = [
+        pltpu.VMEM((8 * BLOCK, 384), f32),
+        pltpu.VMEM((4, 16, BLOCK, 128), bf16),
+        pltpu.SemaphoreType.DMA((4,)),
+    ]
     member = lax.axis_index(QUAD)
     own_norms = lax.dynamic_index_in_dim(norms[:12].reshape(4, 384), member, 0, False)
     pull = ((sparsity_weight / TOK_DEV) * colsum / own_norms)[None]
     (dec_grad,) = call(
         decoder_gradient,
+        places,
         gout_every,
         acts_every,
         dec_t,
         pull,
         reach.astype(f32),
         out=[((LAYERS, 288, 384), f32)],
-        scratch=[total],
+        scratch=scratch,
     )
     got, dec_grad = together((got, dec_grad))
-    enc_grad, sums = call(
+    enc_grad, bias_grad, loss = call(
         encoder_gradient,
+        places,
         x_every,
         got,
         pick.astype(f32),
-        out=[((288, 384), f32), ((8, 128), f32)],
-        scratch=[total],
-    )
-    bias_grad = sums[:3].reshape(384)
-    loss = sums[3].sum() / TOK_DEV
-    recon = lax.ppermute(recon, ALL, back)
-    recon, enc_grad = together((recon, enc_grad))
+        out=[((288, 384), f32), ((3, 128), f32), ((1, 1), f32)],
+        scratch=scratch,
+    )
     recon = recon[:108].reshape(3, 36, 128).transpose(2, 0, 1)
-    return (loss, recon, enc_grad.T, bias_grad, dec_grad.transpose(2, 0, 1))
+    return (loss[0, 0], recon, enc_grad.T, bias_grad.reshape(384), dec_grad.transpose(2, 0, 1))
 
 
 def solution(mesh):

time: 261 us -> 262 us (level)
  blocking collectives: 83.6 us -> 49.1 us
  waiting for transfers between devices: 39.4 us -> 62.8 us
  starting transfers between devices: 81.1 us -> 91.1 us
  Pallas kernels: 12.1 us -> 18.9 us
    all_to_all x2 -> x0, blocking collectives: 36.1 us -> none  [the longest x1 19.5 us: on_device(): got = lax.all_to_all(sent, PLANE, 0, 0)]
    ppermute x2, waiting for transfers between devices: 1.33 us -> 19.1 us  [neighbour(): return lax.ppermute(block, axis, [(0, 1), (1, 0)])]
    ppermute x2, starting transfers between devices: 22.1 us -> 5.43 us  [neighbour(): return lax.ppermute(block, axis, [(0, 1), (1, 0)])]
    all_to_all x0 -> x2, starting transfers between devices: none -> 15.4 us  [the longest x1 10.6 us: on_device(): got = lax.all_to_all(sent, PLANE, 0, 0)]
    all_to_all x1, starting transfers between devices: 27.3 us -> 14.6 us  [share(): lax.all_to_all(jnp.broadcast_to(block[None], (count, *block.shape)), axes...]
    ppermute x1, starting transfers between devices: 4.94 us -> 15.5 us  [on_device(): both = lax.ppermute(both, ALL, to)]
    all_to_all x0 -> x2, waiting for transfers between devices: none -> 9 us  [the longest x1 9 us: on_device(): got = lax.all_to_all(sent, PLANE, 0, 0)]
    pallas_call x9, Pallas kernels: 12.1 us -> 18.9 us  [call(): pl.pallas_call(kernel, in_specs=[place(arg) for arg in args], out_shape=[...]
  transfers between devices with their start and end apart: 12 -> 14, of which waited for: 7 -> 7; matrix products, arithmetic and copies ran while one was open for 4% -> 4% of each run, Pallas kernels for 4% -> 6%
where the time goes in v6:
time: 262 us; the launch traced here: 260 us
  starting transfers between devices  91.1 us (35%)
  waiting for transfers between devices  62.8 us (24%)
  blocking collectives  49.1 us (19%)
  Pallas kernels  18.9 us (7%)
  local copies, waits for them, and re-layouts  17.1 us (7%)
  between operations  14.3 us (5%)
  other arithmetic  6.77 us (3%)
    all_to_all x1, blocking collectives, on_device(): gout_all = lax.all_to_all(gout, 'z', 0, 0)  32.6 us
    all_to_all x1, waiting for transfers between devices, on_device(): partial = lax.all_to_all(partial, DP, 0, 0)  19.8 us
    ppermute x2, waiting for transfers between devices, neighbour(): return lax.ppermute(block, axis, [(0, 1), (1, 0)])  19.1 us
    pallas_call x9, Pallas kernels, call(): pl.pallas_call(kernel, in_specs=[place(arg) for arg in args], out_shape=[...  18.9 us
    all_gather x1, blocking collectives, on_device(): enc_quad = lax.all_gather(enc_own, QUAD)  16.5 us
    ppermute x1, starting transfers between devices, on_device(): both = lax.ppermute(both, ALL, to)  15.5 us
    all_to_all x1, starting transfers between devices, on_device(): parts = lax.all_to_all(terms, 'z', 0, 0)  14.7 us
    all_to_all x1, starting transfers between devices, share(): lax.all_to_all(jnp.broadcast_to(block[None], (count, *block.shape)), axes...  14.6 us
  transfers between devices with their start and end apart: 14, of which 7 were waited for; matrix products, arithmetic and copies ran while one was open for 4% of the time, Pallas kernels for 6%

profile of v6, /device:TPU:1, one launch (start us, length us, event | category | flops | bytes accessed | tf_op | source)
XLA Modules:
  0.0 260.2 jit_solution(17191134862995052633)
XLA Ops:
  7.2 1.3 fusion.6
  8.5 1.3 multiply_reduce_fusion
  9.8 0.1 reshape.126
  10.1 0.1 copy.51
  10.2 0.5 copy-done.11
  10.7 0.9 pad.24.clone
  11.8 15.5 %collective-permute-start = (bf16[2,112,128]{2,1,0:T(8,128)(2,1)S(1)}, bf16[2,112,128]{2,1,0:T(8,128)(2,1)S(1)}, u32[]{:S(2)}, u32[]{:S(2)}) collective-permute-start(bf16[2,112,128]{2,1,0:T(8,128)(2,1)S(1)} %pad.20), channel_id=1, source_target_pairs={{0,36},{1,44},{2,20},{3,52},{4,40},{5,32},{6,28},{7,24},{320,60},{... | collective-permute-start | bytes 172040 | tf_op jit(solution)/shard_map/ppermute | solution.py:295
  27.4 1.1 collective-permute-done
  28.5 0.6 slice_bitcast_fusion
  29.1 0.8 broadcast_in_dim.56
  30.0 14.6 %all-to-all-start = ((bf16[16,112,128]{2,1,0:T(8,128)(2,1)}), bf16[16,112,128]{2,1,0:T(8,128)(2,1)S(1)}, u32[]{:S(2)}, u32[]{:S(2)}) async-start(bf16[16,112,128]{2,1,0:T(8,128)(2,1)} %broadcast_in_dim.56), calls=%async_computation | async-start | bytes 917504 | tf_op jit(solution)/shard_map/all_to_all | solution.py:76
  44.7 16.5 %all-gather = bf16[1216,384]{1,0:T(8,128)(2,1)S(1)} all-gather(bf16[304,384]{1,0:T(8,128)(2,1)S(1)} %fusion.1), channel_id=2, replica_groups=mesh['x'=4,'yh'=2,'z'=16,'yl'=2,'c'=2] {'yl','c'}, dimensions={0}, use_global_device_ids=true | all-gather | bytes 1167360 | tf_op jit(solution)/shard_map/all_gather | solution.py:305
  61.2 0.1 slice.138
  61.3 0.5 copy.49
  61.8 0.2 copy.44
  62.1 0.1 broadcast_in_dim.59
  62.3 0.2 broadcast_in_dim.63
  62.5 0.8 broadcast_select_fusion
  63.4 0.4 copy.50
  63.7 0.3 pad.22.clone
  64.1 0.7 fusion.5.at_z
  64.8 1.8 shard_map.110
  66.6 1.2 copy-done.3
  67.8 7.3 %all-to-all-start.1 = ((f32[8,400,128]{2,1,0:T(8,128)}), f32[8,400,128]{2,1,0:T(8,128)S(1)}, u32[]{:S(2)}, u32[]{:S(2)}) async-start(f32[8,400,128]{2,1,0:T(8,128)} %copy-done.3), calls=%async_computation.1 | async-start | bytes 3276800 | tf_op jit(solution)/shard_map/all_to_all | solution.py:320
  75.1 19.8 %all-to-all-done.1.parts = f32[8,400,128]{2,1,0:T(8,128)S(1)} async-done(((f32[8,400,128]{2,1,0:T(8,128)}), f32[8,400,128]{2,1,0:T(8,128)S(1)}, u32[]{:S(2)}, u32[]{:S(2)}) %all-to-all-start.1) | async-done | bytes 1638432 | tf_op jit(solution)/shard_map/all_to_all | solution.py:320
  94.9 1.2 copy-done.1
  96.1 1.4 copy-done.2
  97.5 0.1 shard_map.111
  97.6 0.9 copy-done.7
  98.5 0.7 copy-done.8
  99.2 5.4 %all-to-all-start.2 = ((bf16[8,384,128]{2,1,0:T(8,128)(2,1)}), bf16[8,384,128]{2,1,0:T(8,128)(2,1)S(1)}, u32[]{:S(2)}, u32[]{:S(2)}) async-start(bf16[8,384,128]{2,1,0:T(8,128)(2,1)} %copy-done.7), calls=%async_computation.2 | async-start | bytes 1572864 | tf_op jit(solution)/shard_map/all_to_all | solution.py:328
  104.6 0.7 all-gather.9.cloned.1.call-update
  105.3 9.1 %all-to-all-done.2.acts = bf16[8,384,128]{2,1,0:T(8,128)(2,1)S(1)} async-done(((bf16[8,384,128]{2,1,0:T(8,128)(2,1)}), bf16[8,384,128]{2,1,0:T(8,128)(2,1)S(1)}, u32[]{:S(2)}, u32[]{:S(2)}) %all-to-all-start.2) | async-done | bytes 786464 | tf_op jit(solution)/shard_map/all_to_all | solution.py:328
  114.4 2.1 shard_map.112
  116.6 0.8 copy-done.6
  117.4 14.7 %all-to-all-start.3 = ((bf16[16,112,128]{2,1,0:T(8,128)(2,1)}), bf16[16,112,128]{2,1,0:T(8,128)(2,1)}, u32[]{:S(2)}, u32[]{:S(2)}) async-start(bf16[16,112,128]{2,1,0:T(8,128)(2,1)} %copy-done.6), calls=%async_computation.3 | async-start | bytes 917504 | tf_op jit(solution)/shard_map/all_to_all | solution.py:332
  132.2 0.1 maximum_select_fusion
  132.4 0.2 maximum_select_fusion.1
  132.6 1.9 collective-permute-start.1
  134.5 18.5 %collective-permute-done.1 = bf16[2,8,96,128]{3,2,0,1:T(8,128)(2,1)S(1)} collective-permute-done((bf16[2,8,96,128]{3,2,0,1:T(8,128)(2,1)S(1)}, bf16[2,8,96,128]{3,2,0,1:T(8,128)(2,1)S(1)}, u32[]{:S(2)}, u32[]{:S(2)}) %collective-permute-start.1) | collective-permute-done | bytes 393248 | tf_op jit(solution)/shard_map/ppermute | solution.py:268
  153.1 3.5 %collective-permute-start.2 = (bf16[2,8,96,128]{3,2,0,1:T(8,128)(2,1)S(1)}, bf16[2,8,96,128]{3,2,0,1:T(8,128)(2,1)}, u32[]{:S(2)}, u32[]{:S(2)}) collective-permute-start(bf16[2,8,96,128]{3,2,0,1:T(8,128)(2,1)S(1)} %pad_maximum_fusion.1), channel_id=1, source_target_pairs={{0,1},{1,0},{2,3},{3,2},{4,5},{5,4},{6,7},{7,6},{8,9},{9,8},{10,11... | collective-permute-start | bytes 1179656 | tf_op jit(solution)/shard_map/ppermute | solution.py:268
  156.6 0.8 pad_maximum_fusion
  157.4 0.7 collective-permute-done.2
  158.0 1.1 shard_map.113
  159.2 32.6 %all_to_all.40.gout = bf16[16,112,128]{2,1,0:T(8,128)(2,1)} all-to-all(bf16[16,112,128]{2,1,0:T(8,128)(2,1)S(1)} %get-tuple-element.38), channel_id=1, replica_groups=mesh['x'=4,'yh'=2,'z'=16,'yl'=2,'c'=2] {'z'}, dimensions={0} | all-to-all | bytes 917504 | tf_op jit(solution)/shard_map/all_to_all | solution.py:350
  191.8 1.0 copy-done.5
  192.8 2.7 %shard_map.114 = (bf16[8,384,128]{2,1,0:T(8,128)(2,1)}, f32[8,128]{1,0:T(8,128)S(1)}) custom-call(s32[16]{0:T(128)S(1)} %fusion.5.at_z, bf16[16,112,128]{2,1,0:T(8,128)(2,1)S(1)} %copy-done.5, bf16[4,896,384]{2,1,0:T(8,128)(2,1)S(1)} %copy-done), custom_call_target="tpu_custom_call" | custom-call | tf_op jit(solution)/shard_map/pallas_call | solution.py:87
  195.5 4.8 %all-to-all-start.5 = ((bf16[8,384,128]{2,1,0:T(8,128)(2,1)}), bf16[8,384,128]{2,1,0:T(8,128)(2,1)S(1)}, u32[]{:S(2)}, u32[]{:S(2)}) async-start(bf16[8,384,128]{2,1,0:T(8,128)(2,1)} %get-tuple-element.39), calls=%async_computation.5 | async-start | bytes 1572864 | tf_op jit(solution)/shard_map/all_to_all | solution.py:356
  200.4 1.3 dynamic-slice_bitcast_fusion.places
  201.7 8.3 %collective-permute-start.3 = (bf16[112,128]{1,0:T(8,128)(2,1)S(1)}, bf16[112,128]{1,0:T(8,128)(2,1)S(1)}, u32[]{:S(2)}, u32[]{:S(2)}) collective-permute-start(bf16[112,128]{1,0:T(8,128)(2,1)S(1)} %get-tuple-element.43), channel_id=1, source_target_pairs={{36,0},{44,1},{20,2},{52,3},{40,4},{32,5},{28,6},{24,7},{60,320},{... | collective-permute-start | bytes 86024 | tf_op jit(solution)/shard_map/ppermute | solution.py:360
  210.0 1.1 fusion.11
  211.1 0.2 maximum_select_fusion.2
  211.3 0.9 shard_map.115
  212.2 10.6 %all-to-all-start.6 = ((bf16[8,112,128]{2,1,0:T(8,128)(2,1)}), bf16[8,112,128]{2,1,0:T(8,128)(2,1)S(1)}, u32[]{:S(2)}, u32[]{:S(2)}) async-start(bf16[8,112,128]{2,1,0:T(8,128)(2,1)} %shard_map.115), calls=%async_computation.6 | async-start | bytes 458752 | tf_op jit(solution)/shard_map/all_to_all | solution.py:358
  222.8 9.0 %all-to-all-done.6.got = bf16[8,112,128]{2,1,0:T(8,128)(2,1)S(1)} async-done(((bf16[8,112,128]{2,1,0:T(8,128)(2,1)}), bf16[8,112,128]{2,1,0:T(8,128)(2,1)S(1)}, u32[]{:S(2)}, u32[]{:S(2)}) %all-to-all-start.6) | async-done | bytes 229408 | tf_op jit(solution)/shard_map/all_to_all | solution.py:358
  231.8 1.0 shard_map.116
  232.8 4.4 %all-to-all-start.7 = ((bf16[4,784,128]{2,1,0:T(8,128)(2,1)}), bf16[4,784,128]{2,1,0:T(8,128)(2,1)S(1)}, u32[]{:S(2)}, u32[]{:S(2)}) async-start(bf16[4,784,128]{2,1,0:T(8,128)(2,1)} %shard_map.116), calls=%async_computation.7 | async-start | bytes 1605632 | tf_op jit(solution)/shard_map/all_to_all | solution.py:362
  237.2 1.3 convert_reduce_fusion
  238.5 0.6 bitcast_divide_fusion.pull
  239.1 0.6 reshape.131
  239.7 4.9 %shard_map.117 = f32[3,288,384]{2,1,0:T(8,128)} custom-call(s32[4,16]{1,0:T(4,128)} %dynamic-slice_bitcast_fusion.places, bf16[4,16,112,128]{3,2,1,0:T(8,128)(2,1)} %bitcast.66, bf16[8,384,128]{2,1,0:T(8,128)(2,1)} %bitcast.61, bf16[3,288,384]{2,1,0:T(8,128)(2,1)} %copy-done.11, f32[1,384]{1,0:T(1,128)} %bitcast_divide_fusion.pull, ...), custom_call_target="tpu_custom_call" | custom-call | tf_op jit(solution)/shard_map/pallas_call | solution.py:87
  244.6 3.9 %all-to-all-done.7.dpre = bf16[4,784,128]{2,1,0:T(8,128)(2,1)S(1)} async-done(((bf16[4,784,128]{2,1,0:T(8,128)(2,1)}), bf16[4,784,128]{2,1,0:T(8,128)(2,1)S(1)}, u32[]{:S(2)}, u32[]{:S(2)}) %all-to-all-start.7) | async-done | bytes 802848 | tf_op jit(solution)/shard_map/all_to_all | solution.py:362
  248.5 0.9 copy-done.12
  249.4 4.3 %shard_map.118 = (f32[288,384]{1,0:T(8,128)}, f32[3,128]{1,0:T(4,128)}, f32[1,1]{1,0:T(1,128)}) custom-call(s32[4,16]{1,0:T(4,128)} %dynamic-slice_bitcast_fusion.places, bf16[4,16,112,128]{3,2,1,0:T(8,128)(2,1)} %bitcast.65, bf16[4,784,128]{2,1,0:T(8,128)(2,1)} %copy-done.12, f32[3,384]{1,0:T(4,128)} %get-tuple-element.82.pick), custom_call_target="tpu_custom_call" | custom-call | tf_op jit(solution)/shard_map/pallas_call | solution.py:87
  (74 shorter events, 1.1 us)
Async XLA Ops:
  7.2 88.9 %all-gather.7.cloned.1.call-start = ((), (), s32[]{:S(2)}) async-start(), calls=%async_computation.8 | async-start | bytes 3440640 | tf_op jit(solution)/shard_map/all_gather | solution.py:306
  9.8 0.9 copy-start.11
  10.1 1.6 copy-start.15
  10.1 1.6 copy-start.16
  10.1 17.2 %copy-start.17 = (s32[384]{0:T(512)S(1)}, s32[384]{0:T(512)}, u32[]{:S(2)}) copy-start(s32[384]{0:T(512)} %param.12) | copy-start | bytes 4612
  10.1 17.2 %copy-start.18 = (f32[384]{0:T(512)S(1)}, f32[384]{0:T(512)}, u32[]{:S(2)}) copy-start(f32[384]{0:T(512)} %param.10) | copy-start | bytes 4612
  10.7 33.9 %copy-start.14 = (bf16[384,288]{0,1:T(8,128)(2,1)S(1)}, bf16[384,288]{0,1:T(8,128)(2,1)}, u32[]{:S(2)}) copy-start(bf16[384,288]{0,1:T(8,128)(2,1)} %param.9) | copy-start | bytes 663556
  11.8 16.7 %collective-permute-start = (bf16[2,112,128]{2,1,0:T(8,128)(2,1)S(1)}, bf16[2,112,128]{2,1,0:T(8,128)(2,1)S(1)}, u32[]{:S(2)}, u32[]{:S(2)}) collective-permute-start(bf16[2,112,128]{2,1,0:T(8,128)(2,1)S(1)} %pad.20), channel_id=1, source_target_pairs={{0,36},{1,44},{2,20},{3,52},{4,40},{5,32},{6,28},{7,24},{320,60},{... | collective-permute-start | bytes 172040 | tf_op jit(solution)/shard_map/ppermute | solution.py:295
  30.0 34.8 %all-to-all-start = ((bf16[16,112,128]{2,1,0:T(8,128)(2,1)}), bf16[16,112,128]{2,1,0:T(8,128)(2,1)S(1)}, u32[]{:S(2)}, u32[]{:S(2)}) async-start(bf16[16,112,128]{2,1,0:T(8,128)(2,1)} %broadcast_in_dim.56), calls=%async_computation | async-start | bytes 917504 | tf_op jit(solution)/shard_map/all_to_all | solution.py:76
  64.8 1.8 copy-start.4
  66.6 1.2 copy-start.3
  67.8 27.1 %all-to-all-start.1 = ((f32[8,400,128]{2,1,0:T(8,128)}), f32[8,400,128]{2,1,0:T(8,128)S(1)}, u32[]{:S(2)}, u32[]{:S(2)}) async-start(f32[8,400,128]{2,1,0:T(8,128)} %copy-done.3), calls=%async_computation.1 | async-start | bytes 3276800 | tf_op jit(solution)/shard_map/all_to_all | solution.py:320
  94.9 1.2 copy-start.1
  96.1 1.4 copy-start.2
  97.5 16.9 %copy-start = (bf16[4,896,384]{2,1,0:T(8,128)(2,1)S(1)}, bf16[4,896,384]{2,1,0:T(8,128)(2,1)}, u32[]{:S(2)}) copy-start(bf16[4,896,384]{2,1,0:T(8,128)(2,1)} %all-gather.7.cloned.1.call-done.rows) | copy-start | bytes 8257540
  97.6 0.9 copy-start.7
  98.5 0.7 copy-start.8
  99.2 15.2 %all-to-all-start.2 = ((bf16[8,384,128]{2,1,0:T(8,128)(2,1)}), bf16[8,384,128]{2,1,0:T(8,128)(2,1)S(1)}, u32[]{:S(2)}, u32[]{:S(2)}) async-start(bf16[8,384,128]{2,1,0:T(8,128)(2,1)} %copy-done.7), calls=%async_computation.2 | async-start | bytes 1572864 | tf_op jit(solution)/shard_map/all_to_all | solution.py:328
  104.5 54.6 %all-gather.9.cloned.1.call-start = ((), (), s32[]{:S(2)}) async-start(), calls=%async_computation.9 | async-start | bytes 2293760 | tf_op jit(solution)/shard_map/all_gather | solution.py:348
  116.6 0.8 copy-start.6
  117.4 40.7 %all-to-all-start.3 = ((bf16[16,112,128]{2,1,0:T(8,128)(2,1)}), bf16[16,112,128]{2,1,0:T(8,128)(2,1)}, u32[]{:S(2)}, u32[]{:S(2)}) async-start(bf16[16,112,128]{2,1,0:T(8,128)(2,1)} %copy-done.6), calls=%async_computation.3 | async-start | bytes 917504 | tf_op jit(solution)/shard_map/all_to_all | solution.py:332
  132.1 107.6 %all-gather.11.cloned.1.call-start = ((), (), s32[]{:S(2)}) async-start(), calls=%async_computation.10 | async-start | bytes 2293760 | tf_op jit(solution)/shard_map/all_gather | solution.py:352
  132.5 25.5 %copy-start.10 = (bf16[112,128]{1,0:T(8,128)(2,1)S(1)}, bf16[112,128]{1,0:T(8,128)(2,1)}, u32[]{:S(2)}) copy-start(bf16[112,128]{1,0:T(8,128)(2,1)} %get-tuple-element.77.target) | copy-start | bytes 86020
  132.6 20.4 %collective-permute-start.1 = (bf16[2,8,96,128]{3,2,0,1:T(8,128)(2,1)S(1)}, bf16[2,8,96,128]{3,2,0,1:T(8,128)(2,1)S(1)}, u32[]{:S(2)}, u32[]{:S(2)}) collective-permute-start(bf16[2,8,96,128]{3,2,0,1:T(8,128)(2,1)S(1)} %slice.152), channel_id=1, source_target_pairs={{0,2},{2,0},{1,3},{3,1},{4,6},{6,4},{5,7},{7,5},{8,10},{10,8},{9,1... | collective-permute-start | bytes 1179656 | tf_op jit(solution)/shard_map/ppermute | solution.py:268
  153.1 5.0 %collective-permute-start.2 = (bf16[2,8,96,128]{3,2,0,1:T(8,128)(2,1)S(1)}, bf16[2,8,96,128]{3,2,0,1:T(8,128)(2,1)}, u32[]{:S(2)}, u32[]{:S(2)}) collective-permute-start(bf16[2,8,96,128]{3,2,0,1:T(8,128)(2,1)S(1)} %pad_maximum_fusion.1), channel_id=1, source_target_pairs={{0,1},{1,0},{2,3},{3,2},{4,5},{5,4},{6,7},{7,6},{8,9},{9,8},{10,11... | collective-permute-start | bytes 1179656 | tf_op jit(solution)/shard_map/ppermute | solution.py:268
  191.8 1.0 copy-start.5
  195.5 14.5 %copy-start.13 = (bf16[2,8,96,128]{3,2,0,1:T(8,128)(2,1)S(1)}, bf16[2,8,96,128]{3,2,0,1:T(8,128)(2,1)}, u32[]{:S(2)}) copy-start(bf16[2,8,96,128]{3,2,0,1:T(8,128)(2,1)} %pad_maximum_fusion) | copy-start | bytes 1179652
  195.5 15.7 %all-to-all-start.5 = ((bf16[8,384,128]{2,1,0:T(8,128)(2,1)}), bf16[8,384,128]{2,1,0:T(8,128)(2,1)S(1)}, u32[]{:S(2)}, u32[]{:S(2)}) async-start(bf16[8,384,128]{2,1,0:T(8,128)(2,1)} %get-tuple-element.39), calls=%async_computation.5 | async-start | bytes 1572864 | tf_op jit(solution)/shard_map/all_to_all | solution.py:356
  200.4 10.9 %copy-start.9 = (f32[384,128]{1,0:T(8,128)S(1)}, f32[384,128]{1,0:T(8,128)}, u32[]{:S(2)}) copy-start(f32[384,128]{1,0:T(8,128)} %copy-done.8) | copy-start | bytes 589828
  201.7 31.1 %collective-permute-start.3 = (bf16[112,128]{1,0:T(8,128)(2,1)S(1)}, bf16[112,128]{1,0:T(8,128)(2,1)S(1)}, u32[]{:S(2)}, u32[]{:S(2)}) collective-permute-start(bf16[112,128]{1,0:T(8,128)(2,1)S(1)} %get-tuple-element.43), channel_id=1, source_target_pairs={{36,0},{44,1},{20,2},{52,3},{40,4},{32,5},{28,6},{24,7},{60,320},{... | collective-permute-start | bytes 86024 | tf_op jit(solution)/shard_map/ppermute | solution.py:360
  212.2 19.6 %all-to-all-start.6 = ((bf16[8,112,128]{2,1,0:T(8,128)(2,1)}), bf16[8,112,128]{2,1,0:T(8,128)(2,1)S(1)}, u32[]{:S(2)}, u32[]{:S(2)}) async-start(bf16[8,112,128]{2,1,0:T(8,128)(2,1)} %shard_map.115), calls=%async_computation.6 | async-start | bytes 458752 | tf_op jit(solution)/shard_map/all_to_all | solution.py:358
  232.8 15.7 %all-to-all-start.7 = ((bf16[4,784,128]{2,1,0:T(8,128)(2,1)}), bf16[4,784,128]{2,1,0:T(8,128)(2,1)S(1)}, u32[]{:S(2)}, u32[]{:S(2)}) async-start(bf16[4,784,128]{2,1,0:T(8,128)(2,1)} %shard_map.116), calls=%async_computation.7 | async-start | bytes 1605632 | tf_op jit(solution)/shard_map/all_to_all | solution.py:362
  248.5 0.9 copy-start.12
Sparse Core Ops, SparseCore 0:
  11.8 53.1 all-gather.6
  107.5 46.3 all-gather.8
  191.9 39.0 all-gather.10

commit v7 on v6

--- a/solution.py
+++ b/solution.py
@@ -76,21 +76,44 @@
     return lax.all_to_all(jnp.broadcast_to(block[None], (count, *block.shape)), axes, 0, 0)
 
 
-def call(kernel, *args, out, scratch=()):
-    def place(arg):
+def call(kernel, *args, out, far=(), scratch=()):
+    def place(k, arg):
         if arg.dtype == jnp.int32:
             return pl.BlockSpec(memory_space=pltpu.SMEM)
-        if arg.shape == (4, 16, BLOCK, 128):
-            return pl.BlockSpec(memory_space=pl.ANY)
-        return pl.BlockSpec(memory_space=pltpu.VMEM)
+        return pl.BlockSpec(memory_space=pl.ANY if k in far else pltpu.VMEM)
 
     return pl.pallas_call(
         kernel,
-        in_specs=[place(arg) for arg in args],
+        in_specs=[place(k, arg) for k, arg in enumerate(args)],
         out_shape=[jax.ShapeDtypeStruct(shape, dtype) for shape, dtype in out],
         scratch_shapes=scratch,
-        compiler_params=pltpu.CompilerParams(vmem_limit_bytes=(58 if scratch else 40) * 2**20),
+        compiler_params=pltpu.CompilerParams(vmem_limit_bytes=(56 if scratch else 40) * 2**20),
     )(*args)
+
+
+ORDERED = [pltpu.VMEM((16 * BLOCK, 128), bf16), pltpu.SemaphoreType.DMA((16,))]
+ROWS = [pltpu.VMEM((4, 8 * BLOCK, 384), bf16), pltpu.SemaphoreType.DMA((4,))]
+EVERY = [
+    pltpu.VMEM((8 * BLOCK, 384), f32),
+    pltpu.VMEM((4, 16 * BLOCK, 128), bf16),
+    pltpu.SemaphoreType.DMA((4, 16)),
+]
+
+
+def in_order(at_z, blocks, held, sems):
+    copies = []
+    for k in range(16):
+        part = held.at[pl.ds(k * BLOCK, BLOCK)]
+        copies.append(pltpu.make_async_copy(blocks.at[at_z(k)], part, sems.at[k]))
+        copies[-1].start()
+    return copies
+
+
+def in_parts(rows, held, sems):
+    copies = [pltpu.make_async_copy(rows.at[q], held.at[q], sems.at[q]) for q in range(4)]
+    for copy in copies:
+        copy.start()
+    return copies
 
 
 def split(value):
@@ -104,9 +127,12 @@
     return lax.dot_general(a, b, (((left,), (right,)), ((), ())), preferred_element_type=f32)
 
 
-def encode(at_z, x, rows, squares, out):
+def encode(at_z, x, rows, squares, out, held, sems):
+    copies = in_order(lambda k: at_z[k], x, held, sems)
     for half in range(2):
-        tokens = jnp.concatenate([x[at_z[half * 8 + r]] for r in range(8)], axis=0)
+        for copy in copies[half * 8 : half * 8 + 8]:
+            copy.wait()
+        tokens = held[half * 8 * BLOCK : (half + 1) * 8 * BLOCK]
         for q in range(4):
             product = matmul(tokens, rows[q], 0, 0)
             for g in range(4):
@@ -139,14 +165,17 @@
     return ref[half * 4 : half * 4 + 4, column * 32 : column * 32 + 32].reshape(128, 128)
 
 
-def decode(at_z, rows, acts, out):
-    for half in range(2):
-        total = None
-        for q in range(4):
+def decode(at_z, far_rows, acts, out, rows, sems):
+    copies = in_parts(far_rows, rows, sems)
+    totals = [None, None]
+    for q in range(4):
+        copies[q].wait()
+        for half in range(2):
             wide = jnp.concatenate([tokens_of(acts, half, q * 3 + c) for c in range(3)], axis=1)
             product = matmul(rows[q], wide, 1, 1)
-            total = product if total is None else total + product
-        low = total.astype(bf16)
+            totals[half] = product if q == 0 else totals[half] + product
+    for half in range(2):
+        low = totals[half].astype(bf16)
         for r in range(8):
             out[at_z[half * 8 + r]] = low[r * BLOCK : (r + 1) * BLOCK]
 
@@ -165,12 +194,19 @@
         gout[z] = low
 
 
-def pull_back(at_z, gout, rows, out, loss):
-    total = jnp.sum(gout[:, 96:112].astype(f32), axis=0)
+def pull_back(at_z, gout, far_rows, out, loss, held, sems, rows, row_sems):
+    copies = in_order(lambda k: at_z[k], gout, held, sems)
+    row_copies = in_parts(far_rows, rows, row_sems)
+    for copy in copies:
+        copy.wait()
+    total = jnp.zeros((16, 128), f32)
+    for k in range(16):
+        total = total + held[k * BLOCK + 96 : k * BLOCK + 112].astype(f32)
     loss[...] = jnp.broadcast_to(jnp.sum(total[12:15], axis=0, keepdims=True), (8, 128))
-    for half in range(2):
-        tokens = jnp.concatenate([gout[at_z[half * 8 + r]] for r in range(8)], axis=0)
-        for q in range(4):
+    for q in range(4):
+        row_copies[q].wait()
+        for half in range(2):
+            tokens = held[half * 8 * BLOCK : (half + 1) * 8 * BLOCK]
             product = matmul(tokens, rows[q], 0, 0).astype(bf16)
             for g in range(4):
                 for c in range(3):
@@ -216,17 +252,14 @@
 
 
 def over_tokens(places, blocks, values, held, sems):
-    copies = [pltpu.make_async_copy(blocks.at[q], held.at[q], sems.at[q]) for q in range(4)]
-    for copy in copies:
-        copy.start()
+    copies = [
+        in_order(lambda k: places[q, k], blocks.at[q], held.at[q], sems.at[q]) for q in range(4)
+    ]
     total = None
     for q in range(4):
-        copies[q].wait()
-        halves = [
-            jnp.concatenate([held[q, places[q, h * 8 + r]] for r in range(8)], axis=0)
-            for h in range(2)
-        ]
-        wide = jnp.concatenate(halves, axis=1)
+        for copy in copies[q]:
+            copy.wait()
+        wide = jnp.concatenate([held[q, : 8 * BLOCK], held[q, 8 * BLOCK :]], axis=1)
         column = lambda c: jnp.concatenate([values(h, q, c) for h in range(2)], axis=0)
         product = matmul(wide, jnp.concatenate([column(c) for c in range(3)], axis=1), 1, 0)
         total = product if total is None else total + product
@@ -316,9 +349,17 @@
 
     x_quad = share(x_block, "z", 16)
     squares = jnp.pad(square_quad.reshape(12, 128), ((0, 4), (0, 0)))
-    (partial,) = call(encode, at_z, x_quad, enc_rows, squares, out=[((8, 400, 128), f32)])
+    (partial,) = call(
+        encode,
+        at_z,
+        x_quad,
+        enc_rows,
+        squares,
+        out=[((8, 400, 128), f32)],
+        far=(1,),
+        scratch=ORDERED,
+    )
     partial = lax.all_to_all(partial, DP, 0, 0)
-    partial, dec_quad = together((partial, dec_quad))
     pre, norms, acts, sparsity = call(
         activate,
         partial,
@@ -327,14 +368,22 @@
     )
     acts_quad = lax.all_to_all(acts, DP, 0, 0)
 
-    (terms,) = call(decode, at_z, dec_quad, acts_quad, out=[((16, BLOCK, 128), bf16)])
+    (terms,) = call(
+        decode,
+        at_z,
+        dec_quad,
+        acts_quad,
+        out=[((16, BLOCK, 128), bf16)],
+        far=(1,),
+        scratch=ROWS,
+    )
     terms, acts_sent = together((terms, acts_quad))
     parts = lax.all_to_all(terms, "z", 0, 0)
     acts_sent = relative(acts_sent.reshape(8, 4, 96, 128).transpose(1, 0, 2, 3))
     near, far = acts_sent[:2], neighbour(acts_sent[2:], "yl")
     mine = jnp.stack([near[0], far[0]])
     other = neighbour(jnp.stack([near[1], far[1]]), "c")
-    parts, mine, other = together((parts, mine, other))
+    parts, mine, other, x_sent = together((parts, mine, other, x_quad))
     acts_every = relative(jnp.stack([mine[0], other[0], mine[1], other[1]]))
     acts_every = acts_every.transpose(1, 0, 2, 3).reshape(8, 384, 128)
     colsum = jnp.sum(acts_every.reshape(8, 4, 3, 32, 128).astype(f32), axis=(0, 1, 3)).reshape(384)
@@ -345,13 +394,19 @@
         sparsity,
         out=[((BLOCK, 128), bf16), ((16, BLOCK, 128), bf16)],
     )
-    x_every = lax.all_gather(x_quad, QUAD)
-    gout, x_every = together((gout, x_every))
+    x_every = lax.all_gather(x_sent, QUAD)
     gout_all = lax.all_to_all(gout, "z", 0, 0)
 
-    gout_every = lax.all_gather(gout_all, QUAD)
+    gout_sent, x_every = together((gout_all, x_every))
+    gout_every = lax.all_gather(gout_sent, QUAD)
     slopes, loss_z = call(
-        pull_back, at_z, gout_all, dec_quad, out=[((8, 384, 128), bf16), ((8, 128), f32)]
+        pull_back,
+        at_z,
+        gout_all,
+        dec_quad,
+        out=[((8, 384, 128), bf16), ((8, 128), f32)],
+        far=(1, 2),
+        scratch=ORDERED + ROWS,
     )
     slopes = lax.all_to_all(slopes, DP, 0, 0)
     (sent,) = call(slopes_of, slopes, pre, norms, loss_z, out=[((8, 112, 128), bf16)])
@@ -361,11 +416,6 @@
     sent, recon = together((sent, recon))
     got = lax.all_to_all(sent, "x", 0, 0)
 
-    scratch = [
-        pltpu.VMEM((8 * BLOCK, 384), f32),
-        pltpu.VMEM((4, 16, BLOCK, 128), bf16),
-        pltpu.SemaphoreType.DMA((4,)),
-    ]
     member = lax.axis_index(QUAD)
     own_norms = lax.dynamic_index_in_dim(norms[:12].reshape(4, 384), member, 0, False)
     pull = ((sparsity_weight / TOK_DEV) * colsum / own_norms)[None]
@@ -378,7 +428,8 @@
         pull,
         reach.astype(f32),
         out=[((LAYERS, 288, 384), f32)],
-        scratch=scratch,
+        far=(1,),
+        scratch=EVERY,
     )
     got, dec_grad = together((got, dec_grad))
     enc_grad, bias_grad, loss = call(
@@ -388,7 +439,8 @@
         got,
         pick.astype(f32),
         out=[((288, 384), f32), ((3, 128), f32), ((1, 1), f32)],
-        scratch=scratch,
+        far=(1,),
+        scratch=EVERY,
     )
     recon = recon[:108].reshape(3, 36, 128).transpose(2, 0, 1)
     return (loss[0, 0], recon, enc_grad.T, bias_grad.reshape(384), dec_grad.transpose(2, 0, 1))

time: 262 us -> 264 us (level)
  Pallas kernels: 18.9 us -> 29.3 us
  waiting for transfers between devices: 62.8 us -> 58.7 us
  local copies, waits for them, and re-layouts: 17.1 us -> 13.9 us
    pallas_call x9, Pallas kernels: 18.9 us -> 29.3 us  [call(): pl.pallas_call(kernel, in_specs=[place(k, arg) for k, arg in enumerate(ar...]
    ppermute x2, waiting for transfers between devices: 19.1 us -> 10 us  [neighbour(): return lax.ppermute(block, axis, [(0, 1), (1, 0)])]
    unnamed x41 -> x25, local copies, waits for them, and re-layouts: 9.48 us -> 4.05 us
    all_to_all x1, starting transfers between devices: 14.7 us -> 17.7 us  [on_device(): parts = lax.all_to_all(terms, 'z', 0, 0)]
    all_to_all x1, waiting for transfers between devices: 0.01 us -> 2.65 us  [on_device(): slopes = lax.all_to_all(slopes, DP, 0, 0)]
  transfers between devices with their start and end apart: 14 -> 14, of which waited for: 7 -> 10; matrix products, arithmetic and copies ran while one was open for 4% -> 5% of each run, Pallas kernels for 6% -> 7%
where the time goes in v7:
time: 264 us; the launch traced here: 262 us
  starting transfers between devices  89.4 us (34%)
  waiting for transfers between devices  58.7 us (22%)
  blocking collectives  50.3 us (19%)
  Pallas kernels  29.3 us (11%)
  between operations  14.2 us (5%)
  local copies, waits for them, and re-layouts  13.9 us (5%)
  other arithmetic  5.97 us (2%)
    all_to_all x1, blocking collectives, on_device(): gout_all = lax.all_to_all(gout, 'z', 0, 0)  33.8 us
    pallas_call x9, Pallas kernels, call(): pl.pallas_call(kernel, in_specs=[place(k, arg) for k, arg in enumerate(ar...  29.3 us
    all_to_all x1, waiting for transfers between devices, on_device(): partial = lax.all_to_all(partial, DP, 0, 0)  20.1 us
    all_to_all x1, starting transfers between devices, on_device(): parts = lax.all_to_all(terms, 'z', 0, 0)  17.7 us
    all_gather x1, blocking collectives, on_device(): enc_quad = lax.all_gather(enc_own, QUAD)  16.5 us
    ppermute x1, starting transfers between devices, on_device(): both = lax.ppermute(both, ALL, to)  15.5 us
    all_to_all x1, starting transfers between devices, share(): lax.all_to_all(jnp.broadcast_to(block[None], (count, *block.shape)), axes...  14.6 us
    ppermute x2, waiting for transfers between devices, neighbour(): return lax.ppermute(block, axis, [(0, 1), (1, 0)])  10 us
  transfers between devices with their start and end apart: 14, of which 10 were waited for; matrix products, arithmetic and copies ran while one was open for 5% of the time, Pallas kernels for 7%

profile of v7, /device:TPU:1, one launch (start us, length us, event | category | flops | bytes accessed | tf_op | source)
XLA Modules:
  0.0 261.9 jit_solution(15815354668853278835)
XLA Ops:
  7.2 1.3 fusion.6
  8.5 1.3 multiply_reduce_fusion
  9.8 0.1 reshape.124
  10.0 0.1 copy.39
  10.1 0.1 copy.50
  10.2 0.5 copy-done.3
  10.7 1.0 pad.20.clone
  11.9 15.5 %collective-permute-start = (bf16[2,112,128]{2,1,0:T(8,128)(2,1)S(1)}, bf16[2,112,128]{2,1,0:T(8,128)(2,1)S(1)}, u32[]{:S(2)}, u32[]{:S(2)}) collective-permute-start(bf16[2,112,128]{2,1,0:T(8,128)(2,1)S(1)} %pad.21), channel_id=1, source_target_pairs={{0,36},{1,44},{2,20},{3,52},{4,40},{5,32},{6,28},{7,24},{320,60},{... | collective-permute-start | bytes 172040 | tf_op jit(solution)/shard_map/ppermute | solution.py:328
  27.5 1.1 collective-permute-done
  28.6 0.8 broadcast_in_dim.58
  29.4 14.6 %all-to-all-start = ((bf16[16,112,128]{2,1,0:T(8,128)(2,1)}), bf16[16,112,128]{2,1,0:T(8,128)(2,1)S(1)}, u32[]{:S(2)}, u32[]{:S(2)}) async-start(bf16[16,112,128]{2,1,0:T(8,128)(2,1)} %broadcast_in_dim.58), calls=%async_computation | async-start | bytes 917504 | tf_op jit(solution)/shard_map/all_to_all | solution.py:76
  44.1 16.5 %all-gather = bf16[1216,384]{1,0:T(8,128)(2,1)S(1)} all-gather(bf16[304,384]{1,0:T(8,128)(2,1)S(1)} %fusion.1), channel_id=2, replica_groups=mesh['x'=4,'yh'=2,'z'=16,'yl'=2,'c'=2] {'yl','c'}, dimensions={0}, use_global_device_ids=true | all-gather | bytes 1167360 | tf_op jit(solution)/shard_map/all_gather | solution.py:338
  60.7 0.1 slice.138
  60.8 0.5 copy.49
  61.2 0.2 copy.46
  61.5 0.1 broadcast_compare_fusion
  61.6 0.1 broadcast_in_dim.59
  61.7 0.1 copy.44
  61.7 0.2 broadcast_in_dim.63
  62.0 0.8 broadcast_select_fusion
  62.8 0.4 copy.51
  63.2 1.8 pad.23.clone
  65.1 0.6 pad.24.squares
  65.7 1.2 fusion.5.at_z
  66.9 0.8 copy-done.4
  67.7 5.4 %shard_map.110 = f32[8,400,128]{2,1,0:T(8,128)} custom-call(s32[16]{0:T(128)} %fusion.5.at_z, bf16[16,112,128]{2,1,0:T(8,128)(2,1)} %copy-done.4, bf16[4,896,384]{2,1,0:T(8,128)(2,1)} %bitcast.56, f32[16,128]{1,0:T(8,128)} %pad.24.squares), custom_call_target="tpu_custom_call" | custom-call | tf_op jit(solution)/shard_map/pallas_call | solution.py:85
  73.1 4.9 %all-to-all-start.1 = ((f32[8,400,128]{2,1,0:T(8,128)}), f32[8,400,128]{2,1,0:T(8,128)S(1)}, u32[]{:S(2)}, u32[]{:S(2)}) async-start(f32[8,400,128]{2,1,0:T(8,128)} %shard_map.110), calls=%async_computation.1 | async-start | bytes 3276800 | tf_op jit(solution)/shard_map/all_to_all | solution.py:362
  78.0 20.1 %all-to-all-done.1.parts = f32[8,400,128]{2,1,0:T(8,128)S(1)} async-done(((f32[8,400,128]{2,1,0:T(8,128)}), f32[8,400,128]{2,1,0:T(8,128)S(1)}, u32[]{:S(2)}, u32[]{:S(2)}) %all-to-all-start.1) | async-done | bytes 1638432 | tf_op jit(solution)/shard_map/all_to_all | solution.py:362
  98.1 1.0 shard_map.111
  99.1 5.2 %all-to-all-start.2 = ((bf16[8,384,128]{2,1,0:T(8,128)(2,1)}), bf16[8,384,128]{2,1,0:T(8,128)(2,1)S(1)}, u32[]{:S(2)}, u32[]{:S(2)}) async-start(bf16[8,384,128]{2,1,0:T(8,128)(2,1)} %get-tuple-element.28), calls=%async_computation.2 | async-start | bytes 1572864 | tf_op jit(solution)/shard_map/all_to_all | solution.py:369
  104.3 9.9 %all-to-all-done.2.acts = bf16[8,384,128]{2,1,0:T(8,128)(2,1)S(1)} async-done(((bf16[8,384,128]{2,1,0:T(8,128)(2,1)}), bf16[8,384,128]{2,1,0:T(8,128)(2,1)S(1)}, u32[]{:S(2)}, u32[]{:S(2)}) %all-to-all-start.2) | async-done | bytes 786464 | tf_op jit(solution)/shard_map/all_to_all | solution.py:369
  114.2 0.9 copy-done.1
  115.0 5.2 %shard_map.112 = bf16[16,112,128]{2,1,0:T(8,128)(2,1)} custom-call(s32[16]{0:T(128)} %fusion.5.at_z, bf16[4,896,384]{2,1,0:T(8,128)(2,1)} %all-gather.7.cloned.1.call-done.far_rows, bf16[8,384,128]{2,1,0:T(8,128)(2,1)} %copy-done.1), custom_call_target="tpu_custom_call" | custom-call | tf_op jit(solution)/shard_map/pallas_call | solution.py:85
  120.2 17.7 %all-to-all-start.3 = ((bf16[16,112,128]{2,1,0:T(8,128)(2,1)}), bf16[16,112,128]{2,1,0:T(8,128)(2,1)S(1)}, u32[]{:S(2)}, u32[]{:S(2)}) async-start(bf16[16,112,128]{2,1,0:T(8,128)(2,1)} %shard_map.112), calls=%async_computation.3 | async-start | bytes 917504 | tf_op jit(solution)/shard_map/all_to_all | solution.py:381
  138.0 1.2 fusion.10
  139.2 0.1 maximum_select_fusion
  139.3 0.1 maximum_select_fusion.1
  139.5 1.9 collective-permute-start.1
  141.5 8.8 %collective-permute-done.1 = bf16[2,8,96,128]{3,2,0,1:T(8,128)(2,1)S(1)} collective-permute-done((bf16[2,8,96,128]{3,2,0,1:T(8,128)(2,1)S(1)}, bf16[2,8,96,128]{3,2,0,1:T(8,128)(2,1)S(1)}, u32[]{:S(2)}, u32[]{:S(2)}) %collective-permute-start.1) | collective-permute-done | bytes 393248 | tf_op jit(solution)/shard_map/ppermute | solution.py:301
  150.3 4.6 %collective-permute-start.2 = (bf16[2,8,96,128]{3,2,0,1:T(8,128)(2,1)S(1)}, bf16[2,8,96,128]{3,2,0,1:T(8,128)(2,1)S(1)}, u32[]{:S(2)}, u32[]{:S(2)}) collective-permute-start(bf16[2,8,96,128]{3,2,0,1:T(8,128)(2,1)S(1)} %pad_maximum_fusion.1), channel_id=1, source_target_pairs={{0,1},{1,0},{2,3},{3,2},{4,5},{5,4},{6,7},{7,6},{8,9},{9,8},{10,11... | collective-permute-start | bytes 1179656 | tf_op jit(solution)/shard_map/ppermute | solution.py:301
  155.0 1.3 collective-permute-done.2
  156.3 0.5 all-to-all-done.3.parts
  156.9 0.1 shard_map.113
  157.0 33.8 %all_to_all.40.gout = bf16[16,112,128]{2,1,0:T(8,128)(2,1)} all-to-all(bf16[16,112,128]{2,1,0:T(8,128)(2,1)S(1)} %get-tuple-element.33), channel_id=1, replica_groups=mesh['x'=4,'yh'=2,'z'=16,'yl'=2,'c'=2] {'z'}, dimensions={0} | all-to-all | bytes 917504 | tf_op jit(solution)/shard_map/all_to_all | solution.py:398
  190.8 2.0 all-gather.9.cloned.1.call-done
  192.8 5.4 %shard_map.114 = (bf16[8,384,128]{2,1,0:T(8,128)(2,1)}, f32[8,128]{1,0:T(8,128)}) custom-call(s32[16]{0:T(128)} %fusion.5.at_z, bf16[16,112,128]{2,1,0:T(8,128)(2,1)} %all_to_all.40.gout, bf16[4,896,384]{2,1,0:T(8,128)(2,1)} %all-gather.7.cloned.1.call-done.far_rows), custom_call_target="tpu_custom_call" | custom-call | tf_op jit(solution)/shard_map/pallas_call | solution.py:85
  198.3 6.1 %all-to-all-start.5 = ((bf16[8,384,128]{2,1,0:T(8,128)(2,1)}), bf16[8,384,128]{2,1,0:T(8,128)(2,1)S(1)}, u32[]{:S(2)}, u32[]{:S(2)}) async-start(bf16[8,384,128]{2,1,0:T(8,128)(2,1)} %get-tuple-element.36), calls=%async_computation.5 | async-start | bytes 1572864 | tf_op jit(solution)/shard_map/all_to_all | solution.py:411
  204.4 1.3 dynamic-slice_bitcast_fusion.places
  205.7 5.7 %collective-permute-start.3 = (bf16[112,128]{1,0:T(8,128)(2,1)S(1)}, bf16[112,128]{1,0:T(8,128)(2,1)S(1)}, u32[]{:S(2)}, u32[]{:S(2)}) collective-permute-start(bf16[112,128]{1,0:T(8,128)(2,1)S(1)} %get-tuple-element.40), channel_id=1, source_target_pairs={{36,0},{44,1},{20,2},{52,3},{40,4},{32,5},{28,6},{24,7},{60,320},{... | collective-permute-start | bytes 86024 | tf_op jit(solution)/shard_map/ppermute | solution.py:415
  211.4 0.1 fusion.11
  211.5 0.2 maximum_select_fusion.2
  211.6 2.7 %all-to-all-done.5.parts = bf16[8,384,128]{2,1,0:T(8,128)(2,1)S(1)} async-done(((bf16[8,384,128]{2,1,0:T(8,128)(2,1)}), bf16[8,384,128]{2,1,0:T(8,128)(2,1)S(1)}, u32[]{:S(2)}, u32[]{:S(2)}) %all-to-all-start.5) | async-done | bytes 786464 | tf_op jit(solution)/shard_map/all_to_all | solution.py:411
  214.3 0.9 shard_map.115
  215.2 8.3 %all-to-all-start.6 = ((bf16[8,112,128]{2,1,0:T(8,128)(2,1)}), bf16[8,112,128]{2,1,0:T(8,128)(2,1)S(1)}, u32[]{:S(2)}, u32[]{:S(2)}) async-start(bf16[8,112,128]{2,1,0:T(8,128)(2,1)} %shard_map.115), calls=%async_computation.6 | async-start | bytes 458752 | tf_op jit(solution)/shard_map/all_to_all | solution.py:413
  223.5 9.0 %all-to-all-done.6.got = bf16[8,112,128]{2,1,0:T(8,128)(2,1)S(1)} async-done(((bf16[8,112,128]{2,1,0:T(8,128)(2,1)}), bf16[8,112,128]{2,1,0:T(8,128)(2,1)S(1)}, u32[]{:S(2)}, u32[]{:S(2)}) %all-to-all-start.6) | async-done | bytes 229408 | tf_op jit(solution)/shard_map/all_to_all | solution.py:413
  232.5 1.0 shard_map.116
  233.5 4.7 %all-to-all-start.7 = ((bf16[4,784,128]{2,1,0:T(8,128)(2,1)}), bf16[4,784,128]{2,1,0:T(8,128)(2,1)S(1)}, u32[]{:S(2)}, u32[]{:S(2)}) async-start(bf16[4,784,128]{2,1,0:T(8,128)(2,1)} %shard_map.116), calls=%async_computation.7 | async-start | bytes 1605632 | tf_op jit(solution)/shard_map/all_to_all | solution.py:417
  238.2 1.2 convert_reduce_fusion
  239.5 0.6 bitcast_divide_fusion.pull
  240.1 0.6 reshape.131
  240.7 5.4 %shard_map.117 = f32[3,288,384]{2,1,0:T(8,128)} custom-call(s32[4,16]{1,0:T(4,128)} %dynamic-slice_bitcast_fusion.places, bf16[4,16,112,128]{3,2,1,0:T(8,128)(2,1)} %bitcast.66, bf16[8,384,128]{2,1,0:T(8,128)(2,1)} %bitcast.61, bf16[3,288,384]{2,1,0:T(8,128)(2,1)} %copy-done.3, f32[1,384]{1,0:T(1,128)} %bitcast_divide_fusion.pull, ...), custom_call_target="tpu_custom_call" | custom-call | tf_op jit(solution)/shard_map/pallas_call | solution.py:85
  246.1 3.4 %all-to-all-done.7.dpre = bf16[4,784,128]{2,1,0:T(8,128)(2,1)S(1)} async-done(((bf16[4,784,128]{2,1,0:T(8,128)(2,1)}), bf16[4,784,128]{2,1,0:T(8,128)(2,1)S(1)}, u32[]{:S(2)}, u32[]{:S(2)}) %all-to-all-start.7) | async-done | bytes 802848 | tf_op jit(solution)/shard_map/all_to_all | solution.py:417
  249.5 0.9 copy-done.5
  250.4 4.9 %shard_map.118 = (f32[288,384]{1,0:T(8,128)}, f32[3,128]{1,0:T(4,128)}, f32[1,1]{1,0:T(1,128)}) custom-call(s32[4,16]{1,0:T(4,128)} %dynamic-slice_bitcast_fusion.places, bf16[4,16,112,128]{3,2,1,0:T(8,128)(2,1)} %bitcast.65, bf16[4,784,128]{2,1,0:T(8,128)(2,1)} %copy-done.5, f32[3,384]{1,0:T(4,128)} %get-tuple-element.80.pick), custom_call_target="tpu_custom_call" | custom-call | tf_op jit(solution)/shard_map/pallas_call | solution.py:85
  (58 shorter events, 0.8 us)
Async XLA Ops:
  7.2 107.0 %all-gather.7.cloned.1.call-start = ((), (), s32[]{:S(2)}) async-start(), calls=%async_computation.8 | async-start | bytes 3440640 | tf_op jit(solution)/shard_map/all_gather | solution.py:339
  9.8 0.9 copy-start.3
  10.1 1.7 copy-start.7
  10.1 1.7 copy-start.8
  10.1 17.3 %copy-start.10 = (f32[384]{0:T(512)S(1)}, f32[384]{0:T(512)}, u32[]{:S(2)}) copy-start(f32[384]{0:T(512)} %param.10) | copy-start | bytes 4612
  10.1 17.3 %copy-start.9 = (s32[384]{0:T(512)S(1)}, s32[384]{0:T(512)}, u32[]{:S(2)}) copy-start(s32[384]{0:T(512)} %param.12) | copy-start | bytes 4612
  10.7 33.4 %copy-start.6 = (bf16[384,288]{0,1:T(8,128)(2,1)S(1)}, bf16[384,288]{0,1:T(8,128)(2,1)}, u32[]{:S(2)}) copy-start(bf16[384,288]{0,1:T(8,128)(2,1)} %param.9) | copy-start | bytes 663556
  11.9 16.7 %collective-permute-start = (bf16[2,112,128]{2,1,0:T(8,128)(2,1)S(1)}, bf16[2,112,128]{2,1,0:T(8,128)(2,1)S(1)}, u32[]{:S(2)}, u32[]{:S(2)}) collective-permute-start(bf16[2,112,128]{2,1,0:T(8,128)(2,1)S(1)} %pad.21), channel_id=1, source_target_pairs={{0,36},{1,44},{2,20},{3,52},{4,40},{5,32},{6,28},{7,24},{320,60},{... | collective-permute-start | bytes 172040 | tf_op jit(solution)/shard_map/ppermute | solution.py:328
  29.4 37.4 %all-to-all-start = ((bf16[16,112,128]{2,1,0:T(8,128)(2,1)}), bf16[16,112,128]{2,1,0:T(8,128)(2,1)S(1)}, u32[]{:S(2)}, u32[]{:S(2)}) async-start(bf16[16,112,128]{2,1,0:T(8,128)(2,1)} %broadcast_in_dim.58), calls=%async_computation | async-start | bytes 917504 | tf_op jit(solution)/shard_map/all_to_all | solution.py:76
  66.9 0.8 copy-start.4
  73.1 25.0 %all-to-all-start.1 = ((f32[8,400,128]{2,1,0:T(8,128)}), f32[8,400,128]{2,1,0:T(8,128)S(1)}, u32[]{:S(2)}, u32[]{:S(2)}) async-start(f32[8,400,128]{2,1,0:T(8,128)} %shard_map.110), calls=%async_computation.1 | async-start | bytes 3276800 | tf_op jit(solution)/shard_map/all_to_all | solution.py:362
  99.1 15.1 %all-to-all-start.2 = ((bf16[8,384,128]{2,1,0:T(8,128)(2,1)}), bf16[8,384,128]{2,1,0:T(8,128)(2,1)S(1)}, u32[]{:S(2)}, u32[]{:S(2)}) async-start(bf16[8,384,128]{2,1,0:T(8,128)(2,1)} %get-tuple-element.28), calls=%async_computation.2 | async-start | bytes 1572864 | tf_op jit(solution)/shard_map/all_to_all | solution.py:369
  114.2 0.9 copy-start.1
  120.2 18.9 %copy-start.2 = (bf16[8,384,128]{2,1,0:T(8,128)(2,1)S(1)}, bf16[8,384,128]{2,1,0:T(8,128)(2,1)}, u32[]{:S(2)}) copy-start(bf16[8,384,128]{2,1,0:T(8,128)(2,1)} %copy-done.1) | copy-start | bytes 2359300
  120.2 36.6 %all-to-all-start.3 = ((bf16[16,112,128]{2,1,0:T(8,128)(2,1)}), bf16[16,112,128]{2,1,0:T(8,128)(2,1)S(1)}, u32[]{:S(2)}, u32[]{:S(2)}) async-start(bf16[16,112,128]{2,1,0:T(8,128)(2,1)} %shard_map.112), calls=%async_computation.3 | async-start | bytes 917504 | tf_op jit(solution)/shard_map/all_to_all | solution.py:381
  137.9 54.9 %all-gather.9.cloned.1.call-start = ((), (), s32[]{:S(2)}) async-start(), calls=%async_computation.9 | async-start | bytes 2293760 | tf_op jit(solution)/shard_map/all_gather | solution.py:397
  139.5 10.7 %collective-permute-start.1 = (bf16[2,8,96,128]{3,2,0,1:T(8,128)(2,1)S(1)}, bf16[2,8,96,128]{3,2,0,1:T(8,128)(2,1)S(1)}, u32[]{:S(2)}, u32[]{:S(2)}) collective-permute-start(bf16[2,8,96,128]{3,2,0,1:T(8,128)(2,1)S(1)} %slice.152), channel_id=1, source_target_pairs={{0,2},{2,0},{1,3},{3,1},{4,6},{6,4},{5,7},{7,5},{8,10},{10,8},{9,1... | collective-permute-start | bytes 1179656 | tf_op jit(solution)/shard_map/ppermute | solution.py:301
  150.3 5.9 %collective-permute-start.2 = (bf16[2,8,96,128]{3,2,0,1:T(8,128)(2,1)S(1)}, bf16[2,8,96,128]{3,2,0,1:T(8,128)(2,1)S(1)}, u32[]{:S(2)}, u32[]{:S(2)}) collective-permute-start(bf16[2,8,96,128]{3,2,0,1:T(8,128)(2,1)S(1)} %pad_maximum_fusion.1), channel_id=1, source_target_pairs={{0,1},{1,0},{2,3},{3,2},{4,5},{5,4},{6,7},{7,6},{8,9},{9,8},{10,11... | collective-permute-start | bytes 1179656 | tf_op jit(solution)/shard_map/ppermute | solution.py:301
  156.8 83.9 %all-gather.11.cloned.1.call-start = ((), (), s32[]{:S(2)}) async-start(), calls=%async_computation.10 | async-start | bytes 2293760 | tf_op jit(solution)/shard_map/all_gather | solution.py:401
  198.3 16.0 %all-to-all-start.5 = ((bf16[8,384,128]{2,1,0:T(8,128)(2,1)}), bf16[8,384,128]{2,1,0:T(8,128)(2,1)S(1)}, u32[]{:S(2)}, u32[]{:S(2)}) async-start(bf16[8,384,128]{2,1,0:T(8,128)(2,1)} %get-tuple-element.36), calls=%async_computation.5 | async-start | bytes 1572864 | tf_op jit(solution)/shard_map/all_to_all | solution.py:411
  204.4 9.9 %copy-start = (f32[8,128]{1,0:T(8,128)S(1)}, f32[8,128]{1,0:T(8,128)}, u32[]{:S(2)}) copy-start(f32[8,128]{1,0:T(8,128)} %get-tuple-element.39.loss) | copy-start | bytes 12292
  205.7 27.8 %collective-permute-start.3 = (bf16[112,128]{1,0:T(8,128)(2,1)S(1)}, bf16[112,128]{1,0:T(8,128)(2,1)S(1)}, u32[]{:S(2)}, u32[]{:S(2)}) collective-permute-start(bf16[112,128]{1,0:T(8,128)(2,1)S(1)} %get-tuple-element.40), channel_id=1, source_target_pairs={{36,0},{44,1},{20,2},{52,3},{40,4},{32,5},{28,6},{24,7},{60,320},{... | collective-permute-start | bytes 86024 | tf_op jit(solution)/shard_map/ppermute | solution.py:415
  215.2 17.4 %all-to-all-start.6 = ((bf16[8,112,128]{2,1,0:T(8,128)(2,1)}), bf16[8,112,128]{2,1,0:T(8,128)(2,1)S(1)}, u32[]{:S(2)}, u32[]{:S(2)}) async-start(bf16[8,112,128]{2,1,0:T(8,128)(2,1)} %shard_map.115), calls=%async_computation.6 | async-start | bytes 458752 | tf_op jit(solution)/shard_map/all_to_all | solution.py:413
  233.5 16.0 %all-to-all-start.7 = ((bf16[4,784,128]{2,1,0:T(8,128)(2,1)}), bf16[4,784,128]{2,1,0:T(8,128)(2,1)S(1)}, u32[]{:S(2)}, u32[]{:S(2)}) async-start(bf16[4,784,128]{2,1,0:T(8,128)(2,1)} %shard_map.116), calls=%async_computation.7 | async-start | bytes 1605632 | tf_op jit(solution)/shard_map/all_to_all | solution.py:417
  249.5 0.9 copy-start.5
Sparse Core Ops, SparseCore 0:
  11.9 53.1 all-gather.6
  156.9 35.8 all-gather.8
  194.9 38.5 all-gather.10

commit v8 on v5

--- a/solution.py
+++ b/solution.py
@@ -60,6 +60,20 @@
 
 def matmul(a, b, left, right):
     return lax.dot_general(a, b, (((left,), (right,)), ((), ())), preferred_element_type=f32)
+
+
+def arrange(dec, reach, out, square, masked, ordered):
+    total = jnp.zeros((1, 384), f32)
+    for layer in range(LAYERS):
+        masked[...] = jnp.where(reach[layer : layer + 1] > 0, dec[layer].astype(f32), 0.0)
+        total = total + jnp.sum(masked[...] * masked[...], axis=0, keepdims=True)
+        for r in range(8):
+            at = r * BLOCK + layer * 36
+            ordered[at : at + 36] = masked[r * 36 : r * 36 + 36]
+    for r in range(8):
+        ordered[r * BLOCK + 108 : (r + 1) * BLOCK] = jnp.zeros((BLOCK - 108, 384), f32)
+    out[...] = ordered[...].astype(bf16)
+    square[...] = total
 
 
 def encode(x, rows, squares, out):
@@ -182,17 +196,26 @@
     return total
 
 
-def decoder_gradient(blocks, acts, rows, pull, reach, out, total):
-    total[...] = over_tokens(blocks, lambda h, q, c: tokens_of(acts, h, q * 3 + c))
+def decoder_gradient(blocks, acts, rows, norms, reach, out, total):
+    def values(half, q, c):
+        here = acts[q, half * 4 : half * 4 + 4, c * 32 : c * 32 + 32]
+        return here.reshape(128, 128)
+
+    total[...] = over_tokens(blocks, values)
+    sums = []
+    for c in range(3):
+        column = acts[:, :, c * 32 : c * 32 + 32].reshape(1024, 128).astype(f32)
+        sums.append(jnp.sum(column, axis=0, keepdims=True))
+    pull = (sparsity_weight / TOK_DEV) * jnp.concatenate(sums, axis=1) / norms[...]
     for layer in range(LAYERS):
         for r in range(8):
             at = r * BLOCK + layer * 36
             out[layer, r * 36 : r * 36 + 36] = total[at : at + 36]
-        whole = out[layer] + pull[0:1] * rows[layer].astype(f32)
+        whole = out[layer] + pull * rows[layer].astype(f32)
         out[layer] = jnp.where(reach[layer : layer + 1] > 0, whole, 0.0)
 
 
-def encoder_gradient(blocks, dpre, pick, out, sums, total):
+def encoder_gradient(blocks, dpre, pick, out, bias, loss, total):
     def values(half, q, c):
         parts = [
             dpre[half * 2 + g // 2, pl.ds(((g % 2) * 4 + q) * 96 + c * 32, 32)] for g in range(4)
@@ -207,20 +230,9 @@
             own = own + jnp.where(pick[layer : layer + 1] > 0, total[at : at + 36], 0.0)
         out[r * 36 : r * 36 + 36] = own
     tail = jnp.sum(dpre[:, 768:784].astype(f32), axis=0)
-    sums[0:4] = tail[0:4] + tail[4:8] + tail[8:12]
-    sums[4:8] = jnp.zeros((4, 128), f32)
-
-
-def neighbour(block, axis):
-    return lax.ppermute(block, axis, [(0, 1), (1, 0)])
-
-
-def relative(blocks):
-    yl, c = lax.axis_index("yl"), lax.axis_index("c")
-    swapped = jnp.concatenate([blocks[2:], blocks[:2]])
-    blocks = jnp.where(yl == 1, swapped, blocks)
-    swapped = jnp.stack([blocks[1], blocks[0], blocks[3], blocks[2]])
-    return jnp.where(c == 1, swapped, blocks)
+    tail = tail[0:4] + tail[4:8] + tail[8:12]
+    bias[...] = tail[0:3]
+    loss[...] = jnp.sum(tail[3:4], axis=1, keepdims=True) / TOK_DEV
 
 
 together = lax.optimization_barrier
@@ -239,11 +251,16 @@
     x_block, target_block = both[0], both[1]
 
     enc_t = enc_weight.T
-    dec_t = jnp.where(reach[:, None, :], dec_weight.transpose(1, 2, 0), 0)
-    square = jnp.sum(jnp.square(dec_t.astype(f32)), axis=(0, 1))
-    dec_own = dec_t.reshape(3, 8, 36, 384).transpose(1, 0, 2, 3).reshape(8, 108, 384)
-    dec_own = jnp.pad(dec_own, ((0, 0), (0, BLOCK - 108), (0, 0))).reshape(8 * BLOCK, 384)
-    extra = jnp.stack([source.astype(bf16), *pieces(enc_bias), *pieces(square)])
+    dec_t = dec_weight.transpose(1, 2, 0)
+    reach_wide = reach.astype(f32)
+    dec_own, square = call(
+        arrange,
+        dec_t,
+        reach_wide,
+        out=[((8 * BLOCK, 384), bf16), ((1, 384), f32)],
+        scratch=[pltpu.VMEM((288, 384), f32), pltpu.VMEM((8 * BLOCK, 384), f32)],
+    )
+    extra = jnp.stack([source.astype(bf16), *pieces(enc_bias), *pieces(square[0])])
     enc_own = jnp.concatenate([enc_t, jnp.pad(extra, ((0, 9), (0, 0)))])
     enc_quad = lax.all_gather(enc_own, QUAD)
     dec_quad = lax.all_gather(dec_own, QUAD)
@@ -259,7 +276,6 @@
 
     x_quad = share(x_block, "z", 16).reshape(2, 8 * BLOCK, 128)
     squares = jnp.pad(square_quad.reshape(12, 128), ((0, 4), (0, 0)))
-    x_quad, dec_quad = together((x_quad, dec_quad))
     (partial,) = call(encode, x_quad, enc_rows, squares, out=[((8, 400, 128), f32)])
     partial = lax.all_to_all(partial, DP, 0, 0)
     pre, norms, acts, sparsity = call(
@@ -268,19 +284,14 @@
         bias_quad.reshape(12, 128),
         out=[((384, 128), f32), ((16, 128), f32), ((8, 384, 128), bf16), ((8, 128), f32)],
     )
+    acts, dec_quad = together((acts, dec_quad))
     acts_quad = lax.all_to_all(acts, DP, 0, 0)
 
     (terms,) = call(decode, dec_quad, acts_quad, out=[((16, BLOCK, 128), bf16)])
-    terms, acts_sent = together((terms, acts_quad))
     parts = lax.all_to_all(terms, "z", 0, 0)
-    acts_sent = relative(acts_sent.reshape(8, 4, 96, 128).transpose(1, 0, 2, 3))
-    near, far = acts_sent[:2], neighbour(acts_sent[2:], "yl")
-    mine = jnp.stack([near[0], far[0]])
-    other = neighbour(jnp.stack([near[1], far[1]]), "c")
-    acts_every = relative(jnp.stack([mine[0], other[0], mine[1], other[1]]))
-    acts_every = acts_every.transpose(1, 0, 2, 3).reshape(8, 384, 128)
-    colsum = jnp.sum(acts_every.reshape(8, 4, 3, 32, 128).astype(f32), axis=(0, 1, 3)).reshape(384)
-    parts, acts_every, colsum = together((parts, acts_every, colsum))
+    acts_every = lax.all_gather(acts_quad, QUAD)
+    member = lax.axis_index(QUAD)
+    acts_every = lax.dynamic_slice_in_dim(acts_every, member * 96, 96, 2)
     recon, gout = call(
         compare,
         parts,
@@ -300,37 +311,33 @@
     (sent,) = call(slopes_of, slopes, pre, norms, loss_z, out=[((8, 112, 128), bf16)])
     got = lax.all_to_all(sent, PLANE, 0, 0)
     (sent,) = call(regroup, got, out=[((4, 784, 128), bf16)])
+    recon = lax.ppermute(recon, ALL, back)
+    sent, recon = together((sent, recon))
     got = lax.all_to_all(sent, "x", 0, 0)
 
     total = pltpu.VMEM((8 * BLOCK, 384), f32)
-    member = lax.axis_index(QUAD)
-    own_norms = lax.dynamic_index_in_dim(norms[:12].reshape(4, 384), member, 0, False)
-    pull = ((sparsity_weight / TOK_DEV) * colsum / own_norms)[None]
+    own_norms = lax.dynamic_index_in_dim(norms[:12].reshape(4, 384), member, 0, True)
     (dec_grad,) = call(
         decoder_gradient,
         gout_every,
         acts_every,
         dec_t,
-        pull,
-        reach.astype(f32),
+        own_norms,
+        reach_wide,
         out=[((LAYERS, 288, 384), f32)],
         scratch=[total],
     )
     got, dec_grad = together((got, dec_grad))
-    enc_grad, sums = call(
+    enc_grad, bias_grad, loss = call(
         encoder_gradient,
         x_every,
         got,
         pick.astype(f32),
-        out=[((288, 384), f32), ((8, 128), f32)],
+        out=[((288, 384), f32), ((3, 128), f32), ((1, 1), f32)],
         scratch=[total],
     )
-    bias_grad = sums[:3].reshape(384)
-    loss = sums[3].sum() / TOK_DEV
-    recon = lax.ppermute(recon, ALL, back)
-    recon, enc_grad = together((recon, enc_grad))
     recon = recon[:108].reshape(3, 36, 128).transpose(2, 0, 1)
-    return (loss, recon, enc_grad.T, bias_grad, dec_grad.transpose(2, 0, 1))
+    return (loss[0, 0], recon, enc_grad.T, bias_grad.reshape(384), dec_grad.transpose(2, 0, 1))
 
 
 def solution(mesh):

time: 261 us -> 263 us (level)
  the two profiles are of different devices: /device:TPU:1 before, /device:TPU:16 now
where the time goes in v8:
time: 263 us; the launch traced here: 262 us
  blocking collectives  121 us (46%)
  starting transfers between devices  48.8 us (19%)
  waiting for transfers between devices  48 us (18%)
  local copies, waits for them, and re-layouts  15.3 us (6%)
  between operations  14.1 us (5%)
  Pallas kernels  11.6 us (4%)
    all_to_all x1, blocking collectives, on_device(): parts = lax.all_to_all(terms, 'z', 0, 0)  36.4 us
    all_to_all x1, blocking collectives, on_device(): gout_all = lax.all_to_all(gout, 'z', 0, 0)  31.8 us
    all_to_all x1, blocking collectives, on_device(): slopes = lax.all_to_all(slopes, DP, 0, 0)  18.4 us
    all_to_all x1, blocking collectives, on_device(): acts_quad = lax.all_to_all(acts, DP, 0, 0)  17.9 us
    all_to_all x1, waiting for transfers between devices, on_device(): partial = lax.all_to_all(partial, DP, 0, 0)  17.5 us
    all_gather x1, blocking collectives, on_device(): enc_quad = lax.all_gather(enc_own, QUAD)  16.9 us
    ppermute x1, starting transfers between devices, on_device(): both = lax.ppermute(both, ALL, to)  15.5 us
    all_to_all x1, starting transfers between devices, share(): lax.all_to_all(jnp.broadcast_to(block[None], (count, *block.shape)), axes...  13 us
  transfers between devices with their start and end apart: 10, of which 6 were waited for; matrix products, arithmetic and copies ran while one was open for 2% of the time, Pallas kernels for 3%

profile of v8, /device:TPU:16, one launch (start us, length us, event | category | flops | bytes accessed | tf_op | source)
XLA Modules:
  0.0 261.8 jit_solution(13163623023382824411)
XLA Ops:
  7.2 0.0 all-gather.12.cloned.1.call-start
  7.2 0.7 fusion.3
  7.9 1.1 copy-done.7
  9.0 1.3 shard_map.101
  10.3 0.0 all-gather.12.cloned.1.call-update
  10.3 0.8 maximum_bitcast_fusion
  11.2 15.5 %collective-permute-start = (bf16[2,112,128]{2,1,0:T(8,128)(2,1)S(1)}, bf16[2,112,128]{2,1,0:T(8,128)(2,1)S(1)}, u32[]{:S(2)}, u32[]{:S(2)}) collective-permute-start(bf16[2,112,128]{2,1,0:T(8,128)(2,1)S(1)} %pad.16), channel_id=1, source_target_pairs={{0,0},{1,4},{2,8},{3,12},{4,16},{5,20},{6,24},{7,28},{8,64},{9,68}... | collective-permute-start | bytes 172040 | tf_op jit(solution)/shard_map/ppermute | solution.py:250
  26.7 1.8 collective-permute-done
  28.5 0.8 broadcast_in_dim.42
  29.3 13.0 %all-to-all-start = ((bf16[16,112,128]{2,1,0:T(8,128)(2,1)}), bf16[16,112,128]{2,1,0:T(8,128)(2,1)S(1)}, u32[]{:S(2)}, u32[]{:S(2)}) async-start(bf16[16,112,128]{2,1,0:T(8,128)(2,1)} %broadcast_in_dim.42), calls=%async_computation | async-start | bytes 917504 | tf_op jit(solution)/shard_map/all_to_all | solution.py:42
  42.3 0.0 all-gather.8.cloned.1.call-start
  42.4 0.0 copy-done.12
  42.4 0.0 copy-done.13
  42.5 16.9 %all-gather = bf16[1216,384]{1,0:T(8,128)(2,1)S(1)} all-gather(bf16[304,384]{1,0:T(8,128)(2,1)S(1)} %fusion.1), channel_id=2, replica_groups=mesh['x'=4,'yh'=2,'z'=16,'yl'=2,'c'=2] {'yl','c'}, dimensions={0}, use_global_device_ids=true | all-gather | bytes 1167360 | tf_op jit(solution)/shard_map/all_gather | solution.py:265
  59.5 9.9 %all-to-all-done = bf16[16,112,128]{2,1,0:T(8,128)(2,1)S(1)} async-done(((bf16[16,112,128]{2,1,0:T(8,128)(2,1)}), bf16[16,112,128]{2,1,0:T(8,128)(2,1)S(1)}, u32[]{:S(2)}, u32[]{:S(2)}) %all-to-all-start) | async-done | bytes 458784 | tf_op jit(solution)/shard_map/all_to_all | solution.py:42
  69.4 0.8 copy-done.4
  70.2 0.0 all-gather.8.cloned.1.call-update
  70.3 0.1 slice.55
  70.4 0.5 copy.27
  70.8 0.2 copy.24
  71.0 0.1 broadcast_compare_fusion
  71.1 0.1 broadcast_in_dim.43
  71.2 0.1 copy.22
  71.3 0.2 broadcast_in_dim.47
  71.5 0.8 broadcast_select_fusion
  72.4 0.4 copy.28
  72.8 0.3 pad.18.clone
  73.1 0.7 copy-done.5
  73.8 1.3 shard_map.102
  75.1 1.2 copy-done.3
  76.3 7.5 %all-to-all-start.1 = ((f32[8,400,128]{2,1,0:T(8,128)}), f32[8,400,128]{2,1,0:T(8,128)S(1)}, u32[]{:S(2)}, u32[]{:S(2)}) async-start(f32[8,400,128]{2,1,0:T(8,128)} %copy-done.3), calls=%async_computation.1 | async-start | bytes 3276800 | tf_op jit(solution)/shard_map/all_to_all | solution.py:280
  83.8 0.0 all-gather.14.cloned.1.call-start
  83.8 17.5 %all-to-all-done.1.parts = f32[8,400,128]{2,1,0:T(8,128)S(1)} async-done(((f32[8,400,128]{2,1,0:T(8,128)}), f32[8,400,128]{2,1,0:T(8,128)S(1)}, u32[]{:S(2)}, u32[]{:S(2)}) %all-to-all-start.1) | async-done | bytes 1638432 | tf_op jit(solution)/shard_map/all_to_all | solution.py:280
  101.3 0.1 shard_map.103
  101.4 0.0 all-gather.12.cloned.1.call-done
  101.4 17.9 %all_to_all.40.acts = bf16[8,384,128]{2,1,0:T(8,128)(2,1)} all-to-all(bf16[8,384,128]{2,1,0:T(8,128)(2,1)S(1)} %get-tuple-element.30), channel_id=1, replica_groups=mesh['x'=4,'yh'=2,'z'=16,'yl'=2,'c'=2] {'x','yh'}, dimensions={0} | all-to-all | bytes 1572864 | tf_op jit(solution)/shard_map/all_to_all | solution.py:288
  119.3 0.0 all-gather.14.cloned.1.call-update
  119.4 0.0 all-gather.10.cloned.1.call-start
  119.4 1.8 copy-done
  121.2 1.1 copy-done.2
  122.3 1.6 shard_map.104
  123.9 36.4 %all_to_all.41.parts = bf16[16,112,128]{2,1,0:T(8,128)(2,1)S(1)} all-to-all(bf16[16,112,128]{2,1,0:T(8,128)(2,1)S(1)} %shard_map.104), channel_id=1, replica_groups=mesh['x'=4,'yh'=2,'z'=16,'yl'=2,'c'=2] {'z'}, dimensions={0} | all-to-all | bytes 917504 | tf_op jit(solution)/shard_map/all_to_all | solution.py:291
  160.3 0.1 shard_map.105
  160.4 0.0 all-gather.8.cloned.1.call-done.blocks
  160.5 31.8 %all_to_all.42.gout = bf16[16,112,128]{2,1,0:T(8,128)(2,1)} all-to-all(bf16[16,112,128]{2,1,0:T(8,128)(2,1)S(1)} %get-tuple-element.34), channel_id=1, replica_groups=mesh['x'=4,'yh'=2,'z'=16,'yl'=2,'c'=2] {'z'}, dimensions={0} | all-to-all | bytes 917504 | tf_op jit(solution)/shard_map/all_to_all | solution.py:304
  192.3 0.0 all-gather.10.cloned.1.call-update
  192.3 1.0 copy-done.6
  193.3 1.3 shard_map.106
  194.6 18.4 %all_to_all.43.parts = bf16[8,384,128]{2,1,0:T(8,128)(2,1)S(1)} all-to-all(bf16[8,384,128]{2,1,0:T(8,128)(2,1)S(1)} %get-tuple-element.35), channel_id=1, replica_groups=mesh['x'=4,'yh'=2,'z'=16,'yl'=2,'c'=2] {'x','yh'}, dimensions={0} | all-to-all | bytes 1572864 | tf_op jit(solution)/shard_map/all_to_all | solution.py:310
  213.0 0.9 shard_map.107
  213.8 5.8 %all-to-all-start.6 = ((bf16[8,112,128]{2,1,0:T(8,128)(2,1)}), bf16[8,112,128]{2,1,0:T(8,128)(2,1)S(1)}, u32[]{:S(2)}, u32[]{:S(2)}) async-start(bf16[8,112,128]{2,1,0:T(8,128)(2,1)} %shard_map.107), calls=%async_computation.6 | async-start | bytes 458752 | tf_op jit(solution)/shard_map/all_to_all | solution.py:312
  219.7 3.2 %collective-permute-start.1 = (bf16[112,128]{1,0:T(8,128)(2,1)S(1)}, bf16[112,128]{1,0:T(8,128)(2,1)S(1)}, u32[]{:S(2)}, u32[]{:S(2)}) collective-permute-start(bf16[112,128]{1,0:T(8,128)(2,1)S(1)} %get-tuple-element.39), channel_id=1, source_target_pairs={{0,0},{4,1},{8,2},{12,3},{16,4},{20,5},{24,6},{28,7},{64,8},{68,9}... | collective-permute-start | bytes 86024 | tf_op jit(solution)/shard_map/ppermute | solution.py:314
  222.9 3.3 %all-to-all-done.6.got = bf16[8,112,128]{2,1,0:T(8,128)(2,1)S(1)} async-done(((bf16[8,112,128]{2,1,0:T(8,128)(2,1)}), bf16[8,112,128]{2,1,0:T(8,128)(2,1)S(1)}, u32[]{:S(2)}, u32[]{:S(2)}) %all-to-all-start.6) | async-done | bytes 229408 | tf_op jit(solution)/shard_map/all_to_all | solution.py:312
  226.3 1.0 shard_map.108
  227.3 9.3 %collective-permute-done.1 = bf16[112,128]{1,0:T(8,128)(2,1)S(1)} collective-permute-done((bf16[112,128]{1,0:T(8,128)(2,1)S(1)}, bf16[112,128]{1,0:T(8,128)(2,1)S(1)}, u32[]{:S(2)}, u32[]{:S(2)}) %collective-permute-start.1) | collective-permute-done | bytes 28704 | tf_op jit(solution)/shard_map/ppermute | solution.py:314
  236.6 3.6 %all-to-all-start.7 = ((bf16[4,784,128]{2,1,0:T(8,128)(2,1)}), bf16[4,784,128]{2,1,0:T(8,128)(2,1)S(1)}, u32[]{:S(2)}, u32[]{:S(2)}) async-start(bf16[4,784,128]{2,1,0:T(8,128)(2,1)} %shard_map.108), calls=%async_computation.7 | async-start | bytes 1605632 | tf_op jit(solution)/shard_map/all_to_all | solution.py:316
  240.2 0.6 reshape.54
  240.8 1.2 constant_dynamic-slice_fusion.1.acts
  242.1 0.0 all-gather.10.cloned.1.call-done.blocks
  242.1 1.5 copy-done.10
  243.6 2.2 shard_map.109
  245.8 6.1 %all-to-all-done.7.dpre = bf16[4,784,128]{2,1,0:T(8,128)(2,1)S(1)} async-done(((bf16[4,784,128]{2,1,0:T(8,128)(2,1)}), bf16[4,784,128]{2,1,0:T(8,128)(2,1)S(1)}, u32[]{:S(2)}, u32[]{:S(2)}) %all-to-all-start.7) | async-done | bytes 802848 | tf_op jit(solution)/shard_map/all_to_all | solution.py:316
  251.9 1.5 copy-done.9
  253.4 1.9 shard_map.110
  (40 shorter events, 0.3 us)
Async XLA Ops:
  7.2 35.2 %copy-start.12 = (s32[384]{0:T(512)S(1)}, s32[384]{0:T(512)}, u32[]{:S(2)}) copy-start(s32[384]{0:T(512)} %param.11) | copy-start | bytes 4612
  7.2 35.2 %copy-start.13 = (f32[384]{0:T(512)S(1)}, f32[384]{0:T(512)}, u32[]{:S(2)}) copy-start(f32[384]{0:T(512)} %param.9) | copy-start | bytes 4612
  7.2 94.2 %all-gather.12.cloned.1.call-start = ((), (), s32[]{:S(2)}) async-start(), calls=%async_computation.10 | async-start | bytes 3440640 | tf_op jit(solution)/shard_map/all_gather | solution.py:266
  7.9 1.1 copy-start.7
  9.0 33.5 %copy-start.11 = (bf16[384,288]{0,1:T(8,128)(2,1)S(1)}, bf16[384,288]{0,1:T(8,128)(2,1)}, u32[]{:S(2)}) copy-start(bf16[384,288]{0,1:T(8,128)(2,1)} %param.8) | copy-start | bytes 663556
  11.2 17.3 %collective-permute-start = (bf16[2,112,128]{2,1,0:T(8,128)(2,1)S(1)}, bf16[2,112,128]{2,1,0:T(8,128)(2,1)S(1)}, u32[]{:S(2)}, u32[]{:S(2)}) collective-permute-start(bf16[2,112,128]{2,1,0:T(8,128)(2,1)S(1)} %pad.16), channel_id=1, source_target_pairs={{0,0},{1,4},{2,8},{3,12},{4,16},{5,20},{6,24},{7,28},{8,64},{9,68}... | collective-permute-start | bytes 172040 | tf_op jit(solution)/shard_map/ppermute | solution.py:250
  29.3 40.1 %all-to-all-start = ((bf16[16,112,128]{2,1,0:T(8,128)(2,1)}), bf16[16,112,128]{2,1,0:T(8,128)(2,1)S(1)}, u32[]{:S(2)}, u32[]{:S(2)}) async-start(bf16[16,112,128]{2,1,0:T(8,128)(2,1)} %broadcast_in_dim.42), calls=%async_computation | async-start | bytes 917504 | tf_op jit(solution)/shard_map/all_to_all | solution.py:42
  42.3 118.1 %all-gather.8.cloned.1.call-start = ((), (), s32[]{:S(2)}) async-start(), calls=%async_computation.8 | async-start | bytes 2293760 | tf_op jit(solution)/shard_map/all_gather | solution.py:302
  69.4 0.8 copy-start.4
  72.7 1.0 copy-start.5
  75.0 1.2 copy-start.3
  76.3 25.0 %all-to-all-start.1 = ((f32[8,400,128]{2,1,0:T(8,128)}), f32[8,400,128]{2,1,0:T(8,128)S(1)}, u32[]{:S(2)}, u32[]{:S(2)}) async-start(f32[8,400,128]{2,1,0:T(8,128)} %copy-done.3), calls=%async_computation.1 | async-start | bytes 3276800 | tf_op jit(solution)/shard_map/all_to_all | solution.py:280
  83.8 157.1 %all-gather.14.cloned.1.call-start = ((), (), s32[]{:S(2)}) async-start(), calls=%async_computation.11 | async-start | bytes 3932160 | tf_op jit(solution)/shard_map/all_gather | solution.py:292
  119.4 122.7 %all-gather.10.cloned.1.call-start = ((), (), s32[]{:S(2)}) async-start(), calls=%async_computation.9 | async-start | bytes 2293760 | tf_op jit(solution)/shard_map/all_gather | solution.py:306
  119.4 1.8 copy-start
  121.2 1.1 copy-start.2
  122.3 70.0 %copy-start.1 = (bf16[3584,384]{1,0:T(8,128)(2,1)S(1)}, bf16[3584,384]{1,0:T(8,128)(2,1)}, u32[]{:S(2)}) copy-start(bf16[3584,384]{1,0:T(8,128)(2,1)} %all-gather.12.cloned.1.call-done) | copy-start | bytes 8257540
  192.3 1.0 copy-start.6
  213.8 28.2 %copy-start.8 = (bf16[384,3,288]{0,2,1:T(8,128)(2,1)S(1)}, bf16[384,3,288]{0,2,1:T(8,128)(2,1)}, u32[]{:S(2)}) copy-start(bf16[384,3,288]{0,2,1:T(8,128)(2,1)} %param.10) | copy-start | bytes 1990660
  213.8 12.4 %all-to-all-start.6 = ((bf16[8,112,128]{2,1,0:T(8,128)(2,1)}), bf16[8,112,128]{2,1,0:T(8,128)(2,1)S(1)}, u32[]{:S(2)}, u32[]{:S(2)}) async-start(bf16[8,112,128]{2,1,0:T(8,128)(2,1)} %shard_map.107), calls=%async_computation.6 | async-start | bytes 458752 | tf_op jit(solution)/shard_map/all_to_all | solution.py:312
  219.7 16.9 %collective-permute-start.1 = (bf16[112,128]{1,0:T(8,128)(2,1)S(1)}, bf16[112,128]{1,0:T(8,128)(2,1)S(1)}, u32[]{:S(2)}, u32[]{:S(2)}) collective-permute-start(bf16[112,128]{1,0:T(8,128)(2,1)S(1)} %get-tuple-element.39), channel_id=1, source_target_pairs={{0,0},{4,1},{8,2},{12,3},{16,4},{20,5},{24,6},{28,7},{64,8},{68,9}... | collective-permute-start | bytes 86024 | tf_op jit(solution)/shard_map/ppermute | solution.py:314
  236.6 15.3 %all-to-all-start.7 = ((bf16[4,784,128]{2,1,0:T(8,128)(2,1)}), bf16[4,784,128]{2,1,0:T(8,128)(2,1)S(1)}, u32[]{:S(2)}, u32[]{:S(2)}) async-start(bf16[4,784,128]{2,1,0:T(8,128)(2,1)} %shard_map.108), calls=%async_computation.7 | async-start | bytes 1605632 | tf_op jit(solution)/shard_map/all_to_all | solution.py:316
  242.1 1.5 copy-start.10
  251.9 1.5 copy-start.9
Sparse Core Ops, SparseCore 0:
  10.7 50.9 all-gather.11
  70.4 53.5 all-gather.7
  126.0 41.3 all-gather.13
  192.4 36.2 all-gather.9

commit v9 on v8

--- a/solution.py
+++ b/solution.py
@@ -76,10 +76,20 @@
     square[...] = total
 
 
-def encode(x, rows, squares, out):
+def encode(x, rows, sources, squares, out, wide, by_layer):
+    wide[...] = x[...].reshape(16 * BLOCK, 128).astype(f32)
     for half in range(2):
+        for layer in range(LAYERS):
+            for r in range(8):
+                at = (half * 8 + r) * BLOCK + layer * 36
+                by_layer[half, layer, r * 36 : r * 36 + 36] = wide[at : at + 36]
+    for half in range(2):
+        tokens = [by_layer[half, layer].astype(bf16) for layer in range(LAYERS)]
         for q in range(4):
-            product = matmul(x[half], rows[q], 0, 0)
+            product = jnp.zeros((128, 384), f32)
+            for layer in range(LAYERS):
+                here = matmul(tokens[layer], rows[q, 0:288], 0, 0)
+                product = product + jnp.where(sources[q : q + 1] == layer, here, 0.0)
             for g in range(4):
                 for c in range(3):
                     at = (q * 3 + c) * 32
@@ -268,15 +278,18 @@
     source_quad = tail[:, 0]
     bias_quad = (tail[:, 1] + tail[:, 2] + tail[:, 3]).reshape(1536)
     square_quad = (tail[:, 4] + tail[:, 5] + tail[:, 6]).reshape(1536)
-    enc_rows = enc_quad[:, :288].reshape(4, 8, 1, 36, 384)
-    pick_quad = source_quad[:, None, :] == layer_ids[None, :, None].astype(f32)
-    enc_rows = jnp.where(pick_quad[:, None, :, None, :], enc_rows, 0).reshape(4, 8, 108, 384)
-    enc_rows = jnp.pad(enc_rows, ((0, 0), (0, 0), (0, BLOCK - 108), (0, 0)))
-    enc_rows = enc_rows.reshape(4, 8 * BLOCK, 384)
-
-    x_quad = share(x_block, "z", 16).reshape(2, 8 * BLOCK, 128)
+    x_quad = share(x_block, "z", 16)
     squares = jnp.pad(square_quad.reshape(12, 128), ((0, 4), (0, 0)))
-    (partial,) = call(encode, x_quad, enc_rows, squares, out=[((8, 400, 128), f32)])
+    x_quad, dec_quad, squares = together((x_quad, dec_quad, squares))
+    (partial,) = call(
+        encode,
+        x_quad,
+        enc_quad,
+        source_quad,
+        squares,
+        out=[((8, 400, 128), f32)],
+        scratch=[pltpu.VMEM((16 * BLOCK, 128), f32), pltpu.VMEM((2, LAYERS, 288, 128), f32)],
+    )
     partial = lax.all_to_all(partial, DP, 0, 0)
     pre, norms, acts, sparsity = call(
         activate,
@@ -284,7 +297,7 @@
         bias_quad.reshape(12, 128),
         out=[((384, 128), f32), ((16, 128), f32), ((8, 384, 128), bf16), ((8, 128), f32)],
     )
-    acts, dec_quad = together((acts, dec_quad))
+    acts, x_sent = together((acts, x_quad))
     acts_quad = lax.all_to_all(acts, DP, 0, 0)
 
     (terms,) = call(decode, dec_quad, acts_quad, out=[((16, BLOCK, 128), bf16)])
@@ -299,7 +312,7 @@
         sparsity,
         out=[((BLOCK, 128), bf16), ((16, BLOCK, 128), bf16)],
     )
-    x_every = lax.all_gather(x_quad, QUAD)
+    x_every = lax.all_gather(x_sent.reshape(2, 8 * BLOCK, 128), QUAD)
     gout, x_every = together((gout, x_every))
     gout_all = lax.all_to_all(gout, "z", 0, 0)
 
@@ -308,11 +321,11 @@
         pull_back, gout_all, dec_quad, out=[((8, 384, 128), bf16), ((8, 128), f32)]
     )
     slopes = lax.all_to_all(slopes, DP, 0, 0)
+    recon = lax.ppermute(recon, ALL, back)
+    slopes, recon = together((slopes, recon))
     (sent,) = call(slopes_of, slopes, pre, norms, loss_z, out=[((8, 112, 128), bf16)])
     got = lax.all_to_all(sent, PLANE, 0, 0)
     (sent,) = call(regroup, got, out=[((4, 784, 128), bf16)])
-    recon = lax.ppermute(recon, ALL, back)
-    sent, recon = together((sent, recon))
     got = lax.all_to_all(sent, "x", 0, 0)
 
     total = pltpu.VMEM((8 * BLOCK, 384), f32)

time: 263 us -> 254 us (0.966)
  the two profiles are of different devices: /device:TPU:16 before, /device:TPU:1 now
where the time goes in v9:
time: 254 us; the launch traced here: 252 us
  blocking collectives  123 us (48%)
  starting transfers between devices  54.5 us (21%)
  waiting for transfers between devices  30.9 us (12%)
  Pallas kernels  15.1 us (6%)
  between operations  14 us (6%)
  local copies, waits for them, and re-layouts  12.2 us (5%)
    all_to_all x1, blocking collectives, on_device(): parts = lax.all_to_all(terms, 'z', 0, 0)  38 us
    all_to_all x1, blocking collectives, on_device(): gout_all = lax.all_to_all(gout, 'z', 0, 0)  31.6 us
    all_to_all x1, starting transfers between devices, share(): lax.all_to_all(jnp.broadcast_to(block[None], (count, *block.shape)), axes...  27.3 us
    all_to_all x1, blocking collectives, on_device(): got = lax.all_to_all(sent, PLANE, 0, 0)  22.7 us
    all_to_all x1, waiting for transfers between devices, on_device(): partial = lax.all_to_all(partial, DP, 0, 0)  16.8 us
    all_gather x1, blocking collectives, on_device(): enc_quad = lax.all_gather(enc_own, QUAD)  16 us
    all_to_all x1, blocking collectives, on_device(): acts_quad = lax.all_to_all(acts, DP, 0, 0)  15.2 us
    pallas_call x10, Pallas kernels, call(): pl.pallas_call(kernel, out_shape=[jax.ShapeDtypeStruct(shape, dtype) for...  15.1 us
  transfers between devices with their start and end apart: 10, of which 5 were waited for; matrix products, arithmetic and copies ran while one was open for 2% of the time, Pallas kernels for 3%

profile of v9, /device:TPU:1, one launch (start us, length us, event | category | flops | bytes accessed | tf_op | source)
XLA Modules:
  0.0 252.4 jit_solution(15541942826368107721)
XLA Ops:
  7.2 0.0 copy-start.16
  7.2 0.0 copy-start.17
  7.2 0.0 all-gather.12.cloned.1.call-start
  7.2 1.3 fusion.3
  8.5 1.1 copy-done.4
  9.6 1.3 shard_map.101
  10.9 0.0 all-gather.12.cloned.1.call-update
  10.9 0.8 maximum_bitcast_fusion
  11.8 4.9 %collective-permute-start = (bf16[2,112,128]{2,1,0:T(8,128)(2,1)S(1)}, bf16[2,112,128]{2,1,0:T(8,128)(2,1)S(1)}, u32[]{:S(2)}, u32[]{:S(2)}) collective-permute-start(bf16[2,112,128]{2,1,0:T(8,128)(2,1)S(1)} %pad.12), channel_id=1, source_target_pairs={{0,0},{1,4},{2,8},{3,12},{4,16},{5,20},{6,24},{7,28},{8,64},{9,68}... | collective-permute-start | bytes 172040 | tf_op jit(solution)/shard_map/ppermute | solution.py:260
  16.7 1.4 collective-permute-done
  18.2 0.6 slice_bitcast_fusion
  18.8 0.8 broadcast_in_dim.5
  19.6 27.3 %all-to-all-start = ((bf16[16,112,128]{2,1,0:T(8,128)(2,1)}), bf16[16,112,128]{2,1,0:T(8,128)(2,1)S(1)}, u32[]{:S(2)}, u32[]{:S(2)}) async-start(bf16[16,112,128]{2,1,0:T(8,128)(2,1)} %broadcast_in_dim.5), calls=%async_computation | async-start | bytes 917504 | tf_op jit(solution)/shard_map/all_to_all | solution.py:42
  46.9 0.0 copy-done.16
  46.9 0.0 copy-done.17
  47.0 0.0 copy-done.15
  47.1 16.0 %all-gather.1 = bf16[1216,384]{1,0:T(8,128)(2,1)S(1)} all-gather(bf16[304,384]{1,0:T(8,128)(2,1)S(1)} %fusion.1), channel_id=3, replica_groups=mesh['x'=4,'yh'=2,'z'=16,'yl'=2,'c'=2] {'yl','c'}, dimensions={0}, use_global_device_ids=true | all-gather | bytes 1167360 | tf_op jit(solution)/shard_map/all_gather | solution.py:275
  63.2 4.4 %all-to-all-done.x = bf16[16,112,128]{2,1,0:T(8,128)(2,1)S(1)} async-done(((bf16[16,112,128]{2,1,0:T(8,128)(2,1)}), bf16[16,112,128]{2,1,0:T(8,128)(2,1)S(1)}, u32[]{:S(2)}, u32[]{:S(2)}) %all-to-all-start) | async-done | bytes 458784 | tf_op jit(solution)/shard_map/all_to_all | solution.py:42
  67.6 3.1 %shard_map.102 = f32[8,400,128]{2,1,0:T(8,128)} custom-call(bf16[16,112,128]{2,1,0:T(8,128)(2,1)S(1)} %all-to-all-done.x, bf16[4,304,384]{2,1,0:T(8,128)(2,1)S(1)} %bitcast.34, f32[4,384]{1,0:T(4,128)S(1)} %get-tuple-element.57.sources, f32[16,128]{1,0:T(8,128)S(1)} %pad.14.squares), custom_call_target="tpu_custom_call" | custom-call | tf_op jit(solution)/shard_map/pallas_call | solution.py:46
  70.7 0.0 copy-done.3
  70.7 4.4 %all-to-all-start.1 = ((f32[8,400,128]{2,1,0:T(8,128)}), f32[8,400,128]{2,1,0:T(8,128)}, u32[]{:S(2)}, u32[]{:S(2)}) async-start(f32[8,400,128]{2,1,0:T(8,128)} %shard_map.102), calls=%async_computation.1 | async-start | bytes 3276800 | tf_op jit(solution)/shard_map/all_to_all | solution.py:293
  75.1 0.0 all-gather.8.cloned.1.call-start
  75.2 0.6 add.45.bias
  75.8 16.8 %all-to-all-done.1.parts = f32[8,400,128]{2,1,0:T(8,128)} async-done(((f32[8,400,128]{2,1,0:T(8,128)}), f32[8,400,128]{2,1,0:T(8,128)}, u32[]{:S(2)}, u32[]{:S(2)}) %all-to-all-start.1) | async-done | bytes 1638432 | tf_op jit(solution)/shard_map/all_to_all | solution.py:293
  92.6 0.7 copy-done.11
  93.3 1.5 shard_map.103
  94.9 0.0 copy-start.8
  94.9 0.7 copy-done.8
  95.5 0.6 copy-done.13
  96.1 0.0 all-gather.8.cloned.1.call-update
  96.2 0.0 all-gather.14.cloned.1.call-start
  96.2 15.2 %all_to_all.40.acts = bf16[8,384,128]{2,1,0:T(8,128)(2,1)} all-to-all(bf16[8,384,128]{2,1,0:T(8,128)(2,1)S(1)} %get-tuple-element.35), channel_id=1, replica_groups=mesh['x'=4,'yh'=2,'z'=16,'yl'=2,'c'=2] {'x','yh'}, dimensions={0} | all-to-all | bytes 1572864 | tf_op jit(solution)/shard_map/all_to_all | solution.py:301
  111.4 0.0 all-gather.14.cloned.1.call-update
  111.4 0.0 all-gather.10.cloned.1.call-start
  111.4 0.0 copy-done
  111.5 1.1 copy-done.1
  112.6 1.6 shard_map.104
  114.2 38.0 %all_to_all.41.parts = bf16[16,112,128]{2,1,0:T(8,128)(2,1)S(1)} all-to-all(bf16[16,112,128]{2,1,0:T(8,128)(2,1)S(1)} %shard_map.104), channel_id=1, replica_groups=mesh['x'=4,'yh'=2,'z'=16,'yl'=2,'c'=2] {'z'}, dimensions={0} | all-to-all | bytes 917504 | tf_op jit(solution)/shard_map/all_to_all | solution.py:304
  152.2 0.0 copy-done.10
  152.2 0.1 shard_map.105
  152.3 0.0 all-gather.8.cloned.1.call-done.blocks
  152.3 31.6 %all_to_all.42.gout = bf16[16,112,128]{2,1,0:T(8,128)(2,1)} all-to-all(bf16[16,112,128]{2,1,0:T(8,128)(2,1)S(1)} %get-tuple-element.40), channel_id=1, replica_groups=mesh['x'=4,'yh'=2,'z'=16,'yl'=2,'c'=2] {'z'}, dimensions={0} | all-to-all | bytes 917504 | tf_op jit(solution)/shard_map/all_to_all | solution.py:317
  183.9 0.0 all-gather.10.cloned.1.call-update
  183.9 1.0 copy-done.2
  184.9 2.2 shard_map.106
  187.1 3.5 %all-to-all-start.5 = ((bf16[8,384,128]{2,1,0:T(8,128)(2,1)}), bf16[8,384,128]{2,1,0:T(8,128)(2,1)S(1)}, u32[]{:S(2)}, u32[]{:S(2)}) async-start(bf16[8,384,128]{2,1,0:T(8,128)(2,1)} %get-tuple-element.41), calls=%async_computation.5 | async-start | bytes 1572864 | tf_op jit(solution)/shard_map/all_to_all | solution.py:323
  190.6 10.3 %collective-permute-start.1 = (bf16[112,128]{1,0:T(8,128)(2,1)S(1)}, bf16[112,128]{1,0:T(8,128)(2,1)S(1)}, u32[]{:S(2)}, u32[]{:S(2)}) collective-permute-start(bf16[112,128]{1,0:T(8,128)(2,1)S(1)} %get-tuple-element.42), channel_id=1, source_target_pairs={{0,0},{4,1},{8,2},{12,3},{16,4},{20,5},{24,6},{28,7},{64,8},{68,9}... | collective-permute-start | bytes 86024 | tf_op jit(solution)/shard_map/ppermute | solution.py:324
  200.9 2.5 %collective-permute-done.1 = bf16[112,128]{1,0:T(8,128)(2,1)S(1)} collective-permute-done((bf16[112,128]{1,0:T(8,128)(2,1)S(1)}, bf16[112,128]{1,0:T(8,128)(2,1)S(1)}, u32[]{:S(2)}, u32[]{:S(2)}) %collective-permute-start.1) | collective-permute-done | bytes 28704 | tf_op jit(solution)/shard_map/ppermute | solution.py:324
  203.5 0.0 all-to-all-done.5.parts
  203.5 0.2 shard_map.107
  203.6 22.7 %all_to_all.43.got = bf16[8,112,128]{2,1,0:T(8,128)(2,1)S(1)} all-to-all(bf16[8,112,128]{2,1,0:T(8,128)(2,1)S(1)} %shard_map.107), channel_id=1, replica_groups=mesh['x'=4,'yh'=2,'z'=16,'yl'=2,'c'=2] {'yh','yl','c'}, dimensions={0} | all-to-all | bytes 458752 | tf_op jit(solution)/shard_map/all_to_all | solution.py:327
  226.4 1.0 shard_map.108
  227.4 3.8 %all-to-all-start.7 = ((bf16[4,784,128]{2,1,0:T(8,128)(2,1)}), bf16[4,784,128]{2,1,0:T(8,128)(2,1)S(1)}, u32[]{:S(2)}, u32[]{:S(2)}) async-start(bf16[4,784,128]{2,1,0:T(8,128)(2,1)} %shard_map.108), calls=%async_computation.7 | async-start | bytes 1605632 | tf_op jit(solution)/shard_map/all_to_all | solution.py:329
  231.3 0.6 reshape.35
  231.9 1.2 constant_dynamic-slice_fusion.1.acts
  233.1 0.0 all-gather.10.cloned.1.call-done.blocks
  233.1 0.0 copy-done.5
  233.1 0.0 copy-start.7
  233.1 1.5 copy-done.7
  234.6 2.2 shard_map.109
  236.9 5.6 %all-to-all-done.7.dpre = bf16[4,784,128]{2,1,0:T(8,128)(2,1)S(1)} async-done(((bf16[4,784,128]{2,1,0:T(8,128)(2,1)}), bf16[4,784,128]{2,1,0:T(8,128)(2,1)S(1)}, u32[]{:S(2)}, u32[]{:S(2)}) %all-to-all-start.7) | async-done | bytes 802848 | tf_op jit(solution)/shard_map/all_to_all | solution.py:329
  242.5 0.0 copy-done.12
  242.5 1.5 copy-done.6
  244.0 1.9 shard_map.110
  (37 shorter events, 0.3 us)
Async XLA Ops:
  7.2 39.7 %copy-start.16 = (s32[384]{0:T(512)S(1)}, s32[384]{0:T(512)}, u32[]{:S(2)}) copy-start(s32[384]{0:T(512)} %param.11) | copy-start | bytes 4612
  7.2 39.8 %copy-start.17 = (f32[384]{0:T(512)S(1)}, f32[384]{0:T(512)}, u32[]{:S(2)}) copy-start(f32[384]{0:T(512)} %param.9) | copy-start | bytes 4612
  7.2 60.4 %all-gather.12.cloned.1.call-start = ((), (), s32[]{:S(2)}) async-start(), calls=%async_computation.10 | async-start | bytes 3440640 | tf_op jit(solution)/shard_map/all_gather | solution.py:276
  8.5 1.1 copy-start.4
  9.6 37.4 %copy-start.15 = (bf16[384,288]{0,1:T(8,128)(2,1)S(1)}, bf16[384,288]{0,1:T(8,128)(2,1)}, u32[]{:S(2)}) copy-start(bf16[384,288]{0,1:T(8,128)(2,1)} %param.8) | copy-start | bytes 663556
  11.8 6.4 %collective-permute-start = (bf16[2,112,128]{2,1,0:T(8,128)(2,1)S(1)}, bf16[2,112,128]{2,1,0:T(8,128)(2,1)S(1)}, u32[]{:S(2)}, u32[]{:S(2)}) collective-permute-start(bf16[2,112,128]{2,1,0:T(8,128)(2,1)S(1)} %pad.12), channel_id=1, source_target_pairs={{0,0},{1,4},{2,8},{3,12},{4,16},{5,20},{6,24},{7,28},{8,64},{9,68}... | collective-permute-start | bytes 172040 | tf_op jit(solution)/shard_map/ppermute | solution.py:260
  19.6 48.0 %all-to-all-start = ((bf16[16,112,128]{2,1,0:T(8,128)(2,1)}), bf16[16,112,128]{2,1,0:T(8,128)(2,1)S(1)}, u32[]{:S(2)}, u32[]{:S(2)}) async-start(bf16[16,112,128]{2,1,0:T(8,128)(2,1)} %broadcast_in_dim.5), calls=%async_computation | async-start | bytes 917504 | tf_op jit(solution)/shard_map/all_to_all | solution.py:42
  67.6 3.1 %copy-start.3 = (bf16[16,112,128]{2,1,0:T(8,128)(2,1)}, bf16[16,112,128]{2,1,0:T(8,128)(2,1)S(1)}, u32[]{:S(2)}) copy-start(bf16[16,112,128]{2,1,0:T(8,128)(2,1)S(1)} %all-to-all-done.x) | copy-start | bytes 1376260
  70.7 21.9 %all-to-all-start.1 = ((f32[8,400,128]{2,1,0:T(8,128)}), f32[8,400,128]{2,1,0:T(8,128)}, u32[]{:S(2)}, u32[]{:S(2)}) async-start(f32[8,400,128]{2,1,0:T(8,128)} %shard_map.102), calls=%async_computation.1 | async-start | bytes 3276800 | tf_op jit(solution)/shard_map/all_to_all | solution.py:293
  75.1 77.2 %all-gather.8.cloned.1.call-start = ((), (), s32[]{:S(2)}) async-start(), calls=%async_computation.8 | async-start | bytes 2293760 | tf_op jit(solution)/shard_map/all_gather | solution.py:315
  75.8 35.6 %copy-start = (bf16[3584,384]{1,0:T(8,128)(2,1)S(1)}, bf16[3584,384]{1,0:T(8,128)(2,1)}, u32[]{:S(2)}) copy-start(bf16[3584,384]{1,0:T(8,128)(2,1)} %all-gather.12.cloned.1.call-done) | copy-start | bytes 8257540
  92.6 0.7 copy-start.11
  94.9 0.7 copy-start.8
  95.5 0.6 copy-start.13
  96.2 135.7 %all-gather.14.cloned.1.call-start = ((), (), s32[]{:S(2)}) async-start(), calls=%async_computation.11 | async-start | bytes 3932160 | tf_op jit(solution)/shard_map/all_gather | solution.py:305
  111.4 121.7 %all-gather.10.cloned.1.call-start = ((), (), s32[]{:S(2)}) async-start(), calls=%async_computation.9 | async-start | bytes 2293760 | tf_op jit(solution)/shard_map/all_gather | solution.py:319
  111.4 1.1 copy-start.1
  112.6 39.6 %copy-start.10 = (bf16[112,128]{1,0:T(8,128)(2,1)S(1)}, bf16[112,128]{1,0:T(8,128)(2,1)}, u32[]{:S(2)}) copy-start(bf16[112,128]{1,0:T(8,128)(2,1)} %get-tuple-element.53.target) | copy-start | bytes 86020
  112.6 39.6 %copy-start.14 = (f32[8,128]{1,0:T(8,128)S(1)}, f32[8,128]{1,0:T(8,128)}, u32[]{:S(2)}) copy-start(f32[8,128]{1,0:T(8,128)} %copy-done.13) | copy-start | bytes 12292
  183.9 1.0 copy-start.2
  184.9 18.6 %copy-start.9 = (f32[384,128]{1,0:T(8,128)S(1)}, f32[384,128]{1,0:T(8,128)}, u32[]{:S(2)}) copy-start(f32[384,128]{1,0:T(8,128)} %copy-done.8) | copy-start | bytes 589828
  187.1 16.4 %all-to-all-start.5 = ((bf16[8,384,128]{2,1,0:T(8,128)(2,1)}), bf16[8,384,128]{2,1,0:T(8,128)(2,1)S(1)}, u32[]{:S(2)}, u32[]{:S(2)}) async-start(bf16[8,384,128]{2,1,0:T(8,128)(2,1)} %get-tuple-element.41), calls=%async_computation.5 | async-start | bytes 1572864 | tf_op jit(solution)/shard_map/all_to_all | solution.py:323
  190.6 12.8 %collective-permute-start.1 = (bf16[112,128]{1,0:T(8,128)(2,1)S(1)}, bf16[112,128]{1,0:T(8,128)(2,1)S(1)}, u32[]{:S(2)}, u32[]{:S(2)}) collective-permute-start(bf16[112,128]{1,0:T(8,128)(2,1)S(1)} %get-tuple-element.42), channel_id=1, source_target_pairs={{0,0},{4,1},{8,2},{12,3},{16,4},{20,5},{24,6},{28,7},{64,8},{68,9}... | collective-permute-start | bytes 86024 | tf_op jit(solution)/shard_map/ppermute | solution.py:324
  227.4 5.7 %copy-start.5 = (bf16[384,3,288]{0,2,1:T(8,128)(2,1)S(1)}, bf16[384,3,288]{0,2,1:T(8,128)(2,1)}, u32[]{:S(2)}) copy-start(bf16[384,3,288]{0,2,1:T(8,128)(2,1)} %param.10) | copy-start | bytes 1990660
  227.4 15.1 %all-to-all-start.7 = ((bf16[4,784,128]{2,1,0:T(8,128)(2,1)}), bf16[4,784,128]{2,1,0:T(8,128)(2,1)S(1)}, u32[]{:S(2)}, u32[]{:S(2)}) async-start(bf16[4,784,128]{2,1,0:T(8,128)(2,1)} %shard_map.108), calls=%async_computation.7 | async-start | bytes 1605632 | tf_op jit(solution)/shard_map/all_to_all | solution.py:329
  233.1 1.5 copy-start.7
  234.6 7.8 %copy-start.12 = (f32[3,384]{1,0:T(4,128)S(1)}, f32[3,384]{1,0:T(4,128)}, u32[]{:S(2)}) copy-start(f32[3,384]{1,0:T(4,128)} %get-tuple-element.58.pick) | copy-start | bytes 13828
  242.5 1.5 copy-start.6
Sparse Core Ops, SparseCore 0:
  11.0 53.1 all-gather.11
  96.3 39.9 all-gather.7
  138.4 46.9 all-gather.13
  187.3 36.4 all-gather.9

commit v10 on v9

--- a/solution.py
+++ b/solution.py
@@ -62,10 +62,15 @@
     return lax.dot_general(a, b, (((left,), (right,)), ((), ())), preferred_element_type=f32)
 
 
-def arrange(dec, reach, out, square, masked, ordered):
+def spread_out(both, out):
+    for z in range(16):
+        out[z] = both[0]
+
+
+def arrange(dec, source, out, square, masked, ordered):
     total = jnp.zeros((1, 384), f32)
     for layer in range(LAYERS):
-        masked[...] = jnp.where(reach[layer : layer + 1] > 0, dec[layer].astype(f32), 0.0)
+        masked[...] = jnp.where(source[...] <= layer, dec[layer].astype(f32), 0.0)
         total = total + jnp.sum(masked[...] * masked[...], axis=0, keepdims=True)
         for r in range(8):
             at = r * BLOCK + layer * 36
@@ -76,7 +81,7 @@
     square[...] = total
 
 
-def encode(x, rows, sources, squares, out, wide, by_layer):
+def encode(x, rows, sources, bias, squares, out, wide, by_layer):
     wide[...] = x[...].reshape(16 * BLOCK, 128).astype(f32)
     for half in range(2):
         for layer in range(LAYERS):
@@ -86,7 +91,7 @@
     for half in range(2):
         tokens = [by_layer[half, layer].astype(bf16) for layer in range(LAYERS)]
         for q in range(4):
-            product = jnp.zeros((128, 384), f32)
+            product = jnp.broadcast_to(bias[q : q + 1] * 0.125, (128, 384))
             for layer in range(LAYERS):
                 here = matmul(tokens[layer], rows[q, 0:288], 0, 0)
                 product = product + jnp.where(sources[q : q + 1] == layer, here, 0.0)
@@ -100,20 +105,19 @@
         out[g, 384:] = squares[...]
 
 
-def activate(parts, bias, pre, norms, acts, sparsity):
+def activate(parts, state, acts):
     total = jnp.sum(parts[...], axis=0)
     norm = jnp.sqrt(total[384:396] + norm_epsilon)
-    norms[0:12] = norm
-    norms[12:16] = jnp.zeros((4, 128), f32)
+    state[0:384] = total[0:384]
+    state[384:396] = norm
+    state[396:400] = jnp.zeros((4, 128), f32)
     weighted = jnp.zeros((32, 128), f32)
     for c in range(12):
-        here = total[c * 32 : c * 32 + 32] + bias[c : c + 1]
-        pre[c * 32 : c * 32 + 32] = here
-        low = jnp.maximum(here, 0.0).astype(bf16)
+        low = jnp.maximum(total[c * 32 : c * 32 + 32], 0.0).astype(bf16)
         weighted = weighted + low.astype(f32) * norm[c : c + 1]
         for g in range(8):
             acts[g, c * 32 : c * 32 + 32] = low
-    sparsity[...] = jnp.broadcast_to(jnp.sum(weighted, axis=0, keepdims=True), (8, 128))
+    state[400:408] = jnp.broadcast_to(jnp.sum(weighted, axis=0, keepdims=True), (8, 128))
 
 
 def tokens_of(ref, half, column):
@@ -132,11 +136,11 @@
             out[half * 8 + r] = low[r * BLOCK : (r + 1) * BLOCK]
 
 
-def compare(parts, target, sparsity, recon, gout):
+def compare(parts, both, state, recon, gout):
     recon_sum = jnp.sum(parts[...].astype(f32), axis=0)
     recon[...] = recon_sum.astype(bf16)
-    error = recon_sum - target[...].astype(f32)
-    by_lane = jnp.sum(error * error, axis=0, keepdims=True) + sparsity_weight * sparsity[0:1]
+    error = recon_sum - both[1].astype(f32)
+    by_lane = jnp.sum(error * error, axis=0, keepdims=True) + sparsity_weight * state[400:401]
     slope = 2.0 * error / TOK_DEV
     row = lax.broadcasted_iota(jnp.int32, (BLOCK, 128), 0)
     for k, piece in enumerate(split(by_lane)):
@@ -170,14 +174,15 @@
     return tail.astype(bf16)
 
 
-def slopes_of(parts, pre, norms, loss, out):
+def slopes_of(parts, state, loss, out):
     total = jnp.sum(parts[...].astype(f32), axis=0)
     for q in range(4):
         sums = []
         for c in range(3):
             k = q * 3 + c
-            slope = total[k * 32 : k * 32 + 32] + (sparsity_weight / TOK_DEV) * norms[k : k + 1]
-            slope = jnp.where(pre[k * 32 : k * 32 + 32] > 0, slope, 0.0)
+            norm = state[384 + k : 385 + k]
+            slope = total[k * 32 : k * 32 + 32] + (sparsity_weight / TOK_DEV) * norm
+            slope = jnp.where(state[k * 32 : k * 32 + 32] > 0, slope, 0.0)
             sums.append(jnp.sum(slope, axis=0, keepdims=True))
             for yh in range(2):
                 out[yh * 4 + q, c * 32 : c * 32 + 32] = slope.astype(bf16)
@@ -206,7 +211,7 @@
     return total
 
 
-def decoder_gradient(blocks, acts, rows, norms, reach, out, total):
+def decoder_gradient(blocks, acts, rows, norms, source, out, total):
     def values(half, q, c):
         here = acts[q, half * 4 : half * 4 + 4, c * 32 : c * 32 + 32]
         return here.reshape(128, 128)
@@ -222,10 +227,10 @@
             at = r * BLOCK + layer * 36
             out[layer, r * 36 : r * 36 + 36] = total[at : at + 36]
         whole = out[layer] + pull * rows[layer].astype(f32)
-        out[layer] = jnp.where(reach[layer : layer + 1] > 0, whole, 0.0)
-
-
-def encoder_gradient(blocks, dpre, pick, out, bias, loss, total):
+        out[layer] = jnp.where(source[...] <= layer, whole, 0.0)
+
+
+def encoder_gradient(blocks, dpre, source, out, bias, loss, total):
     def values(half, q, c):
         parts = [
             dpre[half * 2 + g // 2, pl.ds(((g % 2) * 4 + q) * 96 + c * 32, 32)] for g in range(4)
@@ -237,7 +242,7 @@
         own = jnp.zeros((36, 384), f32)
         for layer in range(LAYERS):
             at = r * BLOCK + layer * 36
-            own = own + jnp.where(pick[layer : layer + 1] > 0, total[at : at + 36], 0.0)
+            own = own + jnp.where(source[...] == layer, total[at : at + 36], 0.0)
         out[r * 36 : r * 36 + 36] = own
     tail = jnp.sum(dpre[:, 768:784].astype(f32), axis=0)
     tail = tail[0:4] + tail[4:8] + tail[8:12]
@@ -251,22 +256,18 @@
 def on_device(resid, target, enc_weight, enc_bias, dec_weight, source):
     to = spread()
     back = [(d, s) for s, d in to]
-    layer_ids = jnp.arange(LAYERS, dtype=jnp.int32)
-    pick = source[None, :] == layer_ids[:, None]
-    reach = source[None, :] <= layer_ids[:, None]
+    source_row = source[None]
 
     both = jnp.stack([resid, target]).transpose(0, 2, 3, 1).reshape(2, 108, 128)
     both = jnp.pad(both, ((0, 0), (0, BLOCK - 108), (0, 0)))
     both = lax.ppermute(both, ALL, to)
-    x_block, target_block = both[0], both[1]
 
     enc_t = enc_weight.T
     dec_t = dec_weight.transpose(1, 2, 0)
-    reach_wide = reach.astype(f32)
     dec_own, square = call(
         arrange,
         dec_t,
-        reach_wide,
+        source_row,
         out=[((8 * BLOCK, 384), bf16), ((1, 384), f32)],
         scratch=[pltpu.VMEM((288, 384), f32), pltpu.VMEM((8 * BLOCK, 384), f32)],
     )
@@ -276,9 +277,10 @@
     dec_quad = lax.all_gather(dec_own, QUAD)
     tail = enc_quad[:, 288:295].astype(f32)
     source_quad = tail[:, 0]
-    bias_quad = (tail[:, 1] + tail[:, 2] + tail[:, 3]).reshape(1536)
+    bias_quad = tail[:, 1] + tail[:, 2] + tail[:, 3]
     square_quad = (tail[:, 4] + tail[:, 5] + tail[:, 6]).reshape(1536)
-    x_quad = share(x_block, "z", 16)
+    (x_sent,) = call(spread_out, both, out=[((16, BLOCK, 128), bf16)])
+    x_quad = lax.all_to_all(x_sent, "z", 0, 0)
     squares = jnp.pad(square_quad.reshape(12, 128), ((0, 4), (0, 0)))
     x_quad, dec_quad, squares = together((x_quad, dec_quad, squares))
     (partial,) = call(
@@ -286,16 +288,14 @@
         x_quad,
         enc_quad,
         source_quad,
+        bias_quad,
         squares,
         out=[((8, 400, 128), f32)],
         scratch=[pltpu.VMEM((16 * BLOCK, 128), f32), pltpu.VMEM((2, LAYERS, 288, 128), f32)],
     )
     partial = lax.all_to_all(partial, DP, 0, 0)
-    pre, norms, acts, sparsity = call(
-        activate,
-        partial,
-        bias_quad.reshape(12, 128),
-        out=[((384, 128), f32), ((16, 128), f32), ((8, 384, 128), bf16), ((8, 128), f32)],
+    state, acts = call(
+        activate, partial, out=[((408, 128), f32), ((8, 384, 128), bf16)]
     )
     acts, x_sent = together((acts, x_quad))
     acts_quad = lax.all_to_all(acts, DP, 0, 0)
@@ -308,8 +308,8 @@
     recon, gout = call(
         compare,
         parts,
-        target_block,
-        sparsity,
+        both,
+        state,
         out=[((BLOCK, 128), bf16), ((16, BLOCK, 128), bf16)],
     )
     x_every = lax.all_gather(x_sent.reshape(2, 8 * BLOCK, 128), QUAD)
@@ -321,22 +321,20 @@
         pull_back, gout_all, dec_quad, out=[((8, 384, 128), bf16), ((8, 128), f32)]
     )
     slopes = lax.all_to_all(slopes, DP, 0, 0)
-    recon = lax.ppermute(recon, ALL, back)
-    slopes, recon = together((slopes, recon))
-    (sent,) = call(slopes_of, slopes, pre, norms, loss_z, out=[((8, 112, 128), bf16)])
+    (sent,) = call(slopes_of, slopes, state, loss_z, out=[((8, 112, 128), bf16)])
     got = lax.all_to_all(sent, PLANE, 0, 0)
     (sent,) = call(regroup, got, out=[((4, 784, 128), bf16)])
     got = lax.all_to_all(sent, "x", 0, 0)
 
     total = pltpu.VMEM((8 * BLOCK, 384), f32)
-    own_norms = lax.dynamic_index_in_dim(norms[:12].reshape(4, 384), member, 0, True)
+    own_norms = lax.dynamic_index_in_dim(state[384:396].reshape(4, 384), member, 0, True)
     (dec_grad,) = call(
         decoder_gradient,
         gout_every,
         acts_every,
         dec_t,
         own_norms,
-        reach_wide,
+        source_row,
         out=[((LAYERS, 288, 384), f32)],
         scratch=[total],
     )
@@ -345,10 +343,12 @@
         encoder_gradient,
         x_every,
         got,
-        pick.astype(f32),
+        source_row,
         out=[((288, 384), f32), ((3, 128), f32), ((1, 1), f32)],
         scratch=[total],
     )
+    recon = lax.ppermute(recon, ALL, back)
+    recon, enc_grad = together((recon, enc_grad))
     recon = recon[:108].reshape(3, 36, 128).transpose(2, 0, 1)
     return (loss[0, 0], recon, enc_grad.T, bias_grad.reshape(384), dec_grad.transpose(2, 0, 1))
 

time: 254 us -> 244 us (0.961); the launches traced: 252 us -> 240 us
  blocking collectives: 123 us -> 154 us
  waiting for transfers between devices: 30.9 us -> 7.99 us
  starting transfers between devices: 54.5 us -> 40.4 us
  Pallas kernels: 15.1 us -> 12.5 us
    all_to_all x0 -> x2, blocking collectives: none -> 33.6 us  [the longest x1 20.2 us: on_device(): partial = lax.all_to_all(partial, DP, 0, 0)]
    all_to_all x3 -> x1, waiting for transfers between devices: 21.2 us -> 4.38 us  [on_device(): x_quad = lax.all_to_all(x_sent, 'z', 0, 0)]
    all_to_all x3 -> x1, starting transfers between devices: 35.3 us -> 27.3 us  [on_device(): x_quad = lax.all_to_all(x_sent, 'z', 0, 0)]
    ppermute x1, starting transfers between devices: 10.3 us -> 4.4 us  [on_device(): recon = lax.ppermute(recon, ALL, back)]
    all_to_all x1, waiting for transfers between devices: 5.59 us -> 2.06 us  [on_device(): got = lax.all_to_all(sent, 'x', 0, 0)]
    all_to_all x1, blocking collectives: 22.7 us -> 19.8 us  [on_device(): got = lax.all_to_all(sent, PLANE, 0, 0)]
    pallas_call x10 -> x11, Pallas kernels: 15.1 us -> 12.5 us  [call(): pl.pallas_call(kernel, out_shape=[jax.ShapeDtypeStruct(shape, dtype) for...]
    ppermute x1, waiting for transfers between devices: 2.55 us -> 0.01 us  [on_device(): recon = lax.ppermute(recon, ALL, back)]
  transfers between devices with their start and end apart: 10 -> 8, of which waited for: 5 -> 3; matrix products, arithmetic and copies ran while one was open for 2% -> 1% of each run, Pallas kernels for 3% -> 4%
where the time goes in v10:
time: 244 us; the launch traced here: 240 us
  blocking collectives  154 us (63%)
  starting transfers between devices  40.4 us (17%)
  between operations  14.1 us (6%)
  Pallas kernels  12.5 us (5%)
  local copies, waits for them, and re-layouts  9.8 us (4%)
  waiting for transfers between devices  7.99 us (3%)
    all_to_all x1, blocking collectives, on_device(): parts = lax.all_to_all(terms, 'z', 0, 0)  37.5 us
    all_to_all x1, blocking collectives, on_device(): gout_all = lax.all_to_all(gout, 'z', 0, 0)  32.8 us
    all_to_all x1, starting transfers between devices, on_device(): x_quad = lax.all_to_all(x_sent, 'z', 0, 0)  27.3 us
    all_to_all x1, blocking collectives, on_device(): partial = lax.all_to_all(partial, DP, 0, 0)  20.2 us
    all_to_all x1, blocking collectives, on_device(): got = lax.all_to_all(sent, PLANE, 0, 0)  19.8 us
    all_gather x1, blocking collectives, on_device(): enc_quad = lax.all_gather(enc_own, QUAD)  16 us
    all_to_all x1, blocking collectives, on_device(): acts_quad = lax.all_to_all(acts, DP, 0, 0)  14.5 us
    all_to_all x1, blocking collectives, on_device(): slopes = lax.all_to_all(slopes, DP, 0, 0)  13.4 us
  transfers between devices with their start and end apart: 8, of which 3 were waited for; matrix products, arithmetic and copies ran while one was open for 1% of the time, Pallas kernels for 4%

profile of v10, /device:TPU:1, one launch (start us, length us, event | category | flops | bytes accessed | tf_op | source)
XLA Modules:
  0.0 239.8 jit_solution(4621533423076242000)
XLA Ops:
  7.2 0.0 copy-start.10
  7.2 0.0 copy-start.11
  7.2 0.0 all-gather.12.cloned.1.call-start
  7.2 0.7 broadcast_in_dim.3.source
  7.9 0.0 copy-start.4
  7.9 1.1 copy-done.4
  9.0 0.0 copy-start.9
  9.0 1.3 shard_map.102
  10.3 0.0 all-gather.12.cloned.1.call-update
  10.3 0.8 maximum_bitcast_fusion
  11.2 4.9 %collective-permute-start = (bf16[2,112,128]{2,1,0:T(8,128)(2,1)S(1)}, bf16[2,112,128]{2,1,0:T(8,128)(2,1)S(1)}, u32[]{:S(2)}, u32[]{:S(2)}) collective-permute-start(bf16[2,112,128]{2,1,0:T(8,128)(2,1)S(1)} %pad.12), channel_id=1, source_target_pairs={{0,0},{1,4},{2,8},{3,12},{4,16},{5,20},{6,24},{7,28},{8,64},{9,68}... | collective-permute-start | bytes 172040 | tf_op jit(solution)/shard_map/ppermute | solution.py:263
  16.1 1.4 collective-permute-done.both
  17.6 0.8 shard_map.101
  18.4 27.3 %all-to-all-start = ((bf16[16,112,128]{2,1,0:T(8,128)(2,1)}), bf16[16,112,128]{2,1,0:T(8,128)(2,1)S(1)}, u32[]{:S(2)}, u32[]{:S(2)}) async-start(bf16[16,112,128]{2,1,0:T(8,128)(2,1)} %shard_map.101), calls=%async_computation | async-start | bytes 917504 | tf_op jit(solution)/shard_map/all_to_all | solution.py:283
  45.7 0.0 all-gather.8.cloned.1.call-start
  45.7 0.0 copy-done.10
  45.8 0.0 copy-done.11
  45.9 0.0 copy-done.9
  45.9 16.0 %all-gather.1 = bf16[1216,384]{1,0:T(8,128)(2,1)S(1)} all-gather(bf16[304,384]{1,0:T(8,128)(2,1)S(1)} %fusion.1), channel_id=3, replica_groups=mesh['x'=4,'yh'=2,'z'=16,'yl'=2,'c'=2] {'yl','c'}, dimensions={0}, use_global_device_ids=true | all-gather | bytes 1167360 | tf_op jit(solution)/shard_map/all_gather | solution.py:276
  62.0 4.4 %all-to-all-done.x = bf16[16,112,128]{2,1,0:T(8,128)(2,1)S(1)} async-done(((bf16[16,112,128]{2,1,0:T(8,128)(2,1)}), bf16[16,112,128]{2,1,0:T(8,128)(2,1)S(1)}, u32[]{:S(2)}, u32[]{:S(2)}) %all-to-all-start) | async-done | bytes 458784 | tf_op jit(solution)/shard_map/all_to_all | solution.py:283
  66.4 0.0 copy-start.3
  66.4 0.0 all-gather.12.cloned.1.call-done
  66.4 1.9 shard_map.103
  68.3 20.2 %all_to_all.40.parts = f32[8,400,128]{2,1,0:T(8,128)S(1)} all-to-all(f32[8,400,128]{2,1,0:T(8,128)S(1)} %shard_map.103), channel_id=1, replica_groups=mesh['x'=4,'yh'=2,'z'=16,'yl'=2,'c'=2] {'x','yh'}, dimensions={0} | all-to-all | bytes 3276800 | tf_op jit(solution)/shard_map/all_to_all | solution.py:296
  88.5 0.0 copy-done.3
  88.5 0.0 copy-start
  88.5 0.1 shard_map.104
  88.7 0.0 copy-start.8
  88.7 0.9 copy-done.8
  89.6 0.0 all-gather.8.cloned.1.call-update
  89.6 0.0 all-gather.14.cloned.1.call-start
  89.6 14.5 %all_to_all.41.acts = bf16[8,384,128]{2,1,0:T(8,128)(2,1)} all-to-all(bf16[8,384,128]{2,1,0:T(8,128)(2,1)} %copy-done.8), channel_id=1, replica_groups=mesh['x'=4,'yh'=2,'z'=16,'yl'=2,'c'=2] {'x','yh'}, dimensions={0} | all-to-all | bytes 1572864 | tf_op jit(solution)/shard_map/all_to_all | solution.py:301
  104.1 0.0 all-gather.14.cloned.1.call-update
  104.1 0.0 all-gather.10.cloned.1.call-start
  104.2 0.0 copy-done
  104.2 0.0 copy-start.1
  104.2 1.1 copy-done.1
  105.3 1.6 shard_map.105
  106.9 37.5 %all_to_all.42.parts = bf16[16,112,128]{2,1,0:T(8,128)(2,1)S(1)} all-to-all(bf16[16,112,128]{2,1,0:T(8,128)(2,1)S(1)} %shard_map.105), channel_id=1, replica_groups=mesh['x'=4,'yh'=2,'z'=16,'yl'=2,'c'=2] {'z'}, dimensions={0} | all-to-all | bytes 917504 | tf_op jit(solution)/shard_map/all_to_all | solution.py:304
  144.5 0.1 shard_map.106
  144.6 0.0 all-gather.8.cloned.1.call-done.blocks
  144.6 32.8 %all_to_all.43.gout = bf16[16,112,128]{2,1,0:T(8,128)(2,1)} all-to-all(bf16[16,112,128]{2,1,0:T(8,128)(2,1)S(1)} %get-tuple-element.38), channel_id=1, replica_groups=mesh['x'=4,'yh'=2,'z'=16,'yl'=2,'c'=2] {'z'}, dimensions={0} | all-to-all | bytes 917504 | tf_op jit(solution)/shard_map/all_to_all | solution.py:317
  177.4 0.0 all-gather.10.cloned.1.call-update
  177.4 0.0 copy-start.2
  177.4 1.0 copy-done.2
  178.4 1.3 shard_map.107
  179.7 13.4 %all_to_all.44.parts = bf16[8,384,128]{2,1,0:T(8,128)(2,1)S(1)} all-to-all(bf16[8,384,128]{2,1,0:T(8,128)(2,1)S(1)} %get-tuple-element.39), channel_id=1, replica_groups=mesh['x'=4,'yh'=2,'z'=16,'yl'=2,'c'=2] {'x','yh'}, dimensions={0} | all-to-all | bytes 1572864 | tf_op jit(solution)/shard_map/all_to_all | solution.py:323
  193.1 0.2 shard_map.108
  193.3 19.8 %all_to_all.45.got = bf16[8,112,128]{2,1,0:T(8,128)(2,1)S(1)} all-to-all(bf16[8,112,128]{2,1,0:T(8,128)(2,1)S(1)} %shard_map.108), channel_id=1, replica_groups=mesh['x'=4,'yh'=2,'z'=16,'yl'=2,'c'=2] {'yh','yl','c'}, dimensions={0} | all-to-all | bytes 458752 | tf_op jit(solution)/shard_map/all_to_all | solution.py:325
  213.1 1.0 shard_map.109
  214.1 3.6 %all-to-all-start.7 = ((bf16[4,784,128]{2,1,0:T(8,128)(2,1)}), bf16[4,784,128]{2,1,0:T(8,128)(2,1)S(1)}, u32[]{:S(2)}, u32[]{:S(2)}) async-start(bf16[4,784,128]{2,1,0:T(8,128)(2,1)} %shard_map.109), calls=%async_computation.7 | async-start | bytes 1605632 | tf_op jit(solution)/shard_map/all_to_all | solution.py:327
  217.7 4.4 %collective-permute-start.1 = (bf16[112,128]{1,0:T(8,128)(2,1)S(1)}, bf16[112,128]{1,0:T(8,128)(2,1)S(1)}, u32[]{:S(2)}, u32[]{:S(2)}) collective-permute-start(bf16[112,128]{1,0:T(8,128)(2,1)S(1)} %get-tuple-element.43), channel_id=1, source_target_pairs={{0,0},{4,1},{8,2},{12,3},{16,4},{20,5},{24,6},{28,7},{64,8},{68,9}... | collective-permute-start | bytes 86024 | tf_op jit(solution)/shard_map/ppermute | solution.py:350
  222.2 0.0 all-gather.14.cloned.1.call-done
  222.2 1.2 constant_dynamic-slice_fusion.1.acts
  223.4 0.0 all-gather.10.cloned.1.call-done.blocks
  223.4 0.0 copy-done.5
  223.4 0.0 copy-start.6
  223.4 1.5 copy-done.6
  224.9 2.2 shard_map.110
  227.2 2.1 all-to-all-done.7.dpre
  229.2 1.5 copy-done.7
  230.7 1.9 shard_map.111
  232.6 0.0 collective-permute-done.1
  232.7 0.6 reshape.31
  (22 shorter events, 0.2 us)
Async XLA Ops:
  7.2 38.6 %copy-start.10 = (s32[384]{0:T(512)S(1)}, s32[384]{0:T(512)}, u32[]{:S(2)}) copy-start(s32[384]{0:T(512)} %param.11) | copy-start | bytes 4612
  7.2 38.6 %copy-start.11 = (f32[384]{0:T(512)S(1)}, f32[384]{0:T(512)}, u32[]{:S(2)}) copy-start(f32[384]{0:T(512)} %param.9) | copy-start | bytes 4612
  7.2 59.2 %all-gather.12.cloned.1.call-start = ((), (), s32[]{:S(2)}) async-start(), calls=%async_computation.10 | async-start | bytes 3440640 | tf_op jit(solution)/shard_map/all_gather | solution.py:277
  7.9 1.1 copy-start.4
  9.0 36.9 %copy-start.9 = (bf16[384,288]{0,1:T(8,128)(2,1)S(1)}, bf16[384,288]{0,1:T(8,128)(2,1)}, u32[]{:S(2)}) copy-start(bf16[384,288]{0,1:T(8,128)(2,1)} %param.8) | copy-start | bytes 663556
  11.2 6.4 %collective-permute-start = (bf16[2,112,128]{2,1,0:T(8,128)(2,1)S(1)}, bf16[2,112,128]{2,1,0:T(8,128)(2,1)S(1)}, u32[]{:S(2)}, u32[]{:S(2)}) collective-permute-start(bf16[2,112,128]{2,1,0:T(8,128)(2,1)S(1)} %pad.12), channel_id=1, source_target_pairs={{0,0},{1,4},{2,8},{3,12},{4,16},{5,20},{6,24},{7,28},{8,64},{9,68}... | collective-permute-start | bytes 172040 | tf_op jit(solution)/shard_map/ppermute | solution.py:263
  18.4 48.0 %all-to-all-start = ((bf16[16,112,128]{2,1,0:T(8,128)(2,1)}), bf16[16,112,128]{2,1,0:T(8,128)(2,1)S(1)}, u32[]{:S(2)}, u32[]{:S(2)}) async-start(bf16[16,112,128]{2,1,0:T(8,128)(2,1)} %shard_map.101), calls=%async_computation | async-start | bytes 917504 | tf_op jit(solution)/shard_map/all_to_all | solution.py:283
  45.7 98.9 %all-gather.8.cloned.1.call-start = ((), (), s32[]{:S(2)}) async-start(), calls=%async_computation.8 | async-start | bytes 2293760 | tf_op jit(solution)/shard_map/all_gather | solution.py:315
  66.4 22.1 %copy-start.3 = (bf16[16,112,128]{2,1,0:T(8,128)(2,1)}, bf16[16,112,128]{2,1,0:T(8,128)(2,1)S(1)}, u32[]{:S(2)}) copy-start(bf16[16,112,128]{2,1,0:T(8,128)(2,1)S(1)} %all-to-all-done.x) | copy-start | bytes 1376260
  88.5 15.6 %copy-start = (bf16[3584,384]{1,0:T(8,128)(2,1)S(1)}, bf16[3584,384]{1,0:T(8,128)(2,1)}, u32[]{:S(2)}) copy-start(bf16[3584,384]{1,0:T(8,128)(2,1)} %all-gather.12.cloned.1.call-done) | copy-start | bytes 8257540
  88.7 0.9 copy-start.8
  89.6 132.6 %all-gather.14.cloned.1.call-start = ((), (), s32[]{:S(2)}) async-start(), calls=%async_computation.11 | async-start | bytes 3932160 | tf_op jit(solution)/shard_map/all_gather | solution.py:305
  104.1 119.3 %all-gather.10.cloned.1.call-start = ((), (), s32[]{:S(2)}) async-start(), calls=%async_computation.9 | async-start | bytes 2293760 | tf_op jit(solution)/shard_map/all_gather | solution.py:319
  104.2 1.1 copy-start.1
  177.4 1.0 copy-start.2
  214.1 9.4 %copy-start.5 = (bf16[384,3,288]{0,2,1:T(8,128)(2,1)S(1)}, bf16[384,3,288]{0,2,1:T(8,128)(2,1)}, u32[]{:S(2)}) copy-start(bf16[384,3,288]{0,2,1:T(8,128)(2,1)} %param.10) | copy-start | bytes 1990660
  214.1 15.2 %all-to-all-start.7 = ((bf16[4,784,128]{2,1,0:T(8,128)(2,1)}), bf16[4,784,128]{2,1,0:T(8,128)(2,1)S(1)}, u32[]{:S(2)}, u32[]{:S(2)}) async-start(bf16[4,784,128]{2,1,0:T(8,128)(2,1)} %shard_map.109), calls=%async_computation.7 | async-start | bytes 1605632 | tf_op jit(solution)/shard_map/all_to_all | solution.py:327
  217.7 14.9 %collective-permute-start.1 = (bf16[112,128]{1,0:T(8,128)(2,1)S(1)}, bf16[112,128]{1,0:T(8,128)(2,1)S(1)}, u32[]{:S(2)}, u32[]{:S(2)}) collective-permute-start(bf16[112,128]{1,0:T(8,128)(2,1)S(1)} %get-tuple-element.43), channel_id=1, source_target_pairs={{0,0},{4,1},{8,2},{12,3},{16,4},{20,5},{24,6},{28,7},{64,8},{68,9}... | collective-permute-start | bytes 86024 | tf_op jit(solution)/shard_map/ppermute | solution.py:350
  223.4 1.5 copy-start.6
  229.2 1.5 copy-start.7
Sparse Core Ops, SparseCore 0:
  10.7 53.1 all-gather.11
  89.7 41.3 all-gather.7
  133.2 45.8 all-gather.13
  181.1 37.7 all-gather.9

commit v11 on v10

--- a/solution.py
+++ b/solution.py
@@ -42,10 +42,18 @@
     return lax.all_to_all(jnp.broadcast_to(block[None], (count, *block.shape)), axes, 0, 0)
 
 
-def call(kernel, *args, out, scratch=()):
+def call(kernel, *args, out, far=(), scratch=()):
+    inside = pl.BlockSpec(memory_space=pltpu.VMEM)
+    outside = pl.BlockSpec(memory_space=pltpu.HBM)
+    shapes = [
+        pltpu.HBM(shape, dtype) if k in far else jax.ShapeDtypeStruct(shape, dtype)
+        for k, (shape, dtype) in enumerate(out)
+    ]
     return pl.pallas_call(
         kernel,
-        out_shape=[jax.ShapeDtypeStruct(shape, dtype) for shape, dtype in out],
+        in_specs=[inside] * len(args),
+        out_specs=[outside if k in far else inside for k in range(len(out))],
+        out_shape=shapes,
         scratch_shapes=scratch,
         compiler_params=pltpu.CompilerParams(vmem_limit_bytes=40 * 1024 * 1024),
     )(*args)
@@ -81,7 +89,9 @@
     square[...] = total
 
 
-def encode(x, rows, sources, bias, squares, out, wide, by_layer):
+def encode(x, rows, sources, bias, squares, out, kept, wide, by_layer, sem):
+    copy = pltpu.make_async_copy(x, kept, sem)
+    copy.start()
     wide[...] = x[...].reshape(16 * BLOCK, 128).astype(f32)
     for half in range(2):
         for layer in range(LAYERS):
@@ -103,28 +113,35 @@
                     ]
     for g in range(8):
         out[g, 384:] = squares[...]
-
-
-def activate(parts, state, acts):
+    copy.wait()
+
+
+def activate(parts, far_state, acts, state, sem):
     total = jnp.sum(parts[...], axis=0)
     norm = jnp.sqrt(total[384:396] + norm_epsilon)
     state[0:384] = total[0:384]
     state[384:396] = norm
     state[396:400] = jnp.zeros((4, 128), f32)
+    lows = [jnp.maximum(total[c * 32 : c * 32 + 32], 0.0).astype(bf16) for c in range(12)]
     weighted = jnp.zeros((32, 128), f32)
     for c in range(12):
-        low = jnp.maximum(total[c * 32 : c * 32 + 32], 0.0).astype(bf16)
-        weighted = weighted + low.astype(f32) * norm[c : c + 1]
+        weighted = weighted + lows[c].astype(f32) * norm[c : c + 1]
+    state[400:408] = jnp.broadcast_to(jnp.sum(weighted, axis=0, keepdims=True), (8, 128))
+    copy = pltpu.make_async_copy(state, far_state, sem)
+    copy.start()
+    for c in range(12):
         for g in range(8):
-            acts[g, c * 32 : c * 32 + 32] = low
-    state[400:408] = jnp.broadcast_to(jnp.sum(weighted, axis=0, keepdims=True), (8, 128))
+            acts[g, c * 32 : c * 32 + 32] = lows[c]
+    copy.wait()
 
 
 def tokens_of(ref, half, column):
     return ref[half * 4 : half * 4 + 4, column * 32 : column * 32 + 32].reshape(128, 128)
 
 
-def decode(rows, acts, out):
+def decode(rows, acts, out, kept, sem):
+    copy = pltpu.make_async_copy(acts, kept, sem)
+    copy.start()
     for half in range(2):
         total = None
         for q in range(4):
@@ -134,6 +151,7 @@
         low = total.astype(bf16)
         for r in range(8):
             out[half * 8 + r] = low[r * BLOCK : (r + 1) * BLOCK]
+    copy.wait()
 
 
 def compare(parts, both, state, recon, gout):
@@ -150,7 +168,9 @@
         gout[z] = low
 
 
-def pull_back(gout, rows, out, loss):
+def pull_back(gout, rows, out, loss, kept, sem):
+    copy = pltpu.make_async_copy(gout, kept, sem)
+    copy.start()
     total = jnp.sum(gout[:, 96:112].astype(f32), axis=0)
     loss[...] = jnp.broadcast_to(jnp.sum(total[12:15], axis=0, keepdims=True), (8, 128))
     for half in range(2):
@@ -163,6 +183,7 @@
                     out[half * 4 + g, at : at + 32] = product[
                         g * 32 : g * 32 + 32, c * 128 : c * 128 + 128
                     ]
+    copy.wait()
 
 
 def tail_of(values):
@@ -283,26 +304,42 @@
     x_quad = lax.all_to_all(x_sent, "z", 0, 0)
     squares = jnp.pad(square_quad.reshape(12, 128), ((0, 4), (0, 0)))
     x_quad, dec_quad, squares = together((x_quad, dec_quad, squares))
-    (partial,) = call(
+    partial, x_kept = call(
         encode,
         x_quad,
         enc_quad,
         source_quad,
         bias_quad,
         squares,
-        out=[((8, 400, 128), f32)],
-        scratch=[pltpu.VMEM((16 * BLOCK, 128), f32), pltpu.VMEM((2, LAYERS, 288, 128), f32)],
+        out=[((8, 400, 128), f32), ((16, BLOCK, 128), bf16)],
+        far=(1,),
+        scratch=[
+            pltpu.VMEM((16 * BLOCK, 128), f32),
+            pltpu.VMEM((2, LAYERS, 288, 128), f32),
+            pltpu.SemaphoreType.DMA,
+        ],
     )
     partial = lax.all_to_all(partial, DP, 0, 0)
     state, acts = call(
-        activate, partial, out=[((408, 128), f32), ((8, 384, 128), bf16)]
-    )
-    acts, x_sent = together((acts, x_quad))
+        activate,
+        partial,
+        out=[((408, 128), f32), ((8, 384, 128), bf16)],
+        far=(0,),
+        scratch=[pltpu.VMEM((408, 128), f32), pltpu.SemaphoreType.DMA],
+    )
+    acts, x_sent = together((acts, x_kept))
     acts_quad = lax.all_to_all(acts, DP, 0, 0)
 
-    (terms,) = call(decode, dec_quad, acts_quad, out=[((16, BLOCK, 128), bf16)])
+    terms, acts_kept = call(
+        decode,
+        dec_quad,
+        acts_quad,
+        out=[((16, BLOCK, 128), bf16), ((8, 384, 128), bf16)],
+        far=(1,),
+        scratch=[pltpu.SemaphoreType.DMA],
+    )
     parts = lax.all_to_all(terms, "z", 0, 0)
-    acts_every = lax.all_gather(acts_quad, QUAD)
+    acts_every = lax.all_gather(acts_kept, QUAD)
     member = lax.axis_index(QUAD)
     acts_every = lax.dynamic_slice_in_dim(acts_every, member * 96, 96, 2)
     recon, gout = call(
@@ -316,10 +353,15 @@
     gout, x_every = together((gout, x_every))
     gout_all = lax.all_to_all(gout, "z", 0, 0)
 
-    gout_every = lax.all_gather(gout_all.reshape(2, 8 * BLOCK, 128), QUAD)
-    slopes, loss_z = call(
-        pull_back, gout_all, dec_quad, out=[((8, 384, 128), bf16), ((8, 128), f32)]
-    )
+    slopes, loss_z, gout_kept = call(
+        pull_back,
+        gout_all,
+        dec_quad,
+        out=[((8, 384, 128), bf16), ((8, 128), f32), ((16, BLOCK, 128), bf16)],
+        far=(2,),
+        scratch=[pltpu.SemaphoreType.DMA],
+    )
+    gout_every = lax.all_gather(gout_kept.reshape(2, 8 * BLOCK, 128), QUAD)
     slopes = lax.all_to_all(slopes, DP, 0, 0)
     (sent,) = call(slopes_of, slopes, state, loss_z, out=[((8, 112, 128), bf16)])
     got = lax.all_to_all(sent, PLANE, 0, 0)

time: 244 us -> 241 us (0.988)
  no operation moved by 1% of the time
where the time goes in v11:
time: 241 us; the launch traced here: 238 us
  blocking collectives  153 us (63%)
  starting transfers between devices  40.4 us (17%)
  between operations  14.1 us (6%)
  Pallas kernels  13.1 us (5%)
  local copies, waits for them, and re-layouts  8.29 us (3%)
  waiting for transfers between devices  7.94 us (3%)
    all_to_all x1, blocking collectives, on_device(): parts = lax.all_to_all(terms, 'z', 0, 0)  37.3 us
    all_to_all x1, blocking collectives, on_device(): gout_all = lax.all_to_all(gout, 'z', 0, 0)  32.7 us
    all_to_all x1, starting transfers between devices, on_device(): x_quad = lax.all_to_all(x_sent, 'z', 0, 0)  27.3 us
    all_to_all x1, blocking collectives, on_device(): partial = lax.all_to_all(partial, DP, 0, 0)  20.2 us
    all_to_all x1, blocking collectives, on_device(): got = lax.all_to_all(sent, PLANE, 0, 0)  19.8 us
    all_gather x1, blocking collectives, on_device(): enc_quad = lax.all_gather(enc_own, QUAD)  16 us
    all_to_all x1, blocking collectives, on_device(): slopes = lax.all_to_all(slopes, DP, 0, 0)  14.3 us
    pallas_call x11, Pallas kernels, call(): pl.pallas_call(kernel, in_specs=[inside] * len(args), out_specs=[outside...  13.1 us
  transfers between devices with their start and end apart: 8, of which 3 were waited for; matrix products, arithmetic and copies ran while one was open for 1% of the time, Pallas kernels for 4%

profile of v11, /device:TPU:1, one launch (start us, length us, event | category | flops | bytes accessed | tf_op | source)
XLA Modules:
  0.0 237.7 jit_solution(3104661516825843187)
XLA Ops:
  7.2 0.0 copy-start.10
  7.2 0.0 copy-start.11
  7.2 0.0 all-gather.12.cloned.1.call-start
  7.2 0.7 broadcast_in_dim.3.source
  7.9 0.0 copy-start.1
  7.9 1.1 copy-done.1
  9.0 0.0 copy-start.9
  9.0 1.3 shard_map.102
  10.3 0.0 all-gather.12.cloned.1.call-update
  10.3 0.8 maximum_bitcast_fusion
  11.2 4.9 %collective-permute-start = (bf16[2,112,128]{2,1,0:T(8,128)(2,1)S(1)}, bf16[2,112,128]{2,1,0:T(8,128)(2,1)S(1)}, u32[]{:S(2)}, u32[]{:S(2)}) collective-permute-start(bf16[2,112,128]{2,1,0:T(8,128)(2,1)S(1)} %pad.12), channel_id=1, source_target_pairs={{0,0},{1,4},{2,8},{3,12},{4,16},{5,20},{6,24},{7,28},{8,64},{9,68}... | collective-permute-start | bytes 172040 | tf_op jit(solution)/shard_map/ppermute | solution.py:284
  16.1 1.4 collective-permute-done.both
  17.5 0.9 shard_map.101
  18.4 0.0 copy-start.7
  18.4 0.6 copy-done.7
  19.0 27.3 %all-to-all-start = ((bf16[16,112,128]{2,1,0:T(8,128)(2,1)}), bf16[16,112,128]{2,1,0:T(8,128)(2,1)S(1)}, u32[]{:S(2)}, u32[]{:S(2)}) async-start(bf16[16,112,128]{2,1,0:T(8,128)(2,1)} %shard_map.101), calls=%async_computation | async-start | bytes 917504 | tf_op jit(solution)/shard_map/all_to_all | solution.py:304
  46.3 0.0 all-gather.8.cloned.1.call-start
  46.4 0.0 copy-done.10
  46.4 0.0 copy-done.11
  46.5 0.0 copy-done.9
  46.6 16.0 %all-gather.1 = bf16[1216,384]{1,0:T(8,128)(2,1)S(1)} all-gather(bf16[304,384]{1,0:T(8,128)(2,1)S(1)} %fusion.1), channel_id=3, replica_groups=mesh['x'=4,'yh'=2,'z'=16,'yl'=2,'c'=2] {'yl','c'}, dimensions={0}, use_global_device_ids=true | all-gather | bytes 1167360 | tf_op jit(solution)/shard_map/all_gather | solution.py:297
  62.7 4.4 %all-to-all-done.x = bf16[16,112,128]{2,1,0:T(8,128)(2,1)S(1)} async-done(((bf16[16,112,128]{2,1,0:T(8,128)(2,1)}), bf16[16,112,128]{2,1,0:T(8,128)(2,1)S(1)}, u32[]{:S(2)}, u32[]{:S(2)}) %all-to-all-start) | async-done | bytes 458784 | tf_op jit(solution)/shard_map/all_to_all | solution.py:304
  67.0 0.0 all-gather.12.cloned.1.call-done
  67.0 1.9 shard_map.103
  68.9 20.2 %all_to_all.40.parts = f32[8,400,128]{2,1,0:T(8,128)S(1)} all-to-all(f32[8,400,128]{2,1,0:T(8,128)S(1)} %get-tuple-element.37), channel_id=1, replica_groups=mesh['x'=4,'yh'=2,'z'=16,'yl'=2,'c'=2] {'x','yh'}, dimensions={0} | all-to-all | bytes 3276800 | tf_op jit(solution)/shard_map/all_to_all | solution.py:322
  89.1 0.0 copy-start
  89.1 0.8 shard_map.104
  90.0 0.0 all-gather.8.cloned.1.call-update
  90.0 0.0 all-gather.14.cloned.1.call-start
  90.1 12.7 %all_to_all.41.acts = bf16[8,384,128]{2,1,0:T(8,128)(2,1)S(1)} all-to-all(bf16[8,384,128]{2,1,0:T(8,128)(2,1)S(1)} %get-tuple-element.40), channel_id=1, replica_groups=mesh['x'=4,'yh'=2,'z'=16,'yl'=2,'c'=2] {'x','yh'}, dimensions={0} | all-to-all | bytes 1572864 | tf_op jit(solution)/shard_map/all_to_all | solution.py:331
  102.7 0.0 copy-done
  102.7 0.0 copy-start.5
  102.7 0.0 copy-start.8
  102.7 1.6 shard_map.105
  104.3 0.0 all-gather.14.cloned.1.call-update
  104.4 0.0 all-gather.10.cloned.1.call-start
  104.4 37.3 %all_to_all.42.parts = bf16[16,112,128]{2,1,0:T(8,128)(2,1)S(1)} all-to-all(bf16[16,112,128]{2,1,0:T(8,128)(2,1)S(1)} %get-tuple-element.41), channel_id=1, replica_groups=mesh['x'=4,'yh'=2,'z'=16,'yl'=2,'c'=2] {'z'}, dimensions={0} | all-to-all | bytes 917504 | tf_op jit(solution)/shard_map/all_to_all | solution.py:341
  141.7 0.0 copy-done.5
  141.7 0.0 copy-done.8
  141.7 0.1 shard_map.106
  141.8 0.0 all-gather.8.cloned.1.call-done.blocks
  141.8 32.7 %all_to_all.43.gout = bf16[16,112,128]{2,1,0:T(8,128)(2,1)S(1)} all-to-all(bf16[16,112,128]{2,1,0:T(8,128)(2,1)S(1)} %get-tuple-element.46), channel_id=1, replica_groups=mesh['x'=4,'yh'=2,'z'=16,'yl'=2,'c'=2] {'z'}, dimensions={0} | all-to-all | bytes 917504 | tf_op jit(solution)/shard_map/all_to_all | solution.py:354
  174.5 1.3 shard_map.107
  175.8 0.0 copy-start.6
  175.8 0.9 copy-done.6
  176.7 0.0 all-gather.10.cloned.1.call-update
  176.7 14.3 %all_to_all.44.parts = bf16[8,384,128]{2,1,0:T(8,128)(2,1)S(1)} all-to-all(bf16[8,384,128]{2,1,0:T(8,128)(2,1)} %copy-done.6), channel_id=1, replica_groups=mesh['x'=4,'yh'=2,'z'=16,'yl'=2,'c'=2] {'x','yh'}, dimensions={0} | all-to-all | bytes 1572864 | tf_op jit(solution)/shard_map/all_to_all | solution.py:365
  191.0 0.2 shard_map.108
  191.2 19.8 %all_to_all.45.got = bf16[8,112,128]{2,1,0:T(8,128)(2,1)S(1)} all-to-all(bf16[8,112,128]{2,1,0:T(8,128)(2,1)S(1)} %shard_map.108), channel_id=1, replica_groups=mesh['x'=4,'yh'=2,'z'=16,'yl'=2,'c'=2] {'yh','yl','c'}, dimensions={0} | all-to-all | bytes 458752 | tf_op jit(solution)/shard_map/all_to_all | solution.py:367
  211.0 1.0 shard_map.109
  212.0 3.6 %all-to-all-start.7 = ((bf16[4,784,128]{2,1,0:T(8,128)(2,1)}), bf16[4,784,128]{2,1,0:T(8,128)(2,1)S(1)}, u32[]{:S(2)}, u32[]{:S(2)}) async-start(bf16[4,784,128]{2,1,0:T(8,128)(2,1)} %shard_map.109), calls=%async_computation.7 | async-start | bytes 1605632 | tf_op jit(solution)/shard_map/all_to_all | solution.py:369
  215.7 4.4 %collective-permute-start.1 = (bf16[112,128]{1,0:T(8,128)(2,1)S(1)}, bf16[112,128]{1,0:T(8,128)(2,1)S(1)}, u32[]{:S(2)}, u32[]{:S(2)}) collective-permute-start(bf16[112,128]{1,0:T(8,128)(2,1)S(1)} %get-tuple-element.53), channel_id=1, source_target_pairs={{0,0},{4,1},{8,2},{12,3},{16,4},{20,5},{24,6},{28,7},{64,8},{68,9}... | collective-permute-start | bytes 86024 | tf_op jit(solution)/shard_map/ppermute | solution.py:392
  220.1 0.0 all-gather.14.cloned.1.call-done
  220.1 1.2 constant_dynamic-slice_fusion.1.acts
  221.3 0.0 all-gather.10.cloned.1.call-done.blocks
  221.4 0.0 copy-done.2
  221.4 0.0 copy-start.3
  221.4 1.5 copy-done.3
  222.9 2.2 shard_map.110
  225.1 2.0 all-to-all-done.7.dpre
  227.1 1.5 copy-done.4
  228.6 1.9 shard_map.111
  230.5 0.0 collective-permute-done.1
  230.5 0.6 reshape.31
  (22 shorter events, 0.2 us)
Async XLA Ops:
  7.2 39.2 %copy-start.10 = (s32[384]{0:T(512)S(1)}, s32[384]{0:T(512)}, u32[]{:S(2)}) copy-start(s32[384]{0:T(512)} %param.11) | copy-start | bytes 4612
  7.2 39.2 %copy-start.11 = (f32[384]{0:T(512)S(1)}, f32[384]{0:T(512)}, u32[]{:S(2)}) copy-start(f32[384]{0:T(512)} %param.9) | copy-start | bytes 4612
  7.2 59.9 %all-gather.12.cloned.1.call-start = ((), (), s32[]{:S(2)}) async-start(), calls=%async_computation.10 | async-start | bytes 3440640 | tf_op jit(solution)/shard_map/all_gather | solution.py:298
  7.9 1.1 copy-start.1
  9.0 37.5 %copy-start.9 = (bf16[384,288]{0,1:T(8,128)(2,1)S(1)}, bf16[384,288]{0,1:T(8,128)(2,1)}, u32[]{:S(2)}) copy-start(bf16[384,288]{0,1:T(8,128)(2,1)} %param.8) | copy-start | bytes 663556
  11.2 6.4 %collective-permute-start = (bf16[2,112,128]{2,1,0:T(8,128)(2,1)S(1)}, bf16[2,112,128]{2,1,0:T(8,128)(2,1)S(1)}, u32[]{:S(2)}, u32[]{:S(2)}) collective-permute-start(bf16[2,112,128]{2,1,0:T(8,128)(2,1)S(1)} %pad.12), channel_id=1, source_target_pairs={{0,0},{1,4},{2,8},{3,12},{4,16},{5,20},{6,24},{7,28},{8,64},{9,68}... | collective-permute-start | bytes 172040 | tf_op jit(solution)/shard_map/ppermute | solution.py:284
  18.4 0.6 copy-start.7
  19.0 48.0 %all-to-all-start = ((bf16[16,112,128]{2,1,0:T(8,128)(2,1)}), bf16[16,112,128]{2,1,0:T(8,128)(2,1)S(1)}, u32[]{:S(2)}, u32[]{:S(2)}) async-start(bf16[16,112,128]{2,1,0:T(8,128)(2,1)} %shard_map.101), calls=%async_computation | async-start | bytes 917504 | tf_op jit(solution)/shard_map/all_to_all | solution.py:304
  46.3 95.5 %all-gather.8.cloned.1.call-start = ((), (), s32[]{:S(2)}) async-start(), calls=%async_computation.8 | async-start | bytes 2293760 | tf_op jit(solution)/shard_map/all_gather | solution.py:352
  89.1 13.6 %copy-start = (bf16[3584,384]{1,0:T(8,128)(2,1)S(1)}, bf16[3584,384]{1,0:T(8,128)(2,1)}, u32[]{:S(2)}) copy-start(bf16[3584,384]{1,0:T(8,128)(2,1)} %all-gather.12.cloned.1.call-done) | copy-start | bytes 8257540
  90.0 130.1 %all-gather.14.cloned.1.call-start = ((), (), s32[]{:S(2)}) async-start(), calls=%async_computation.11 | async-start | bytes 3932160 | tf_op jit(solution)/shard_map/all_gather | solution.py:342
  102.7 39.0 %copy-start.5 = (f32[408,128]{1,0:T(8,128)S(1)}, f32[408,128]{1,0:T(8,128)}, u32[]{:S(2)}) copy-start(f32[408,128]{1,0:T(8,128)} %get-tuple-element.42.state) | copy-start | bytes 626692
  102.7 39.0 %copy-start.8 = (bf16[2,112,128]{2,1,0:T(8,128)(2,1)S(1)}, bf16[2,112,128]{2,1,0:T(8,128)(2,1)}, u32[]{:S(2)}) copy-start(bf16[2,112,128]{2,1,0:T(8,128)(2,1)} %copy-done.7) | copy-start | bytes 172036
  104.4 117.0 %all-gather.10.cloned.1.call-start = ((), (), s32[]{:S(2)}) async-start(), calls=%async_computation.9 | async-start | bytes 2293760 | tf_op jit(solution)/shard_map/all_gather | solution.py:364
  175.8 0.9 copy-start.6
  212.0 9.4 %copy-start.2 = (bf16[384,3,288]{0,2,1:T(8,128)(2,1)S(1)}, bf16[384,3,288]{0,2,1:T(8,128)(2,1)}, u32[]{:S(2)}) copy-start(bf16[384,3,288]{0,2,1:T(8,128)(2,1)} %param.10) | copy-start | bytes 1990660
  212.0 15.2 %all-to-all-start.7 = ((bf16[4,784,128]{2,1,0:T(8,128)(2,1)}), bf16[4,784,128]{2,1,0:T(8,128)(2,1)S(1)}, u32[]{:S(2)}, u32[]{:S(2)}) async-start(bf16[4,784,128]{2,1,0:T(8,128)(2,1)} %shard_map.109), calls=%async_computation.7 | async-start | bytes 1605632 | tf_op jit(solution)/shard_map/all_to_all | solution.py:369
  215.7 14.9 %collective-permute-start.1 = (bf16[112,128]{1,0:T(8,128)(2,1)S(1)}, bf16[112,128]{1,0:T(8,128)(2,1)S(1)}, u32[]{:S(2)}, u32[]{:S(2)}) collective-permute-start(bf16[112,128]{1,0:T(8,128)(2,1)S(1)} %get-tuple-element.53), channel_id=1, source_target_pairs={{0,0},{4,1},{8,2},{12,3},{16,4},{20,5},{24,6},{28,7},{64,8},{68,9}... | collective-permute-start | bytes 86024 | tf_op jit(solution)/shard_map/ppermute | solution.py:392
  221.4 1.5 copy-start.3
  227.1 1.5 copy-start.4
Sparse Core Ops, SparseCore 0:
  10.7 53.1 all-gather.11
  90.1 40.6 all-gather.7
  133.5 46.4 all-gather.13
  181.9 37.8 all-gather.9

commit v12 on v11

--- a/solution.py
+++ b/solution.py
@@ -70,9 +70,12 @@
     return lax.dot_general(a, b, (((left,), (right,)), ((), ())), preferred_element_type=f32)
 
 
-def spread_out(both, out):
+def spread_out(both, out, kept, sem):
+    copy = pltpu.make_async_copy(both, kept, sem)
+    copy.start()
     for z in range(16):
         out[z] = both[0]
+    copy.wait()
 
 
 def arrange(dec, source, out, square, masked, ordered):
@@ -168,9 +171,9 @@
         gout[z] = low
 
 
-def pull_back(gout, rows, out, loss, kept, sem):
-    copy = pltpu.make_async_copy(gout, kept, sem)
-    copy.start()
+def pull_back(gout, rows, far_out, loss, kept, out, sem, sems):
+    copies = [pltpu.make_async_copy(gout, kept, sem)]
+    copies[0].start()
     total = jnp.sum(gout[:, 96:112].astype(f32), axis=0)
     loss[...] = jnp.broadcast_to(jnp.sum(total[12:15], axis=0, keepdims=True), (8, 128))
     for half in range(2):
@@ -183,7 +186,11 @@
                     out[half * 4 + g, at : at + 32] = product[
                         g * 32 : g * 32 + 32, c * 128 : c * 128 + 128
                     ]
-    copy.wait()
+        four = pl.ds(half * 4, 4)
+        copies.append(pltpu.make_async_copy(out.at[four], far_out.at[four], sems.at[half]))
+        copies[-1].start()
+    for copy in copies:
+        copy.wait()
 
 
 def tail_of(values):
@@ -300,7 +307,13 @@
     source_quad = tail[:, 0]
     bias_quad = tail[:, 1] + tail[:, 2] + tail[:, 3]
     square_quad = (tail[:, 4] + tail[:, 5] + tail[:, 6]).reshape(1536)
-    (x_sent,) = call(spread_out, both, out=[((16, BLOCK, 128), bf16)])
+    x_sent, both = call(
+        spread_out,
+        both,
+        out=[((16, BLOCK, 128), bf16), ((2, BLOCK, 128), bf16)],
+        far=(1,),
+        scratch=[pltpu.SemaphoreType.DMA],
+    )
     x_quad = lax.all_to_all(x_sent, "z", 0, 0)
     squares = jnp.pad(square_quad.reshape(12, 128), ((0, 4), (0, 0)))
     x_quad, dec_quad, squares = together((x_quad, dec_quad, squares))
@@ -358,8 +371,12 @@
         gout_all,
         dec_quad,
         out=[((8, 384, 128), bf16), ((8, 128), f32), ((16, BLOCK, 128), bf16)],
-        far=(2,),
-        scratch=[pltpu.SemaphoreType.DMA],
+        far=(0, 2),
+        scratch=[
+            pltpu.VMEM((8, 384, 128), bf16),
+            pltpu.SemaphoreType.DMA,
+            pltpu.SemaphoreType.DMA((2,)),
+        ],
     )
     gout_every = lax.all_gather(gout_kept.reshape(2, 8 * BLOCK, 128), QUAD)
     slopes = lax.all_to_all(slopes, DP, 0, 0)

time: 241 us -> 241 us (level)
    unnamed x24 -> x20, local copies, waits for them, and re-layouts: 5.6 us -> 4.11 us
where the time goes in v12:
time: 241 us; the launch traced here: 237 us
  blocking collectives  153 us (63%)
  starting transfers between devices  40.5 us (17%)
  Pallas kernels  14.5 us (6%)
  between operations  14.1 us (6%)
  waiting for transfers between devices  7.87 us (3%)
  local copies, waits for them, and re-layouts  6.8 us (3%)
    all_to_all x1, blocking collectives, on_device(): parts = lax.all_to_all(terms, 'z', 0, 0)  37.4 us
    all_to_all x1, blocking collectives, on_device(): gout_all = lax.all_to_all(gout, 'z', 0, 0)  32.7 us
    all_to_all x1, starting transfers between devices, on_device(): x_quad = lax.all_to_all(x_sent, 'z', 0, 0)  27.3 us
    all_to_all x1, blocking collectives, on_device(): partial = lax.all_to_all(partial, DP, 0, 0)  20.2 us
    all_to_all x1, blocking collectives, on_device(): got = lax.all_to_all(sent, PLANE, 0, 0)  19.7 us
    all_gather x1, blocking collectives, on_device(): enc_quad = lax.all_gather(enc_own, QUAD)  16 us
    pallas_call x11, Pallas kernels, call(): pl.pallas_call(kernel, in_specs=[inside] * len(args), out_specs=[outside...  14.5 us
    all_to_all x1, blocking collectives, on_device(): slopes = lax.all_to_all(slopes, DP, 0, 0)  14.3 us
  transfers between devices with their start and end apart: 8, of which 3 were waited for; matrix products, arithmetic and copies ran while one was open for 1% of the time, Pallas kernels for 4%

profile of v12, /device:TPU:1, one launch (start us, length us, event | category | flops | bytes accessed | tf_op | source)
XLA Modules:
  0.0 237.5 jit_solution(9619446417366498681)
XLA Ops:
  7.2 0.0 copy-start.8
  7.2 0.0 copy-start.9
  7.2 0.0 all-gather.12.cloned.1.call-start
  7.2 0.7 broadcast_in_dim.3.source
  7.9 0.0 copy-start.1
  7.9 1.1 copy-done.1
  9.0 0.0 copy-start.7
  9.0 1.3 shard_map.102
  10.3 0.0 all-gather.12.cloned.1.call-update
  10.3 0.8 maximum_bitcast_fusion
  11.2 4.9 %collective-permute-start = (bf16[2,112,128]{2,1,0:T(8,128)(2,1)S(1)}, bf16[2,112,128]{2,1,0:T(8,128)(2,1)S(1)}, u32[]{:S(2)}, u32[]{:S(2)}) collective-permute-start(bf16[2,112,128]{2,1,0:T(8,128)(2,1)S(1)} %pad.12), channel_id=1, source_target_pairs={{0,0},{1,4},{2,8},{3,12},{4,16},{5,20},{6,24},{7,28},{8,64},{9,68}... | collective-permute-start | bytes 172040 | tf_op jit(solution)/shard_map/ppermute | solution.py:291
  16.1 1.4 collective-permute-done.both
  17.5 1.4 shard_map.101
  19.0 27.3 %all-to-all-start = ((bf16[16,112,128]{2,1,0:T(8,128)(2,1)}), bf16[16,112,128]{2,1,0:T(8,128)(2,1)S(1)}, u32[]{:S(2)}, u32[]{:S(2)}) async-start(bf16[16,112,128]{2,1,0:T(8,128)(2,1)} %get-tuple-element.34), calls=%async_computation | async-start | bytes 917504 | tf_op jit(solution)/shard_map/all_to_all | solution.py:317
  46.3 0.0 all-gather.8.cloned.1.call-start
  46.4 0.0 copy-done.8
  46.4 0.0 copy-done.9
  46.5 0.0 copy-done.7
  46.5 16.0 %all-gather.1 = bf16[1216,384]{1,0:T(8,128)(2,1)S(1)} all-gather(bf16[304,384]{1,0:T(8,128)(2,1)S(1)} %fusion.1), channel_id=3, replica_groups=mesh['x'=4,'yh'=2,'z'=16,'yl'=2,'c'=2] {'yl','c'}, dimensions={0}, use_global_device_ids=true | all-gather | bytes 1167360 | tf_op jit(solution)/shard_map/all_gather | solution.py:304
  62.6 4.4 %all-to-all-done.x = bf16[16,112,128]{2,1,0:T(8,128)(2,1)S(1)} async-done(((bf16[16,112,128]{2,1,0:T(8,128)(2,1)}), bf16[16,112,128]{2,1,0:T(8,128)(2,1)S(1)}, u32[]{:S(2)}, u32[]{:S(2)}) %all-to-all-start) | async-done | bytes 458784 | tf_op jit(solution)/shard_map/all_to_all | solution.py:317
  67.0 0.0 all-gather.12.cloned.1.call-done
  67.0 1.9 shard_map.103
  68.9 20.2 %all_to_all.40.parts = f32[8,400,128]{2,1,0:T(8,128)S(1)} all-to-all(f32[8,400,128]{2,1,0:T(8,128)S(1)} %get-tuple-element.40), channel_id=1, replica_groups=mesh['x'=4,'yh'=2,'z'=16,'yl'=2,'c'=2] {'x','yh'}, dimensions={0} | all-to-all | bytes 3276800 | tf_op jit(solution)/shard_map/all_to_all | solution.py:335
  89.1 0.0 copy-start
  89.1 0.8 shard_map.104
  89.9 0.0 all-gather.8.cloned.1.call-update
  90.0 0.0 all-gather.14.cloned.1.call-start
  90.0 12.7 %all_to_all.41.acts = bf16[8,384,128]{2,1,0:T(8,128)(2,1)S(1)} all-to-all(bf16[8,384,128]{2,1,0:T(8,128)(2,1)S(1)} %get-tuple-element.43), channel_id=1, replica_groups=mesh['x'=4,'yh'=2,'z'=16,'yl'=2,'c'=2] {'x','yh'}, dimensions={0} | all-to-all | bytes 1572864 | tf_op jit(solution)/shard_map/all_to_all | solution.py:344
  102.7 0.0 copy-done
  102.7 0.0 copy-start.5
  102.7 0.0 copy-start.6
  102.7 1.6 shard_map.105
  104.3 0.0 all-gather.14.cloned.1.call-update
  104.3 0.0 all-gather.10.cloned.1.call-start
  104.4 37.4 %all_to_all.42.parts = bf16[16,112,128]{2,1,0:T(8,128)(2,1)S(1)} all-to-all(bf16[16,112,128]{2,1,0:T(8,128)(2,1)S(1)} %get-tuple-element.44), channel_id=1, replica_groups=mesh['x'=4,'yh'=2,'z'=16,'yl'=2,'c'=2] {'z'}, dimensions={0} | all-to-all | bytes 917504 | tf_op jit(solution)/shard_map/all_to_all | solution.py:354
  141.7 0.0 copy-done.5
  141.7 0.0 copy-done.6
  141.7 0.1 shard_map.106
  141.8 0.0 all-gather.8.cloned.1.call-done.blocks
  141.9 32.7 %all_to_all.43.gout = bf16[16,112,128]{2,1,0:T(8,128)(2,1)S(1)} all-to-all(bf16[16,112,128]{2,1,0:T(8,128)(2,1)S(1)} %get-tuple-element.50), channel_id=1, replica_groups=mesh['x'=4,'yh'=2,'z'=16,'yl'=2,'c'=2] {'z'}, dimensions={0} | all-to-all | bytes 917504 | tf_op jit(solution)/shard_map/all_to_all | solution.py:367
  174.6 2.0 shard_map.107
  176.6 0.0 all-gather.10.cloned.1.call-update
  176.6 14.3 %all_to_all.44.parts = bf16[8,384,128]{2,1,0:T(8,128)(2,1)S(1)} all-to-all(bf16[8,384,128]{2,1,0:T(8,128)(2,1)} %get-tuple-element.51), channel_id=1, replica_groups=mesh['x'=4,'yh'=2,'z'=16,'yl'=2,'c'=2] {'x','yh'}, dimensions={0} | all-to-all | bytes 1572864 | tf_op jit(solution)/shard_map/all_to_all | solution.py:382
  190.9 0.2 shard_map.108
  191.1 19.7 %all_to_all.45.got = bf16[8,112,128]{2,1,0:T(8,128)(2,1)S(1)} all-to-all(bf16[8,112,128]{2,1,0:T(8,128)(2,1)S(1)} %shard_map.108), channel_id=1, replica_groups=mesh['x'=4,'yh'=2,'z'=16,'yl'=2,'c'=2] {'yh','yl','c'}, dimensions={0} | all-to-all | bytes 458752 | tf_op jit(solution)/shard_map/all_to_all | solution.py:384
  210.8 1.0 shard_map.109
  211.8 0.0 copy-start.2
  211.8 3.6 %all-to-all-start.7 = ((bf16[4,784,128]{2,1,0:T(8,128)(2,1)}), bf16[4,784,128]{2,1,0:T(8,128)(2,1)S(1)}, u32[]{:S(2)}, u32[]{:S(2)}) async-start(bf16[4,784,128]{2,1,0:T(8,128)(2,1)} %shard_map.109), calls=%async_computation.7 | async-start | bytes 1605632 | tf_op jit(solution)/shard_map/all_to_all | solution.py:386
  215.5 4.5 %collective-permute-start.1 = (bf16[112,128]{1,0:T(8,128)(2,1)S(1)}, bf16[112,128]{1,0:T(8,128)(2,1)S(1)}, u32[]{:S(2)}, u32[]{:S(2)}) collective-permute-start(bf16[112,128]{1,0:T(8,128)(2,1)S(1)} %get-tuple-element.57), channel_id=1, source_target_pairs={{0,0},{4,1},{8,2},{12,3},{16,4},{20,5},{24,6},{28,7},{64,8},{68,9}... | collective-permute-start | bytes 86024 | tf_op jit(solution)/shard_map/ppermute | solution.py:409
  219.9 0.0 all-gather.14.cloned.1.call-done
  220.0 1.2 constant_dynamic-slice_fusion.1.acts
  221.2 0.0 all-gather.10.cloned.1.call-done.blocks
  221.2 0.0 copy-done.2
  221.2 0.0 copy-start.3
  221.2 1.5 copy-done.3
  222.7 2.2 shard_map.110
  225.0 1.9 all-to-all-done.7.dpre
  226.9 0.0 copy-start.4
  226.9 1.5 copy-done.4
  228.4 1.9 shard_map.111
  230.3 0.0 collective-permute-done.1
  230.3 0.6 reshape.31
  (20 shorter events, 0.2 us)
Async XLA Ops:
  7.2 39.2 %copy-start.8 = (s32[384]{0:T(512)S(1)}, s32[384]{0:T(512)}, u32[]{:S(2)}) copy-start(s32[384]{0:T(512)} %param.11) | copy-start | bytes 4612
  7.2 39.2 %copy-start.9 = (f32[384]{0:T(512)S(1)}, f32[384]{0:T(512)}, u32[]{:S(2)}) copy-start(f32[384]{0:T(512)} %param.9) | copy-start | bytes 4612
  7.2 59.8 %all-gather.12.cloned.1.call-start = ((), (), s32[]{:S(2)}) async-start(), calls=%async_computation.10 | async-start | bytes 3440640 | tf_op jit(solution)/shard_map/all_gather | solution.py:305
  7.9 1.1 copy-start.1
  9.0 37.5 %copy-start.7 = (bf16[384,288]{0,1:T(8,128)(2,1)S(1)}, bf16[384,288]{0,1:T(8,128)(2,1)}, u32[]{:S(2)}) copy-start(bf16[384,288]{0,1:T(8,128)(2,1)} %param.8) | copy-start | bytes 663556
  11.2 6.4 %collective-permute-start = (bf16[2,112,128]{2,1,0:T(8,128)(2,1)S(1)}, bf16[2,112,128]{2,1,0:T(8,128)(2,1)S(1)}, u32[]{:S(2)}, u32[]{:S(2)}) collective-permute-start(bf16[2,112,128]{2,1,0:T(8,128)(2,1)S(1)} %pad.12), channel_id=1, source_target_pairs={{0,0},{1,4},{2,8},{3,12},{4,16},{5,20},{6,24},{7,28},{8,64},{9,68}... | collective-permute-start | bytes 172040 | tf_op jit(solution)/shard_map/ppermute | solution.py:291
  19.0 48.0 %all-to-all-start = ((bf16[16,112,128]{2,1,0:T(8,128)(2,1)}), bf16[16,112,128]{2,1,0:T(8,128)(2,1)S(1)}, u32[]{:S(2)}, u32[]{:S(2)}) async-start(bf16[16,112,128]{2,1,0:T(8,128)(2,1)} %get-tuple-element.34), calls=%async_computation | async-start | bytes 917504 | tf_op jit(solution)/shard_map/all_to_all | solution.py:317
  46.3 95.5 %all-gather.8.cloned.1.call-start = ((), (), s32[]{:S(2)}) async-start(), calls=%async_computation.8 | async-start | bytes 2293760 | tf_op jit(solution)/shard_map/all_gather | solution.py:365
  89.1 13.6 %copy-start = (bf16[3584,384]{1,0:T(8,128)(2,1)S(1)}, bf16[3584,384]{1,0:T(8,128)(2,1)}, u32[]{:S(2)}) copy-start(bf16[3584,384]{1,0:T(8,128)(2,1)} %all-gather.12.cloned.1.call-done) | copy-start | bytes 8257540
  90.0 130.0 %all-gather.14.cloned.1.call-start = ((), (), s32[]{:S(2)}) async-start(), calls=%async_computation.11 | async-start | bytes 3932160 | tf_op jit(solution)/shard_map/all_gather | solution.py:355
  102.7 39.1 %copy-start.5 = (f32[408,128]{1,0:T(8,128)S(1)}, f32[408,128]{1,0:T(8,128)}, u32[]{:S(2)}) copy-start(f32[408,128]{1,0:T(8,128)} %get-tuple-element.46.state) | copy-start | bytes 626692
  102.7 39.1 %copy-start.6 = (bf16[2,112,128]{2,1,0:T(8,128)(2,1)S(1)}, bf16[2,112,128]{2,1,0:T(8,128)(2,1)}, u32[]{:S(2)}) copy-start(bf16[2,112,128]{2,1,0:T(8,128)(2,1)} %get-tuple-element.45.both) | copy-start | bytes 172036
  104.3 116.9 %all-gather.10.cloned.1.call-start = ((), (), s32[]{:S(2)}) async-start(), calls=%async_computation.9 | async-start | bytes 2293760 | tf_op jit(solution)/shard_map/all_gather | solution.py:381
  211.8 9.4 %copy-start.2 = (bf16[384,3,288]{0,2,1:T(8,128)(2,1)S(1)}, bf16[384,3,288]{0,2,1:T(8,128)(2,1)}, u32[]{:S(2)}) copy-start(bf16[384,3,288]{0,2,1:T(8,128)(2,1)} %param.10) | copy-start | bytes 1990660
  211.8 15.1 %all-to-all-start.7 = ((bf16[4,784,128]{2,1,0:T(8,128)(2,1)}), bf16[4,784,128]{2,1,0:T(8,128)(2,1)S(1)}, u32[]{:S(2)}, u32[]{:S(2)}) async-start(bf16[4,784,128]{2,1,0:T(8,128)(2,1)} %shard_map.109), calls=%async_computation.7 | async-start | bytes 1605632 | tf_op jit(solution)/shard_map/all_to_all | solution.py:386
  215.5 14.8 %collective-permute-start.1 = (bf16[112,128]{1,0:T(8,128)(2,1)S(1)}, bf16[112,128]{1,0:T(8,128)(2,1)S(1)}, u32[]{:S(2)}, u32[]{:S(2)}) collective-permute-start(bf16[112,128]{1,0:T(8,128)(2,1)S(1)} %get-tuple-element.57), channel_id=1, source_target_pairs={{0,0},{4,1},{8,2},{12,3},{16,4},{20,5},{24,6},{28,7},{64,8},{68,9}... | collective-permute-start | bytes 86024 | tf_op jit(solution)/shard_map/ppermute | solution.py:409
  221.2 1.5 copy-start.3
  226.9 1.5 copy-start.4
Sparse Core Ops, SparseCore 0:
  10.7 53.1 all-gather.11
  90.1 40.7 all-gather.7
  133.5 46.3 all-gather.13
  181.9 37.8 all-gather.9
